TPU v7x, 32 devices: a whole 2x2x4 slice. The times are simulated.
32 devices in a mesh: tm: 8 (over z, y), head: 4 (over x, core).
Axes of the slice: x: 2, y: 2, z: 4, core: 2. Of those that a mesh axis runs over, the one named last changes fastest.
Arguments:
- series: bfloat16 [2048, 512], P('tm'), may hold values from -6 to 6
- in_weight: bfloat16 [512, 3, 1024], P(None, None, 'head'), may hold values from -0.25 to 0.25
- step_weight: bfloat16 [512, 16], P(None, 'head'), may hold values from -0.25 to 0.25
- step_bias: float32 [16], P('head'), may hold values from -7 to -6
- log_rate: float32 [16], P('head'), as said below
- conv_weight: float32 [4, 2, 1024], P(None, None, 'head'), may hold values from -3 to 3
- conv_bias: float32 [2, 1024], P(None, 'head'), may hold values from -3 to 3
- skip_gain: float32 [16], P('head'), may hold values from 0.5 to 1.5
- norm_gain: float32 [1024], P('head'), may hold values from 0.1 to 1.9
- out_weight: bfloat16 [512, 1024], P(None, 'head'), may hold values from -0.1875 to 0.1875
- cotangent: bfloat16 [2048, 512], P('tm'), may hold values from -6 to 6
Outputs:
- layer_out: bfloat16 [2048, 512], P(('tm', 'head'))
- series_grad: float32 [2048, 512], P(('tm', 'head'))
- w_in_grad: float32 [512, 3, 1024], P('tm', None, 'head')
- w_dt_grad: float32 [512, 16], P('tm', 'head')
- w_out_grad: float32 [512, 1024], P('tm', 'head')
Inputs may be any that keep to these rules, and one draw needn't show every extreme that they name: `log_rate`: each head's logarithm of its decay rate.
All inputs are finite; a program needn't handle non-finite values.
Results may differ from a plain program's by a relative error of at most 0.0076.
Values may be sent and summed in bfloat16 or wider, within the bound.
No kernel may reach another device: no remote copies, remote signals or barrier semaphores. Data moves between devices by JAX's collectives and lax.ppermute only.
A program may use at most 64 MiB of HBM per device.

v0:
```python
import jax
import jax.numpy as jnp
from jax import lax
from jax.sharding import PartitionSpec as P

E = 1024
N = 128
KW = 4
BLOCK = 256


NORM_EPSILON = 1e-05
HIGHEST_PRECISION = lax.Precision.HIGHEST
HIGH_PRECISION = lax.Precision.HIGH


def passed_along(block, axis, distance):
    devices = range(lax.axis_size(axis))
    route = [(i - distance, i) for i in devices if i - distance in devices]
    return lax.ppermute(block, axis, route)


def carried_in(x, axis, combine, identity, reverse):
    count, position = (lax.axis_size(axis), lax.axis_index(axis))
    everything = jax.tree.map(lambda part: lax.all_gather(part, axis), x)
    start = jax.tree.map(
        lambda part, zero: jnp.broadcast_to(jnp.asarray(zero, part.dtype), part.shape), x, identity
    )

    def hop(k, before):
        at = count - 1 - k if reverse else k
        reached = at > position if reverse else at < position
        new = combine(before, jax.tree.map(lambda part: part[at], everything))
        return jax.tree.map(lambda a, b: jnp.where(reached, a, b), new, before)

    return lax.fori_loop(0, count, hop, start)


def contract(left_side, right_side, left_dim, right_dim):
    return lax.dot_general(
        left_side,
        right_side,
        (((left_dim,), (right_dim,)), ((), ())),
        preferred_element_type=jnp.float32,
    )


def silu_grad(values):
    sigmoid_v = jax.nn.sigmoid(values)
    return sigmoid_v * (1.0 + values * (1.0 - sigmoid_v))


def decay_table(log_block):
    running = jnp.cumsum(log_block, axis=0)
    length = log_block.shape[0]
    row_ids = lax.broadcasted_iota(jnp.int32, (length, length), 0)
    col_ids = lax.broadcasted_iota(jnp.int32, (length, length), 1)
    log_gap = running.T[:, :, None] - running.T[:, None, :]
    decays = jnp.exp(jnp.where((col_ids <= row_ids)[None], log_gap, -1e30))
    return (running, decays)


def block_forward(x_block, b_block, c_block, step_block, log_block, start_state, skip_gain):
    per_group = x_block.shape[1] // b_block.shape[1]
    x_wide = x_block.astype(jnp.float32)
    b_wide = b_block.astype(jnp.float32)
    c_wide = c_block.astype(jnp.float32)
    b_heads = jnp.repeat(b_wide, per_group, axis=1)
    c_heads = jnp.repeat(c_wide, per_group, axis=1)
    running, decays = decay_table(log_block)
    scores = jnp.einsum("ign,jgn->gij", c_block, b_block, preferred_element_type=jnp.float32)
    mixing = jnp.repeat(scores, per_group, axis=0) * decays * step_block.T[:, None, :]
    inside = jnp.einsum("hij,jhp->ihp", mixing, x_wide, precision=HIGH_PRECISION)
    from_state = jnp.exp(running)[:, :, None] * jnp.einsum(
        "ihn,hpn->ihp", c_heads, start_state, precision=HIGH_PRECISION
    )
    output = inside + from_state + skip_gain[None, :, None] * x_wide
    remain = jnp.exp(running[-1][None, :] - running) * step_block
    end_state = jnp.exp(running[-1])[:, None, None] * start_state + jnp.einsum(
        "jh,jhp,jhn->hpn", remain, x_wide, b_heads, precision=HIGH_PRECISION
    )
    return (output, end_state)


def block_backward(
    x_block,
    b_block,
    c_block,
    step_block,
    log_block,
    start_state,
    skip_gain,
    grad_y,
    ssm_out,
    after_state,
):
    group_count = b_block.shape[1]
    per_group = x_block.shape[1] // group_count
    length = x_block.shape[0]
    x_wide = x_block.astype(jnp.float32)
    b_wide = b_block.astype(jnp.float32)
    c_wide = c_block.astype(jnp.float32)
    b_heads = jnp.repeat(b_wide, per_group, axis=1)
    c_heads = jnp.repeat(c_wide, per_group, axis=1)
    running, decays = decay_table(log_block)
    scores = jnp.einsum("ign,jgn->gij", c_block, b_block, preferred_element_type=jnp.float32)
    weighted = jnp.repeat(scores, per_group, axis=0) * decays
    remain = jnp.exp(running[-1][None, :] - running)
    back_b = jnp.einsum("hit,ihp->thp", weighted, grad_y, precision=HIGH_PRECISION)
    back_b = back_b + remain[:, :, None] * jnp.einsum(
        "thn,hpn->thp", b_heads, after_state, precision=HIGH_PRECISION
    )
    grad_x = skip_gain[None, :, None] * grad_y + step_block[:, :, None] * back_b
    x_back = jnp.sum(x_wide * back_b, axis=2)
    grad_cum = jnp.sum(grad_y * ssm_out, axis=2) - step_block * x_back
    pair_terms = (
        decays
        * jnp.einsum("ihp,jhp->hij", grad_y, x_wide, precision=HIGH_PRECISION)
        * step_block.T[:, None, :]
    )
    group_terms = pair_terms.reshape(group_count, per_group, length, length).sum(axis=1)
    state_c = jnp.exp(running)[:, :, None] * jnp.einsum(
        "ihp,hpn->ihn", grad_y, start_state, precision=HIGH_PRECISION
    )
    grad_c = jnp.einsum(
        "gij,jgn->ign", group_terms, b_wide, precision=HIGH_PRECISION
    ) + state_c.reshape(length, group_count, per_group, -1).sum(axis=2)
    state_b = (step_block * remain)[:, :, None] * jnp.einsum(
        "jhp,hpn->jhn", x_wide, after_state, precision=HIGH_PRECISION
    )
    grad_b = jnp.einsum(
        "gij,ign->jgn", group_terms, c_wide, precision=HIGH_PRECISION
    ) + state_b.reshape(length, group_count, per_group, -1).sum(axis=2)
    before = jnp.exp(running[-1])[:, None, None] * after_state + jnp.einsum(
        "ih,ihp,ihn->hpn", jnp.exp(running), grad_y, c_heads, precision=HIGH_PRECISION
    )
    return (grad_x, grad_b, grad_c, x_back, grad_cum, before)


def conv_rims(values, shift_by):
    return passed_along(values, "tm", shift_by)


def link_states(earlier_part, later_part):
    return (
        earlier_part[0] + later_part[0],
        jnp.exp(later_part[0])[:, None, None] * earlier_part[1] + later_part[1],
    )


def state_pass(summary, backward):
    identity = (jnp.zeros_like(summary[0]), jnp.zeros_like(summary[1]))
    return carried_in(summary, "tm", link_states, identity, backward)


def channel_total(values):
    return lax.psum(values, "head")


def head_partials(values):
    return lax.psum_scatter(values, "head", scatter_dimension=0, tiled=True)


def body(
    series,
    in_weight,
    step_weight,
    step_bias,
    log_rate,
    conv_weight,
    conv_bias,
    skip_gain,
    norm_gain,
    out_weight,
    cotangent,
):
    row_count = series.shape[0]
    model_width = series.shape[1]
    inner_width = in_weight.shape[2]
    head_count = step_weight.shape[1]
    head_size = inner_width // head_count
    group_count = inner_width // (2 * N)
    per_group = head_count // group_count
    block_count = row_count // BLOCK
    margin = KW - 1
    w_flat = in_weight.reshape(model_width, 3 * inner_width)
    projected = (
        jnp.dot(series, w_flat, preferred_element_type=jnp.float32)
        .astype(jnp.bfloat16)
        .reshape(row_count, 3, inner_width)
    )
    pre_conv = projected[:, 1:, :]
    upper_rim = conv_rims(pre_conv[row_count - margin :].astype(jnp.float32), 1)
    pre_wide = jnp.concatenate([upper_rim, pre_conv.astype(jnp.float32)], axis=0)
    conv_out = conv_bias[None] + conv_weight[0][None] * pre_wide[0:row_count]
    for offset in range(1, KW):
        conv_out = conv_out + conv_weight[offset][None] * pre_wide[offset : offset + row_count]
    activated = jax.nn.silu(conv_out)
    x_heads = activated[:, 0].astype(jnp.bfloat16).reshape(row_count, head_count, head_size)
    bc_values = activated[:, 1].astype(jnp.bfloat16).reshape(row_count, group_count, 2, N)
    b_values = bc_values[:, :, 0]
    c_values = bc_values[:, :, 1]
    gate_raw = projected[:, 0].astype(jnp.float32)
    step_raw = jnp.dot(series, step_weight, preferred_element_type=jnp.float32)
    step_size = jax.nn.softplus(step_raw + step_bias[None])
    decay_rates = jnp.exp(log_rate)
    log_decay = -step_size * decay_rates[None]
    x_wide = x_heads.astype(jnp.float32)
    running = jnp.cumsum(log_decay, axis=0)
    last_log = running[-1]
    own_state = jnp.einsum(
        "lh,lhp,lhn->hpn",
        jnp.exp(last_log[None] - running) * step_size,
        x_wide,
        jnp.repeat(b_values.astype(jnp.float32), per_group, axis=1),
        precision=HIGHEST_PRECISION,
    )
    incoming = state_pass((last_log, own_state), False)[1]
    blocked = (
        x_heads.reshape(block_count, BLOCK, head_count, head_size),
        b_values.reshape(block_count, BLOCK, group_count, N),
        c_values.reshape(block_count, BLOCK, group_count, N),
        step_size.reshape(block_count, BLOCK, head_count),
        log_decay.reshape(block_count, BLOCK, head_count),
    )

    def forward_step(carried, pieces):
        output, end_state = block_forward(
            pieces[0], pieces[1], pieces[2], pieces[3], pieces[4], carried, skip_gain
        )
        return (end_state, (output, carried))

    final_state, (outputs, starts) = lax.scan(forward_step, incoming, blocked)
    y_flat = outputs.reshape(row_count, inner_width)
    gate_act = jax.nn.silu(gate_raw)
    gated_out = y_flat * gate_act
    inv_rms = lax.rsqrt(channel_total(jnp.sum(gated_out * gated_out, axis=1)) / E + NORM_EPSILON)
    normed = (gated_out * inv_rms[:, None] * norm_gain[None]).astype(jnp.bfloat16)
    layer_out = head_partials(contract(normed, out_weight, 1, 1)).astype(jnp.bfloat16)
    grad_normed = jnp.dot(cotangent, out_weight, preferred_element_type=jnp.float32)
    grad_out = contract(cotangent, normed, 0, 0)
    gain_grad = norm_gain[None] * grad_normed
    inner_sum = channel_total(jnp.sum(gated_out * gain_grad, axis=1))
    grad_gated = inv_rms[:, None] * gain_grad - gated_out * (inv_rms**3 * inner_sum / E)[:, None]
    grad_y = (grad_gated * gate_act).reshape(row_count, head_count, head_size)
    grad_gate = grad_gated * y_flat * silu_grad(gate_raw)
    own_back = jnp.einsum(
        "lh,lhp,lhn->hpn",
        jnp.exp(running),
        grad_y,
        jnp.repeat(c_values.astype(jnp.float32), per_group, axis=1),
        precision=HIGHEST_PRECISION,
    )
    after_in = state_pass((last_log, own_back), True)[1]
    ssm_out = outputs - skip_gain[None, None, :, None] * x_wide.reshape(
        block_count, BLOCK, head_count, head_size
    )
    back_inputs = blocked + (
        starts,
        grad_y.reshape(block_count, BLOCK, head_count, head_size),
        ssm_out,
    )

    def backward_step(carried, pieces):
        grad_x, grad_b, grad_c, x_back, grad_cum, before = block_backward(
            pieces[0],
            pieces[1],
            pieces[2],
            pieces[3],
            pieces[4],
            pieces[5],
            skip_gain,
            pieces[6],
            pieces[7],
            carried,
        )
        return (before, (grad_x, grad_b, grad_c, x_back, grad_cum))

    _, (grad_x, grad_b, grad_c, x_back, grad_cum) = lax.scan(
        backward_step, after_in, back_inputs, reverse=True
    )
    grad_cum = grad_cum.reshape(row_count, head_count)
    grad_log = (
        lax.cumsum(grad_cum, axis=0, reverse=True)
        + jnp.sum(after_in * final_state, axis=(1, 2))[None]
    )
    grad_step = x_back.reshape(row_count, head_count) - decay_rates[None] * grad_log
    grad_raw = (grad_step * jax.nn.sigmoid(step_raw + step_bias[None])).astype(jnp.bfloat16)
    grad_bc = jnp.stack(
        [grad_b.reshape(row_count, group_count, N), grad_c.reshape(row_count, group_count, N)],
        axis=2,
    ).reshape(row_count, inner_width)
    grad_act = jnp.stack([grad_x.reshape(row_count, inner_width), grad_bc], axis=1)
    grad_conv = grad_act * silu_grad(conv_out)
    lower_rim = conv_rims(grad_conv[:margin], -1)
    grad_wide = jnp.concatenate([grad_conv, lower_rim], axis=0)
    grad_pre = conv_weight[0][None] * grad_wide[margin : margin + row_count]
    for offset in range(1, KW):
        grad_pre = (
            grad_pre
            + conv_weight[offset][None] * grad_wide[margin - offset : margin - offset + row_count]
        )
    grad_proj = (
        jnp.concatenate([grad_gate[:, None], grad_pre], axis=1)
        .astype(jnp.bfloat16)
        .reshape(row_count, 3 * inner_width)
    )
    grad_in = contract(series, grad_proj, 0, 0).reshape(model_width, 3, inner_width)
    grad_dt = contract(series, grad_raw, 0, 0)
    grad_rows = contract(grad_proj, w_flat, 1, 1) + contract(grad_raw, step_weight, 1, 1)
    series_grad = head_partials(grad_rows)
    w_in_grad, w_dt_grad, w_out_grad = (
        lax.psum_scatter(grad_in, "tm", scatter_dimension=0, tiled=True),
        lax.psum_scatter(grad_dt, "tm", scatter_dimension=0, tiled=True),
        lax.psum_scatter(grad_out, "tm", scatter_dimension=0, tiled=True),
    )
    return (layer_out, series_grad, w_in_grad, w_dt_grad, w_out_grad)


def solution(mesh):
    in_specs = (
        P("tm", None),
        P(None, None, "head"),
        P(None, "head"),
        P("head"),
        P("head"),
        P(None, None, "head"),
        P(None, "head"),
        P("head"),
        P("head"),
        P(None, "head"),
        P("tm", None),
    )
    out_specs = (
        P(("tm", "head"), None),
        P(("tm", "head"), None),
        P("tm", None, "head"),
        P("tm", "head"),
        P("tm", "head"),
    )
    return jax.shard_map(body, mesh=mesh, in_specs=in_specs, out_specs=out_specs, check_vma=False)
```

profile of v0, /device:TPU:0, one launch (start us, length us, event | category | flops | bytes accessed | tf_op | source)
XLA Modules:
  0.0 369.9 jit_solution(15113902599655148444)
XLA Ops:
  7.2 1.4 copy.52
  9.5 4.9 %collective-permute-start = (f32[3,2,256]{2,0,1:T(4,128)S(1)}, f32[3,2,256]{2,0,1:T(4,128)S(1)}, u32[]{:S(2)}, u32[]{:S(2)}) collective-permute-start(f32[3,2,256]{2,0,1:T(4,128)S(1)} %convert_element_type.90), channel_id=1, source_target_pairs={{0,4},{4,8},{8,12},{12,16},{16,20},{20,24},{24,28},{1,5},{5,9},{9,... | collective-permute-start | bytes 18440 | tf_op jit(solution)/shard_map/ppermute | solution.py:20
  14.7 1.2 reduce-window.24
  19.4 19.8 %all-gather.2 = f32[8,1,4]{2,1,0:T(1,128)S(1)} all-gather(f32[1,1,4]{2,1,0:T(1,128)S(1)} %bitcast.285), channel_id=1, replica_groups=mesh['tm'=8,'head'=4] {'tm'}, dimensions={0}, use_global_device_ids=true | all-gather | bytes 144 | tf_op jit(solution)/shard_map/all_gather | solution.py:25
  40.4 19.6 %all-gather.6.cloned.1.call-done = f32[32,64,128]{2,1,0:T(8,128)} async-done(((f32[4,64,128]{2,1,0:T(8,128)}), f32[32,64,128]{2,1,0:T(8,128)}) %all-gather.6.cloned.1.call-update) | async-done | bytes 1048592 | tf_op jit(solution)/shard_map/all_gather | solution.py:25
  60.0 8.3 %while.20 = (s32[]{:T(128)}, f32[4,64,128]{2,1,0:T(8,128)S(1)}, s32[]{:T(128)}, f32[8,4]{1,0:T(8,128)S(1)}, f32[8,4,64,128]{3,2,1,0:T(8,128)}, /*index=5*/s32[]{:T(128)}, s32[]{:T(128)}) while((s32[]{:T(128)}, f32[4,64,128]{2,1,0:T(8,128)S(1)}, s32[]{:T(128)}, f32[8,4]{1,0:T(8,128)S(1)}, f32[8,4,64,128]{3,2,1,0:T(8,128)}, ...), condition=%wide.region_3.4_spmd.clone, body=%wide.region_2.3_spmd.clone.sunk | while | flops 131076 | bytes 393377 | solution.py:36
  70.4 5.7 %all-reduce = (f32[256]{0:T(256)S(1)}, f32[256]{0:T(256)S(1)}) all-reduce(f32[256]{0:T(256)S(1)} %copy-done.31, f32[256]{0:T(256)S(1)} %get-tuple-element.416), channel_id=1, replica_groups=mesh['tm'=8,'head'=4] {'head'}, use_global_device_ids=true, to_apply=%region_5.6 | all-reduce | flops 512 | bytes 4096 | tf_op jit(solution)/shard_map/psum | solution.py:157
  79.8 1.4 convolution_bitcast_fusion.6
  81.4 1.2 fusion.94
  82.7 33.9 %all-gather.8.cloned.1.call-done = f32[32,64,128]{2,1,0:T(8,128)} async-done(((f32[4,64,128]{2,1,0:T(8,128)}), f32[32,64,128]{2,1,0:T(8,128)}) %all-gather.8.cloned.1.call-update) | async-done | bytes 1048592 | tf_op jit(solution)/shard_map/all_gather | solution.py:25
  116.6 13.7 %while.21 = (s32[]{:T(128)}, f32[4,64,128]{2,1,0:T(8,128)S(1)}, s32[]{:T(128)}, f32[8,4]{1,0:T(8,128)}, f32[8,4,64,128]{3,2,1,0:T(8,128)}, /*index=5*/s32[]{:T(128)}, s32[]{:T(128)}, s32[]{:T(128)}, s32[]{:T(128)}) while((s32[]{:T(128)}, f32[4,64,128]{2,1,0:T(8,128)S(1)}, s32[]{:T(128)}, f32[8,4]{1,0:T(8,128)}, ...), condition=%wide.region_10.11_spmd.clone, body=%wide.region_9.10_spmd.clone.sunk | while | flops 131080 | bytes 393439 | solution.py:36
  130.3 2.2 fusion.54
  132.5 5.0 %reduce-window.26 = f32[4,2,128]{2,1,0:T(2,128)S(1)} reduce-window(f32[4,2,128]{2,1,0:T(2,128)S(1)} %reshape.275, f32[]{:T(128)} %constant.141.clone.1), window={size=1x1x128 pad=0_0x0_0x0_127}, to_apply=%region_16.17 | reduce-window | flops 130048 | bytes 8196 | tf_op jit(solution)/shard_map/reduce-window.6
  144.6 1.2 maximum_multiply_fusion
  145.8 1.3 collective-permute-start.1
  148.3 3.0 collective-permute-done.1
  152.0 1.2 convolution_add_fusion
  153.9 1.6 copy.70
  155.6 1.5 convert_element_type.101
  157.1 47.3 %reduce-scatter.16.cloned.1.call-done = f32[64,4]{1,0:T(8,128)} async-done(((f32[512,4]{1,0:T(8,128)}), f32[64,4]{1,0:T(8,128)}) %reduce-scatter.16.cloned.1.call-update) | async-done | bytes 1040
  204.4 1.4 copy.73
  205.8 63.7 %reduce-scatter.18.cloned.1.call-done = f32[64,256]{1,0:T(8,128)} async-done(((f32[512,256]{1,0:T(8,128)}), f32[64,256]{1,0:T(8,128)}) %reduce-scatter.18.cloned.1.call-update) | async-done | bytes 65552
  269.5 23.6 %reduce-scatter.12.cloned.1.call-done = f32[64,512]{1,0:T(8,128)} async-done(((f32[256,512]{1,0:T(8,128)}), f32[64,512]{1,0:T(8,128)}) %reduce-scatter.12.cloned.1.call-update) | async-done | bytes 131088 | tf_op jit(solution)/shard_map/reduce_scatter | solution.py:161
  293.1 70.0 %reduce-scatter.14.cloned.1.call-done = f32[64,3,256]{2,0,1:T(8,128)} async-done(((f32[512,3,256]{2,0,1:T(8,128)}), f32[64,3,256]{2,0,1:T(8,128)}) %reduce-scatter.14.cloned.1.call-update) | async-done | bytes 196624 | tf_op jit(solution)/shard_map/reduce_scatter | solution.py:313
  (197 shorter events, 42.5 us)
Async XLA Ops:
  7.2 52.8 %all-gather.6.cloned.1.call-start = ((), (), s32[]{:S(2)}) async-start(), calls=%async_computation.8 | async-start | bytes 1179648 | tf_op jit(solution)/shard_map/all_gather | solution.py:25
  8.7 8.5 %copy-start.22 = (f32[4,2,256]{2,1,0:T(2,128)S(1)}, f32[4,2,256]{2,1,0:T(2,128)}, u32[]{:S(2)}) copy-start(f32[4,2,256]{2,1,0:T(2,128)} %param.20) | copy-start | bytes 24580
  9.1 8.3 %copy-start.30 = (f32[2,256]{1,0:T(2,128)S(1)}, f32[2,256]{1,0:T(2,128)}, u32[]{:S(2)}) copy-start(f32[2,256]{1,0:T(2,128)} %param.21) | copy-start | bytes 6148
  9.5 7.9 %collective-permute-start = (f32[3,2,256]{2,0,1:T(4,128)S(1)}, f32[3,2,256]{2,0,1:T(4,128)S(1)}, u32[]{:S(2)}, u32[]{:S(2)}) collective-permute-start(f32[3,2,256]{2,0,1:T(4,128)S(1)} %convert_element_type.90), channel_id=1, source_target_pairs={{0,4},{4,8},{8,12},{12,16},{16,20},{20,24},{24,28},{1,5},{5,9},{9,... | collective-permute-start | bytes 18440 | tf_op jit(solution)/shard_map/ppermute | solution.py:20
  14.7 25.0 %copy-start.37 = (f32[4,256]{1,0:T(4,128)}, f32[4,256]{1,0:T(4,128)S(1)}, u32[]{:S(2)}) copy-start(f32[4,256]{1,0:T(4,128)S(1)} %get-tuple-element.436) | copy-start | bytes 12292
  16.3 23.3 %copy-start.18 = (f32[1,4,2,128]{3,1,2,0:T(4,128)}, f32[1,4,2,128]{3,1,2,0:T(4,128)S(1)}, u32[]{:S(2)}) copy-start(f32[1,4,2,128]{3,1,2,0:T(4,128)S(1)} %copy.105) | copy-start | bytes 12292
  19.4 97.3 %all-gather.8.cloned.1.call-start = ((), (), s32[]{:S(2)}) async-start(), calls=%async_computation.9 | async-start | bytes 1179648 | tf_op jit(solution)/shard_map/all_gather | solution.py:25
  39.4 20.6 %copy-start.8 = (pred[256,256]{1,0:T(8,128)(4,1)}, pred[256,256]{1,0:T(8,128)(4,1)S(1)}, u32[]{:S(2)}) copy-start(pred[256,256]{1,0:T(8,128)(4,1)S(1)} %iota_compare_fusion) | copy-start | bytes 196612
  39.7 28.7 %copy-start.34 = (f32[4]{0:T(128)S(1)}, f32[4]{0:T(128)}, u32[]{:S(2)}) copy-start(f32[4]{0:T(128)} %param.22) | copy-start | bytes 52
  60.0 10.1 %copy-start.4 = (bf16[256,512]{1,0:T(8,128)(2,1)S(1)}, bf16[256,512]{1,0:T(8,128)(2,1)}, u32[]{:S(2)}) copy-start(bf16[256,512]{1,0:T(8,128)(2,1)} %param.25) | copy-start | bytes 786436
  60.0 10.1 %copy-start.6 = (bf16[512,256]{1,0:T(8,128)(2,1)S(1)}, bf16[512,256]{1,0:T(8,128)(2,1)}, u32[]{:S(2)}) copy-start(bf16[512,256]{1,0:T(8,128)(2,1)} %param.24) | copy-start | bytes 786436
  60.0 10.1 %copy-start.28 = (f32[256]{0:T(256)S(1)}, f32[256]{0:T(256)}, u32[]{:S(2)}) copy-start(f32[256]{0:T(256)} %param.23) | copy-start | bytes 3076
  70.1 7.3 %copy-start.24 = (f32[4]{0:T(128)S(1)}, f32[4]{0:T(128)}, u32[]{:S(2)}) copy-start(f32[4]{0:T(128)} %copy-done.23) | copy-start | bytes 52
  70.4 8.6 %copy-start.9 = (pred[256,256]{1,0:T(8,128)(4,1)S(1)}, pred[256,256]{1,0:T(8,128)(4,1)}, u32[]{:S(2)}) copy-start(pred[256,256]{1,0:T(8,128)(4,1)} %copy-done.8) | copy-start | bytes 196612
  70.4 8.6 %copy-start.19 = (f32[1,4,2,128]{3,1,2,0:T(4,128)S(1)}, f32[1,4,2,128]{3,1,2,0:T(4,128)}, u32[]{:S(2)}) copy-start(f32[1,4,2,128]{3,1,2,0:T(4,128)} %copy-done.18) | copy-start | bytes 12292
  70.4 8.6 %copy-start.38 = (f32[4,256]{1,0:T(4,128)S(1)}, f32[4,256]{1,0:T(4,128)}, u32[]{:S(2)}) copy-start(f32[4,256]{1,0:T(4,128)} %copy-done.37) | copy-start | bytes 12292
  77.3 78.2 %reduce-scatter.10.cloned.1.call-start = ((), (), s32[]{:S(2)}) async-start(), calls=%async_computation.5 | async-start | bytes 655360 | tf_op jit(solution)/shard_map/reduce_scatter | solution.py:161
  82.6 121.7 %reduce-scatter.16.cloned.1.call-start = ((), (), s32[]{:S(2)}) async-start(), calls=%async_computation.10 | async-start | bytes 294912
  140.6 128.8 %reduce-scatter.18.cloned.1.call-start = ((), (), s32[]{:S(2)}) async-start(), calls=%async_computation.11 | async-start | bytes 589824
  142.9 150.2 %reduce-scatter.12.cloned.1.call-start = ((), (), s32[]{:S(2)}) async-start(), calls=%async_computation.6 | async-start | bytes 655360 | tf_op jit(solution)/shard_map/reduce_scatter | solution.py:161
  144.5 6.8 %copy-start.17 = (f32[2,256]{1,0:T(2,128)S(1)}, f32[2,256]{1,0:T(2,128)}, u32[]{:S(2)}) copy-start(f32[2,256]{1,0:T(2,128)} %copy-done.16) | copy-start | bytes 6148
  144.6 7.1 %copy-start.1 = (bf16[512,3,256]{2,0,1:T(8,128)(2,1)S(1)}, bf16[512,3,256]{2,0,1:T(8,128)(2,1)}, u32[]{:S(2)}) copy-start(bf16[512,3,256]{2,0,1:T(8,128)(2,1)} %param.16) | copy-start | bytes 2359300
  145.8 5.5 %collective-permute-start.1 = (f32[3,2,256]{2,0,1:T(4,128)S(1)}, f32[3,2,256]{2,0,1:T(4,128)S(1)}, u32[]{:S(2)}, u32[]{:S(2)}) collective-permute-start(f32[3,2,256]{2,0,1:T(4,128)S(1)} %slice.122), channel_id=1, source_target_pairs={{4,0},{8,4},{12,8},{16,12},{20,16},{24,20},{28,24},{5,1},{9,5},{13... | collective-permute-start | bytes 18440 | tf_op jit(solution)/shard_map/ppermute | solution.py:20
  153.2 209.9 %reduce-scatter.14.cloned.1.call-start = ((), (), s32[]{:S(2)}) async-start(), calls=%async_computation.7 | async-start | bytes 1769472 | tf_op jit(solution)/shard_map/reduce_scatter | solution.py:313
  (24 other events, 72.2 us)
Sparse Core Ops, SparseCore 0:
  19.5 40.4 all-gather.5
  77.4 39.1 all-gather.7
  119.1 20.3 reduce-scatter.9
  143.1 61.2 reduce-scatter.15
  208.5 60.9 reduce-scatter.17
  272.4 20.6 reduce-scatter.11
  297.5 65.5 reduce-scatter.13
where the time goes:
time: 371 us; the launch traced here: 370 us
  waiting for transfers between devices  261 us (70%)
  other arithmetic  27.9 us (8%)
  blocking collectives  25.4 us (7%)
  matrix products  17.1 us (5%)
  local copies, waits for them, and re-layouts  16.4 us (4%)
  between operations  14.9 us (4%)
  starting transfers between devices  6.45 us (2%)
    unnamed x9, waiting for transfers between devices  111 us
    reduce_scatter x1, waiting for transfers between devices, body(): lax.psum_scatter(grad_in, 'tm', scatter_dimension=0, tiled=True)  70 us
    all_gather x2, waiting for transfers between devices, carried_in(): everything = jax.tree.map(lambda part: lax.all_gather(part, axis), x)  53.5 us
    reduce_scatter x2, waiting for transfers between devices, head_partials(): return lax.psum_scatter(values, 'head', scatter_dimension=0, tiled=True)  23.6 us
    all_gather x1, blocking collectives, carried_in(): everything = jax.tree.map(lambda part: lax.all_gather(part, axis), x)  19.8 us
    select_n x16, other arithmetic, hop(): return jax.tree.map(lambda a, b: jnp.where(reached, a, b), new, before)  16 us
  transfers between devices with their start and end apart: 9, of which 7 were waited for; matrix products, arithmetic and copies ran while one was open for 12% of the time, Pallas kernels for 0%

commit v1 on v0

--- a/solution.py
+++ b/solution.py
@@ -148,9 +148,45 @@
     )
 
 
+def fold(last_logs, states, keep, backward):
+    position = lax.axis_index("tm")
+    count = states.shape[0]
+    before = jnp.zeros(states.shape[1:], jnp.float32)
+    out = [None] * count
+    order = range(count - 1, -1, -1) if backward else range(count)
+    for at in order:
+        out[at] = before
+        scale = jnp.exp(last_logs[at])
+        scale = scale.reshape(scale.shape + (1,) * (states.ndim - 1 - scale.ndim))
+        before = scale * before + states[at].astype(jnp.float32)
+    every = jnp.stack(out)
+    if keep:
+        return lax.dynamic_index_in_dim(every, position, 0, keepdims=False)
+    return every
+
+
+def spread(x):
+    count = lax.axis_size("tm")
+    return lax.all_to_all(jnp.broadcast_to(x[None], (count,) + x.shape), "tm", 0, 0)
+
+
 def state_pass(summary, backward):
-    identity = (jnp.zeros_like(summary[0]), jnp.zeros_like(summary[1]))
-    return carried_in(summary, "tm", link_states, identity, backward)
+    count = lax.axis_size("tm")
+    last_logs, own = summary
+    if not backward:
+        every = spread(own.astype(jnp.bfloat16))
+        return fold(last_logs, every, True, False)
+    heads, size, width = own.shape
+    cut = own.reshape(heads, count, size // count, width).transpose(1, 0, 2, 3)
+    cut = lax.all_to_all(cut, "tm", 0, 0)
+    back = lax.all_to_all(fold(last_logs, cut, False, True), "tm", 0, 0)
+    return back.transpose(1, 0, 2, 3).reshape(heads, size, width)
+
+
+def summed(values, axis):
+    count = lax.axis_size(axis)
+    cut = values.astype(jnp.bfloat16).reshape((count, values.shape[0] // count) + values.shape[1:])
+    return jnp.sum(lax.all_to_all(cut, axis, 0, 0).astype(jnp.float32), axis=0)
 
 
 def channel_total(values):
@@ -158,7 +194,7 @@
 
 
 def head_partials(values):
-    return lax.psum_scatter(values, "head", scatter_dimension=0, tiled=True)
+    return summed(values, "head")
 
 
 def body(
@@ -215,7 +251,8 @@
         jnp.repeat(b_values.astype(jnp.float32), per_group, axis=1),
         precision=HIGHEST_PRECISION,
     )
-    incoming = state_pass((last_log, own_state), False)[1]
+    last_logs = spread(last_log)
+    incoming = state_pass((last_logs, own_state), False)
     blocked = (
         x_heads.reshape(block_count, BLOCK, head_count, head_size),
         b_values.reshape(block_count, BLOCK, group_count, N),
@@ -234,13 +271,15 @@
     y_flat = outputs.reshape(row_count, inner_width)
     gate_act = jax.nn.silu(gate_raw)
     gated_out = y_flat * gate_act
-    inv_rms = lax.rsqrt(channel_total(jnp.sum(gated_out * gated_out, axis=1)) / E + NORM_EPSILON)
+    grad_normed = jnp.dot(cotangent, out_weight, preferred_element_type=jnp.float32)
+    gain_grad = norm_gain[None] * grad_normed
+    square_sum, inner_sum = channel_total(
+        (jnp.sum(gated_out * gated_out, axis=1), jnp.sum(gated_out * gain_grad, axis=1))
+    )
+    inv_rms = lax.rsqrt(square_sum / E + NORM_EPSILON)
     normed = (gated_out * inv_rms[:, None] * norm_gain[None]).astype(jnp.bfloat16)
     layer_out = head_partials(contract(normed, out_weight, 1, 1)).astype(jnp.bfloat16)
-    grad_normed = jnp.dot(cotangent, out_weight, preferred_element_type=jnp.float32)
     grad_out = contract(cotangent, normed, 0, 0)
-    gain_grad = norm_gain[None] * grad_normed
-    inner_sum = channel_total(jnp.sum(gated_out * gain_grad, axis=1))
     grad_gated = inv_rms[:, None] * gain_grad - gated_out * (inv_rms**3 * inner_sum / E)[:, None]
     grad_y = (grad_gated * gate_act).reshape(row_count, head_count, head_size)
     grad_gate = grad_gated * y_flat * silu_grad(gate_raw)
@@ -251,7 +290,7 @@
         jnp.repeat(c_values.astype(jnp.float32), per_group, axis=1),
         precision=HIGHEST_PRECISION,
     )
-    after_in = state_pass((last_log, own_back), True)[1]
+    after_in = state_pass((last_logs, own_back), True)
     ssm_out = outputs - skip_gain[None, None, :, None] * x_wide.reshape(
         block_count, BLOCK, head_count, head_size
     )
@@ -310,9 +349,9 @@
     grad_rows = contract(grad_proj, w_flat, 1, 1) + contract(grad_raw, step_weight, 1, 1)
     series_grad = head_partials(grad_rows)
     w_in_grad, w_dt_grad, w_out_grad = (
-        lax.psum_scatter(grad_in, "tm", scatter_dimension=0, tiled=True),
-        lax.psum_scatter(grad_dt, "tm", scatter_dimension=0, tiled=True),
-        lax.psum_scatter(grad_out, "tm", scatter_dimension=0, tiled=True),
+        summed(grad_in, "tm"),
+        summed(grad_dt, "tm"),
+        summed(grad_out, "tm"),
     )
     return (layer_out, series_grad, w_in_grad, w_dt_grad, w_out_grad)
 

time: 371 us -> 156 us (0.42)
  waiting for transfers between devices: 261 us -> 59.7 us
  starting transfers between devices: 6.45 us -> 39.9 us
  blocking collectives: 25.4 us -> 5.67 us
  between operations: 14.9 us -> 1.64 us
  other arithmetic: 27.9 us -> 20.3 us
    unnamed x9 -> x0, waiting for transfers between devices: 111 us -> none
    reduce_scatter x3 -> x0, waiting for transfers between devices: 93.6 us -> none  [the longest x1 70 us: body(): lax.psum_scatter(grad_in, 'tm', scatter_dimension=0, tiled=True)]
    all_to_all x0 -> x9, waiting for transfers between devices: none -> 59.7 us  [the longest x5 34.2 us: summed(): return jnp.sum(lax.all_to_all(cut, axis, 0, 0).astype(jnp.float32), axis=0)]
    all_gather x2 -> x0, waiting for transfers between devices: 53.5 us -> none  [carried_in(): everything = jax.tree.map(lambda part: lax.all_gather(part, axis), x)]
    all_to_all x0 -> x9, starting transfers between devices: none -> 33.6 us  [the longest x5 18 us: summed(): return jnp.sum(lax.all_to_all(cut, axis, 0, 0).astype(jnp.float32), axis=0)]
    all_gather x1 -> x0, blocking collectives: 19.8 us -> none  [carried_in(): everything = jax.tree.map(lambda part: lax.all_gather(part, axis), x)]
    select_n x16 -> x0, other arithmetic: 16 us -> none  [hop(): return jax.tree.map(lambda a, b: jnp.where(reached, a, b), new, before)]
    unnamed x4 -> x12, other arithmetic: 0.15 us -> 7.36 us
  transfers between devices with their start and end apart: 9 -> 11, of which waited for: 7 -> 8; matrix products, arithmetic and copies ran while one was open for 12% -> 18% of each run, Pallas kernels for 0% -> 0%
where the time goes in v1:
time: 156 us; the launch traced here: 155 us
  waiting for transfers between devices  59.7 us (38%)
  starting transfers between devices  39.9 us (26%)
  other arithmetic  20.3 us (13%)
  matrix products  14.2 us (9%)
  local copies, waits for them, and re-layouts  14 us (9%)
  blocking collectives  5.67 us (4%)
  between operations  1.64 us (1%)
    all_to_all x5, waiting for transfers between devices, summed(): return jnp.sum(lax.all_to_all(cut, axis, 0, 0).astype(jnp.float32), axis=0)  34.2 us
    all_to_all x5, starting transfers between devices, summed(): return jnp.sum(lax.all_to_all(cut, axis, 0, 0).astype(jnp.float32), axis=0)  18 us
    all_to_all x2, waiting for transfers between devices, spread(): lax.all_to_all(jnp.broadcast_to(x[None], (count,) + x.shape), 'tm', 0, 0)  14 us
    all_to_all x2, starting transfers between devices, spread(): lax.all_to_all(jnp.broadcast_to(x[None], (count,) + x.shape), 'tm', 0, 0)  8.37 us
    unnamed x12, other arithmetic  7.36 us
    another operation x5, other arithmetic  6.7 us
    ppermute x2, starting transfers between devices, passed_along(): return lax.ppermute(block, axis, route)  6.3 us
    all_to_all x1, waiting for transfers between devices, state_pass(): back = lax.all_to_all(fold(last_logs, cut, False, True), 'tm', 0, 0)  6.2 us
  transfers between devices with their start and end apart: 11, of which 8 were waited for; matrix products, arithmetic and copies ran while one was open for 18% of the time, Pallas kernels for 0%

profile of v1, /device:TPU:0, one launch (start us, length us, event | category | flops | bytes accessed | tf_op | source)
XLA Modules:
  0.0 155.3 jit_solution(14436423448040772381)
XLA Ops:
  0.6 1.5 copy.44
  3.0 4.9 %collective-permute-start = (f32[3,2,256]{2,0,1:T(4,128)S(1)}, f32[3,2,256]{2,0,1:T(4,128)S(1)}, u32[]{:S(2)}, u32[]{:S(2)}) collective-permute-start(f32[3,2,256]{2,0,1:T(4,128)S(1)} %convert_element_type.181), channel_id=1, source_target_pairs={{0,4},{4,8},{8,12},{12,16},{16,20},{20,24},{24,28},{1,5},{5,9},{9,... | collective-permute-start | bytes 18440 | tf_op jit(solution)/shard_map/ppermute | solution.py:20
  10.6 4.9 %all-to-all-start = ((f32[8,1,4]{2,1,0:T(1,128)}), f32[8,1,4]{2,1,0:T(1,128)S(1)}, u32[]{:S(2)}, u32[]{:S(2)}) async-start(f32[8,1,4]{2,1,0:T(1,128)} %broadcast_in_dim.122), calls=%async_computation | async-start | bytes 8192 | tf_op jit(solution)/shard_map/all_to_all | solution.py:170
  18.9 2.9 %all-to-all-done = f32[8,1,4]{2,1,0:T(1,128)S(1)} async-done(((f32[8,1,4]{2,1,0:T(1,128)}), f32[8,1,4]{2,1,0:T(1,128)S(1)}, u32[]{:S(2)}, u32[]{:S(2)}) %all-to-all-start) | async-done | bytes 160 | tf_op jit(solution)/shard_map/all_to_all | solution.py:170
  22.7 3.5 %all-to-all-start.1 = ((bf16[8,4,64,128]{3,2,1,0:T(8,128)(2,1)}), bf16[8,4,64,128]{3,2,1,0:T(8,128)(2,1)S(1)}, u32[]{:S(2)}, u32[]{:S(2)}) async-start(bf16[8,4,64,128]{3,2,1,0:T(8,128)(2,1)} %broadcast_in_dim.124), calls=%async_computation.1 | async-start | bytes 1048576 | tf_op jit(solution)/shard_map/all_to_all | solution.py:170
  28.4 11.1 %all-to-all-done.1 = bf16[8,4,64,128]{3,2,1,0:T(8,128)(2,1)S(1)} async-done(((bf16[8,4,64,128]{3,2,1,0:T(8,128)(2,1)}), bf16[8,4,64,128]{3,2,1,0:T(8,128)(2,1)S(1)}, u32[]{:S(2)}, u32[]{:S(2)}) %all-to-all-start.1) | async-done | bytes 524320 | tf_op jit(solution)/shard_map/all_to_all | solution.py:170
  46.5 5.7 %all-reduce = (f32[256]{0:T(256)S(1)}, f32[256]{0:T(256)S(1)}) all-reduce(f32[256]{0:T(256)S(1)} %get-tuple-element.131, f32[256]{0:T(256)S(1)} %get-tuple-element.80), channel_id=1, replica_groups=mesh['tm'=8,'head'=4] {'head'}, use_global_device_ids=true, to_apply=%region_3.4 | all-reduce | flops 512 | bytes 4096 | tf_op jit(solution)/shard_map/psum | solution.py:193
  56.8 3.8 %all-to-all-start.3 = ((f32[8,4,8,128]{3,2,1,0:T(8,128)}), f32[8,4,8,128]{3,2,1,0:T(8,128)S(1)}, u32[]{:S(2)}, u32[]{:S(2)}) async-start(f32[8,4,8,128]{3,2,1,0:T(8,128)} %bitcast.278), calls=%async_computation.3 | async-start | bytes 262144 | tf_op jit(solution)/shard_map/all_to_all | solution.py:181
  61.0 1.6 %convolution_bitcast_fusion.5 = f32[256,4,64]{0,2,1:T(8,128)S(1)} fusion(f32[256,4,64]{0,2,1:T(8,128)S(1)} %bitcast.286, f32[4,256]{1,0:T(4,128)S(1)} %bitcast.310, f32[256,256]{1,0:T(8,128)} %copy-done.5, pred[256,256]{1,0:T(8,128)(4,1)S(1)} %copy-done.8), kind=kOutput, calls=%fused_computation.26 | convolution fusion | flops 101449728 | bytes 856064 | tf_op jit(solution)/shard_map/while/body/eval_jaxpr/hit,ihp->thp/dot_general | solution.py:109
  62.7 5.3 %all-to-all-done.3 = f32[8,4,8,128]{3,2,1,0:T(8,128)S(1)} async-done(((f32[8,4,8,128]{3,2,1,0:T(8,128)}), f32[8,4,8,128]{3,2,1,0:T(8,128)S(1)}, u32[]{:S(2)}, u32[]{:S(2)}) %all-to-all-start.3) | async-done | bytes 131104 | tf_op jit(solution)/shard_map/all_to_all | solution.py:181
  73.2 3.4 %all-to-all-start.4 = ((f32[8,4,8,128]{3,2,1,0:T(8,128)}), f32[8,4,8,128]{3,2,1,0:T(8,128)S(1)}, u32[]{:S(2)}, u32[]{:S(2)}) async-start(f32[8,4,8,128]{3,2,1,0:T(8,128)} %constant_dynamic-update-slice_fusion.2), calls=%async_computation.4 | async-start | bytes 262144 | tf_op jit(solution)/shard_map/all_to_all | solution.py:182
  77.6 6.2 %all-to-all-done.4 = f32[8,4,8,128]{3,2,1,0:T(8,128)S(1)} async-done(((f32[8,4,8,128]{3,2,1,0:T(8,128)}), f32[8,4,8,128]{3,2,1,0:T(8,128)S(1)}, u32[]{:S(2)}, u32[]{:S(2)}) %all-to-all-start.4) | async-done | bytes 131104 | tf_op jit(solution)/shard_map/all_to_all | solution.py:182
  83.8 3.4 %all-to-all-start.2 = ((bf16[4,64,512]{2,1,0:T(8,128)(2,1)}), bf16[4,64,512]{2,1,0:T(8,128)(2,1)S(1)}, u32[]{:S(2)}, u32[]{:S(2)}) async-start(bf16[4,64,512]{2,1,0:T(8,128)(2,1)} %bitcast.25), calls=%async_computation.2 | async-start | bytes 524288 | tf_op jit(solution)/shard_map/all_to_all | solution.py:189
  87.8 5.0 %reduce-window.26 = f32[4,2,128]{2,1,0:T(2,128)S(1)} reduce-window(f32[4,2,128]{2,1,0:T(2,128)S(1)} %reshape.367, f32[]{:T(128)} %constant.84.clone.1), window={size=1x1x128 pad=0_0x0_0x0_127}, to_apply=%region_12.13 | reduce-window | flops 130048 | bytes 8196 | tf_op jit(solution)/shard_map/reduce-window.6
  94.3 1.4 collective-permute-start.1
  98.0 4.1 %all-to-all-start.8 = ((bf16[8,64,256]{2,1,0:T(8,128)(2,1)}), bf16[8,64,256]{2,1,0:T(8,128)(2,1)S(1)}, u32[]{:S(2)}, u32[]{:S(2)}) async-start(bf16[8,64,256]{2,1,0:T(8,128)(2,1)} %bitcast.57), calls=%async_computation.8 | async-start | bytes 524288 | tf_op jit(solution)/shard_map/all_to_all | solution.py:189
  103.9 7.5 %all-to-all-done.8 = bf16[8,64,256]{2,1,0:T(8,128)(2,1)S(1)} async-done(((bf16[8,64,256]{2,1,0:T(8,128)(2,1)}), bf16[8,64,256]{2,1,0:T(8,128)(2,1)S(1)}, u32[]{:S(2)}, u32[]{:S(2)}) %all-to-all-start.8) | async-done | bytes 262176 | tf_op jit(solution)/shard_map/all_to_all | solution.py:189
  111.4 3.6 %all-to-all-start.7 = ((bf16[8,2,128]{2,1,0:T(2,128)(2,1)}), bf16[8,2,128]{2,1,0:T(2,128)(2,1)S(1)}, u32[]{:S(2)}, u32[]{:S(2)}) async-start(bf16[8,2,128]{2,1,0:T(2,128)(2,1)} %reshape.395), calls=%async_computation.7 | async-start | bytes 8192 | tf_op jit(solution)/shard_map/all_to_all | solution.py:189
  115.2 6.2 %all-to-all-done.7 = bf16[8,2,128]{2,1,0:T(2,128)(2,1)S(1)} async-done(((bf16[8,2,128]{2,1,0:T(2,128)(2,1)}), bf16[8,2,128]{2,1,0:T(2,128)(2,1)S(1)}, u32[]{:S(2)}, u32[]{:S(2)}) %all-to-all-start.7) | async-done | bytes 4128 | tf_op jit(solution)/shard_map/all_to_all | solution.py:189
  121.4 3.4 %all-to-all-start.5 = ((bf16[4,64,512]{2,1,0:T(8,128)(2,1)}), bf16[4,64,512]{2,1,0:T(8,128)(2,1)S(1)}, u32[]{:S(2)}, u32[]{:S(2)}) async-start(bf16[4,64,512]{2,1,0:T(8,128)(2,1)} %bitcast.52), calls=%async_computation.5 | async-start | bytes 524288 | tf_op jit(solution)/shard_map/all_to_all | solution.py:189
  126.0 1.7 %copy.62 = bf16[8,64,3,256]{3,1,2,0:T(8,128)(2,1)} copy(bf16[8,64,3,256]{1,0,3,2:T(8,128)(2,1)S(1)} %reshape.375) | data formatting | bytes 1572864 | tf_op jit(solution)/shard_map/convert_element_type | solution.py:188
  127.7 3.1 %all-to-all-done.5 = bf16[4,64,512]{2,1,0:T(8,128)(2,1)S(1)} async-done(((bf16[4,64,512]{2,1,0:T(8,128)(2,1)}), bf16[4,64,512]{2,1,0:T(8,128)(2,1)S(1)}, u32[]{:S(2)}, u32[]{:S(2)}) %all-to-all-start.5) | async-done | bytes 262176 | tf_op jit(solution)/shard_map/all_to_all | solution.py:189
  130.8 3.5 %all-to-all-start.6 = ((bf16[8,64,3,256]{3,1,2,0:T(8,128)(2,1)}), bf16[8,64,3,256]{3,1,2,0:T(8,128)(2,1)S(1)}, u32[]{:S(2)}, u32[]{:S(2)}) async-start(bf16[8,64,3,256]{3,1,2,0:T(8,128)(2,1)} %copy.62), calls=%async_computation.6 | async-start | bytes 1572864 | tf_op jit(solution)/shard_map/all_to_all | solution.py:189
  137.0 17.5 %all-to-all-done.6 = bf16[8,64,3,256]{3,1,2,0:T(8,128)(2,1)S(1)} async-done(((bf16[8,64,3,256]{3,1,2,0:T(8,128)(2,1)}), bf16[8,64,3,256]{3,1,2,0:T(8,128)(2,1)S(1)}, u32[]{:S(2)}, u32[]{:S(2)}) %all-to-all-start.6) | async-done | bytes 786464 | tf_op jit(solution)/shard_map/all_to_all | solution.py:189
  (208 shorter events, 38.6 us)
Async XLA Ops:
  3.0 14.7 %collective-permute-start = (f32[3,2,256]{2,0,1:T(4,128)S(1)}, f32[3,2,256]{2,0,1:T(4,128)S(1)}, u32[]{:S(2)}, u32[]{:S(2)}) collective-permute-start(f32[3,2,256]{2,0,1:T(4,128)S(1)} %convert_element_type.181), channel_id=1, source_target_pairs={{0,4},{4,8},{8,12},{12,16},{16,20},{20,24},{24,28},{1,5},{5,9},{9,... | collective-permute-start | bytes 18440 | tf_op jit(solution)/shard_map/ppermute | solution.py:20
  8.1 18.9 %copy-start.49 = (f32[4,256]{1,0:T(4,128)}, f32[4,256]{1,0:T(4,128)S(1)}, u32[]{:S(2)}) copy-start(f32[4,256]{1,0:T(4,128)S(1)} %get-tuple-element.126) | copy-start | bytes 12292
  9.8 17.3 %copy-start.27 = (f32[1,4,2,128]{3,1,2,0:T(4,128)}, f32[1,4,2,128]{3,1,2,0:T(4,128)S(1)}, u32[]{:S(2)}) copy-start(f32[1,4,2,128]{3,1,2,0:T(4,128)S(1)} %copy.113) | copy-start | bytes 12292
  10.6 11.3 %all-to-all-start = ((f32[8,1,4]{2,1,0:T(1,128)}), f32[8,1,4]{2,1,0:T(1,128)S(1)}, u32[]{:S(2)}, u32[]{:S(2)}) async-start(f32[8,1,4]{2,1,0:T(1,128)} %broadcast_in_dim.122), calls=%async_computation | async-start | bytes 8192 | tf_op jit(solution)/shard_map/all_to_all | solution.py:170
  22.7 16.8 %all-to-all-start.1 = ((bf16[8,4,64,128]{3,2,1,0:T(8,128)(2,1)}), bf16[8,4,64,128]{3,2,1,0:T(8,128)(2,1)S(1)}, u32[]{:S(2)}, u32[]{:S(2)}) async-start(bf16[8,4,64,128]{3,2,1,0:T(8,128)(2,1)} %broadcast_in_dim.124), calls=%async_computation.1 | async-start | bytes 1048576 | tf_op jit(solution)/shard_map/all_to_all | solution.py:170
  26.8 15.7 %copy-start.23 = (f32[4]{0:T(128)}, f32[4]{0:T(128)S(1)}, u32[]{:S(2)}) copy-start(f32[4]{0:T(128)S(1)} %get-tuple-element.119) | copy-start | bytes 52
  26.8 15.7 %copy-start.25 = (f32[4]{0:T(128)}, f32[4]{0:T(128)S(1)}, u32[]{:S(2)}) copy-start(f32[4]{0:T(128)S(1)} %get-tuple-element.120) | copy-start | bytes 52
  26.8 15.7 %copy-start.34 = (f32[4]{0:T(128)}, f32[4]{0:T(128)S(1)}, u32[]{:S(2)}) copy-start(f32[4]{0:T(128)S(1)} %get-tuple-element.118) | copy-start | bytes 52
  26.8 17.2 %copy-start.21 = (f32[4]{0:T(128)}, f32[4]{0:T(128)S(1)}, u32[]{:S(2)}) copy-start(f32[4]{0:T(128)S(1)} %get-tuple-element.117) | copy-start | bytes 52
  26.8 17.2 %copy-start.32 = (f32[4]{0:T(128)}, f32[4]{0:T(128)S(1)}, u32[]{:S(2)}) copy-start(f32[4]{0:T(128)S(1)} %get-tuple-element.116) | copy-start | bytes 52
  28.4 16.3 %copy-start.42 = (f32[4]{0:T(128)S(1)}, f32[4]{0:T(128)}, u32[]{:S(2)}) copy-start(f32[4]{0:T(128)} %param.18) | copy-start | bytes 52
  56.8 11.2 %all-to-all-start.3 = ((f32[8,4,8,128]{3,2,1,0:T(8,128)}), f32[8,4,8,128]{3,2,1,0:T(8,128)S(1)}, u32[]{:S(2)}, u32[]{:S(2)}) async-start(f32[8,4,8,128]{3,2,1,0:T(8,128)} %bitcast.278), calls=%async_computation.3 | async-start | bytes 262144 | tf_op jit(solution)/shard_map/all_to_all | solution.py:181
  60.6 15.9 %copy-start.4 = (bf16[512,256]{1,0:T(8,128)(2,1)S(1)}, bf16[512,256]{1,0:T(8,128)(2,1)}, u32[]{:S(2)}) copy-start(bf16[512,256]{1,0:T(8,128)(2,1)} %param.20) | copy-start | bytes 786436
  60.6 15.9 %copy-start.40 = (f32[256]{0:T(256)S(1)}, f32[256]{0:T(256)}, u32[]{:S(2)}) copy-start(f32[256]{0:T(256)} %param.19) | copy-start | bytes 3076
  61.0 26.3 %copy-start.19 = (f32[256,4]{0,1:T(4,128)S(1)}, f32[256,4]{0,1:T(4,128)}, u32[]{:S(2)}) copy-start(f32[256,4]{0,1:T(4,128)} %get-tuple-element.85) | copy-start | bytes 12292
  61.0 26.3 %copy-start.20 = (f32[256,4]{0,1:T(4,128)S(1)}, f32[256,4]{0,1:T(4,128)}, u32[]{:S(2)}) copy-start(f32[256,4]{0,1:T(4,128)} %get-tuple-element.113) | copy-start | bytes 12292
  61.0 26.3 %copy-start.43 = (f32[4]{0:T(128)S(1)}, f32[4]{0:T(128)}, u32[]{:S(2)}) copy-start(f32[4]{0:T(128)} %param.18) | copy-start | bytes 52
  73.2 10.7 %all-to-all-start.4 = ((f32[8,4,8,128]{3,2,1,0:T(8,128)}), f32[8,4,8,128]{3,2,1,0:T(8,128)S(1)}, u32[]{:S(2)}, u32[]{:S(2)}) async-start(f32[8,4,8,128]{3,2,1,0:T(8,128)} %constant_dynamic-update-slice_fusion.2), calls=%async_computation.4 | async-start | bytes 262144 | tf_op jit(solution)/shard_map/all_to_all | solution.py:182
  83.8 14.2 %all-to-all-start.2 = ((bf16[4,64,512]{2,1,0:T(8,128)(2,1)}), bf16[4,64,512]{2,1,0:T(8,128)(2,1)S(1)}, u32[]{:S(2)}, u32[]{:S(2)}) async-start(bf16[4,64,512]{2,1,0:T(8,128)(2,1)} %bitcast.25), calls=%async_computation.2 | async-start | bytes 524288 | tf_op jit(solution)/shard_map/all_to_all | solution.py:189
  94.3 7.8 %collective-permute-start.1 = (f32[3,2,256]{2,0,1:T(4,128)S(1)}, f32[3,2,256]{2,0,1:T(4,128)S(1)}, u32[]{:S(2)}, u32[]{:S(2)}) collective-permute-start(f32[3,2,256]{2,0,1:T(4,128)S(1)} %slice.249), channel_id=1, source_target_pairs={{4,0},{8,4},{12,8},{16,12},{20,16},{24,20},{28,24},{5,1},{9,5},{13... | collective-permute-start | bytes 18440 | tf_op jit(solution)/shard_map/ppermute | solution.py:20
  98.0 13.3 %all-to-all-start.8 = ((bf16[8,64,256]{2,1,0:T(8,128)(2,1)}), bf16[8,64,256]{2,1,0:T(8,128)(2,1)S(1)}, u32[]{:S(2)}, u32[]{:S(2)}) async-start(bf16[8,64,256]{2,1,0:T(8,128)(2,1)} %bitcast.57), calls=%async_computation.8 | async-start | bytes 524288 | tf_op jit(solution)/shard_map/all_to_all | solution.py:189
  111.4 10.0 %all-to-all-start.7 = ((bf16[8,2,128]{2,1,0:T(2,128)(2,1)}), bf16[8,2,128]{2,1,0:T(2,128)(2,1)S(1)}, u32[]{:S(2)}, u32[]{:S(2)}) async-start(bf16[8,2,128]{2,1,0:T(2,128)(2,1)} %reshape.395), calls=%async_computation.7 | async-start | bytes 8192 | tf_op jit(solution)/shard_map/all_to_all | solution.py:189
  121.4 9.4 %all-to-all-start.5 = ((bf16[4,64,512]{2,1,0:T(8,128)(2,1)}), bf16[4,64,512]{2,1,0:T(8,128)(2,1)S(1)}, u32[]{:S(2)}, u32[]{:S(2)}) async-start(bf16[4,64,512]{2,1,0:T(8,128)(2,1)} %bitcast.52), calls=%async_computation.5 | async-start | bytes 524288 | tf_op jit(solution)/shard_map/all_to_all | solution.py:189
  130.8 23.8 %all-to-all-start.6 = ((bf16[8,64,3,256]{3,1,2,0:T(8,128)(2,1)}), bf16[8,64,3,256]{3,1,2,0:T(8,128)(2,1)S(1)}, u32[]{:S(2)}, u32[]{:S(2)}) async-start(bf16[8,64,3,256]{3,1,2,0:T(8,128)(2,1)} %copy.62), calls=%async_computation.6 | async-start | bytes 1572864 | tf_op jit(solution)/shard_map/all_to_all | solution.py:189
  (39 other events, 279.9 us)

commit v2 on v0

v2 whole, which is shorter than its diff:
```python
import functools

import jax
import jax.numpy as jnp
from jax import lax
from jax.experimental import pallas as pl
from jax.experimental.pallas import tpu as pltpu
from jax.sharding import PartitionSpec as P

N = 128
KW = 4
RIM = 16
LOGS = 16
NORM_EPSILON = 1e-05

F32 = jnp.float32
BF16 = jnp.bfloat16
NN = (((1,), (0,)), ((), ()))
NT = (((1,), (1,)), ((), ()))
TN = (((0,), (0,)), ((), ()))


def mm(a, b, dims=NN):
    return lax.dot_general(a.astype(BF16), b.astype(BF16), dims, preferred_element_type=F32)


def mm_exact(a, b, dims=NN):
    return lax.dot_general(
        a, b, dims, precision=lax.Precision.HIGHEST, preferred_element_type=F32
    )


def lanes_of(shape):
    return lax.broadcasted_iota(jnp.int32, shape, len(shape) - 1)


def rows_of(shape):
    return lax.broadcasted_iota(jnp.int32, shape, len(shape) - 2)


def per_row(ref, shape):
    rows = rows_of(shape)
    out = jnp.full(shape, ref[0], F32)
    for h in range(1, shape[0]):
        out = jnp.where(rows == h, ref[h], out)
    return out


def per_lane(ref, heads, width):
    head = lanes_of((1, width)) // (width // heads)
    out = jnp.full((1, width), ref[0], F32)
    for h in range(1, heads):
        out = jnp.where(head == h, ref[h], out)
    return out


def widen(cols, heads, width):
    head = lanes_of((cols.shape[0], width)) // (width // heads)
    out = jnp.broadcast_to(cols[:, 0:1], (cols.shape[0], width))
    for h in range(1, heads):
        out = jnp.where(head == h, cols[:, h : h + 1], out)
    return out


def head_mask(heads, width):
    shape = (8, width)
    return jnp.where(lanes_of(shape) // (width // heads) == rows_of(shape), 1.0, 0.0)


def only_head(x, h, heads):
    width = x.shape[1]
    return jnp.where(lanes_of(x.shape) // (width // heads) == h, x, jnp.zeros_like(x))


def columns(rows):
    short = -rows.shape[0] % 8
    if short:
        rows = jnp.concatenate([rows, jnp.zeros((short, rows.shape[1]), F32)], axis=0)
    return jnp.transpose(rows)


def sigmoid(v):
    return 1.0 / (1.0 + jnp.exp(-v))


def running_sum(x):
    width = x.shape[1]
    lanes = lanes_of(x.shape)
    hop = 1
    while hop < width:
        x = x + jnp.where(lanes >= hop, pltpu.roll(x, hop, 1), 0.0)
        hop *= 2
    return x


def running_sum_back(x):
    width = x.shape[1]
    lanes = lanes_of(x.shape)
    hop = 1
    while hop < width:
        x = x + jnp.where(lanes < width - hop, pltpu.roll(x, width - hop, 1), 0.0)
        hop *= 2
    return x


def decay_of(cols, rows, h):
    length = cols.shape[0]
    gap = cols[:, h : h + 1] - rows[h : h + 1, :]
    shape = (length, length)
    return jnp.exp(jnp.where(lanes_of(shape) <= rows_of(shape), gap, -1e30))


def fold(count, position, msg_ref, log_ref, heads, back):
    size = log_ref.shape[1] - LOGS

    def step(at, before):
        logs = log_ref[at, size:, :].astype(F32)
        logs = logs[0:heads] + logs[heads : 2 * heads] + logs[2 * heads : 3 * heads]
        scale = jnp.exp(logs)
        scale = jnp.concatenate(
            [jnp.broadcast_to(scale[h : h + 1], (size // heads, N)) for h in range(heads)], axis=0
        )
        new = scale * before + msg_ref[at, 0:size, :].astype(F32)
        reached = at > position if back else at < position
        return jnp.where(reached, new, before)

    before = jnp.zeros((size, N), F32)
    if count <= 8:
        for k in range(count):
            before = step(count - 1 - k if back else k, before)
        return before
    return lax.fori_loop(0, count, lambda k, b: step(count - 1 - k if back else k, b), before)


def project_kernel(heads, series, w, dtw, bias, rate, gate, pre, scal):
    width = w.shape[2]
    s = series[...]
    gate[...] = mm(s, w[0]).astype(BF16)
    pre[:, 0:width] = mm(s, w[1]).astype(BF16)
    pre[:, width:] = mm(s, w[2]).astype(BF16)
    raw = mm(dtw[...], s, NT)
    shifted = raw + per_row(bias, raw.shape)
    step = jnp.maximum(shifted, 0.0) + jnp.log1p(jnp.exp(-jnp.abs(shifted)))
    running = running_sum(-step * jnp.exp(per_row(rate, raw.shape)))
    scal[0:heads, :] = running
    scal[heads : 2 * heads, :] = step
    scal[2 * heads : 3 * heads, :] = sigmoid(shifted)
    scal[3 * heads :, :] = jnp.zeros_like(running)


def conv_kernel(heads, count, pre, rim, w, cw, cb, scal, x, bc, conv, own, msg, wide):
    length, both = pre.shape
    width = both // 2
    for s in range(2):
        cut = slice(s * width, (s + 1) * width)
        rims = mm(rim[...], w[1 + s]).astype(BF16).astype(F32)
        wide[0:8, cut] = rims[RIM - 8 :, :]
        wide[8:, cut] = pre[:, cut].astype(F32)
        acc = cb[s : s + 1, :] + cw[0, s : s + 1, :] * wide[5 : 5 + length, cut]
        for k in range(1, KW):
            acc = acc + cw[k, s : s + 1, :] * wide[5 + k : 5 + k + length, cut]
        conv[:, cut] = acc
        act = (acc * sigmoid(acc)).astype(BF16)
        if s == 0:
            x[...] = act
        else:
            bc[...] = act
    running = scal[0:heads, :]
    last = running[:, length - 1 : length]
    remain = jnp.exp(last - running) * scal[heads : 2 * heads, :]
    scaled = x[...].astype(F32) * widen(columns(remain), heads, width)
    state = mm(scaled, bc[:, 0:N], TN)
    own[...] = state
    last = jnp.broadcast_to(last, (heads, N))
    high = last.astype(BF16).astype(F32)
    middle = (last - high).astype(BF16).astype(F32)
    low = last - high - middle
    logs = jnp.concatenate([high, middle, low, jnp.zeros_like(low)], axis=0)
    state = state.astype(BF16)
    logs = logs.astype(BF16)
    for at in range(count):
        msg[at, 0:width, :] = state
        msg[at, width:, :] = logs


def inside_kernel(heads, x, bc, scal, skip, cot, ow, gain, y, gg):
    length, width = x.shape
    xv = x[...].astype(F32)
    rows = scal[...]
    cols = columns(rows)
    scores = mm(bc[:, N:], bc[:, 0:N], NT)
    acc = per_lane(skip, heads, width) * xv
    for h in range(heads):
        mixing = scores * decay_of(cols, rows, h) * rows[heads + h : heads + h + 1, :]
        acc = acc + mm(mixing, only_head(xv, h, heads))
    y[...] = acc
    gg[...] = gain[...] * mm(cot[...], ow[...])


def join_kernel(heads, count, pos, msg, yi, gg, gate, bc, scal, y, sin, sums):
    length, width = yi.shape
    start = fold(count, pos[0], msg, msg, heads, False)
    sin[...] = start
    grow = widen(columns(jnp.exp(scal[0:heads, :])), heads, width)
    yv = yi[...] + grow * mm(bc[:, N:], start, NT)
    y[...] = yv
    g = gate[...].astype(F32)
    gated = yv * (g * sigmoid(g))
    ones = jnp.ones((8, width), F32)
    square = mm_exact(ones, gated * gated, NT)
    inner = mm_exact(ones, gated * gg[...], NT)
    sums[...] = jnp.where(rows_of(square.shape) == 0, square, inner)


def norm_columns(total, every):
    inv = lax.rsqrt(total[0:1, :] / every + NORM_EPSILON)
    coef = inv * inv * inv * total[1:2, :] / every
    return columns(jnp.concatenate([inv, coef], axis=0))


def grad_y_kernel(heads, count, every, total, y, gate, gg, bc, scal, gy, msg):
    length, width = y.shape
    cols = norm_columns(total[...], every)
    g = gate[...].astype(F32)
    act = g * sigmoid(g)
    gated = y[...] * act
    grad = (cols[:, 0:1] * gg[...] - gated * cols[:, 1:2]) * act
    gy[...] = grad
    grow = widen(columns(jnp.exp(scal[0:heads, :])), heads, width)
    back = mm(grad * grow, bc[:, N:], TN).astype(BF16)
    for at in range(count):
        msg[at] = back


def beside_kernel(
    heads, count, parts, every,
    total, y, gate, gg, gain, gy, x, bc, scal, sin, cot, ow, series, w,
    lo_msg, wo_msg, sg, bb, gb, gc,
):
    length, width = y.shape
    depth = series.shape[1]
    cols = norm_columns(total[...], every)
    g = gate[...].astype(F32)
    sig = sigmoid(g)
    act = g * sig
    yv = y[...]
    gated = yv * act
    normed = (gated * cols[:, 0:1] * gain[...]).astype(BF16)
    out = mm(normed, ow[...], NT).astype(BF16)
    piece = length // parts
    for at in range(parts):
        lo_msg[at] = out[at * piece : (at + 1) * piece, :]
    grad_gated = cols[:, 0:1] * gg[...] - gated * cols[:, 1:2]
    grad_gate = (grad_gated * yv * (sig * (1.0 + g * (1.0 - sig)))).astype(BF16)
    sg[...] = mm(grad_gate, w[0], NT)
    w_out = mm(cot[...], normed, TN).astype(BF16)
    w_gate = mm(series[...], grad_gate, TN).astype(BF16)
    piece = depth // count
    for at in range(count):
        wo_msg[at, :, 0:width] = w_out[at * piece : (at + 1) * piece, :]
        wo_msg[at, :, width:] = w_gate[at * piece : (at + 1) * piece, :]
    rows = scal[...]
    cols = columns(rows)
    xv = x[...].astype(F32)
    gyv = gy[...]
    b, c = bc[:, 0:N], bc[:, N:]
    scores = mm(c, b, NT)
    back = jnp.zeros((length, width), F32)
    group = jnp.zeros((length, length), F32)
    for h in range(heads):
        decay = decay_of(cols, rows, h)
        gh = only_head(gyv, h, heads)
        back = back + mm(scores * decay, gh, TN)
        group = group + decay * mm(gh, xv, NT) * rows[heads + h : heads + h + 1, :]
    bb[...] = back
    gb[...] = mm(group, c, TN)
    grow = widen(columns(jnp.exp(rows[0:heads])), heads, width)
    gc[...] = mm(group, b) + mm(gyv * grow, sin[...])


def close_kernel(
    heads, count,
    pos, msg, log_msg, x, bc, scal, gy, y, bb, gb, gc, sin, own, conv, series, rim, cw, skip, rate,
    wi_msg, dt_msg, gp, edge, graw, wide,
):
    length, width = y.shape
    depth = series.shape[1]
    after = fold(count, pos[0], msg, log_msg, heads, True)
    rows = scal[...]
    running, step = rows[0:heads], rows[heads : 2 * heads]
    last = running[:, length - 1 : length]
    remain = jnp.exp(last - running)
    cols = columns(jnp.concatenate([remain, step, remain * step], axis=0))
    xv = x[...].astype(F32)
    gyv = gy[...]
    skips = per_lane(skip, heads, width)
    back = bb[...] + widen(cols, heads, width) * mm(bc[:, 0:N], after, NT)
    grad_x = skips * gyv + widen(cols[:, heads:], heads, width) * back
    mask = head_mask(heads, width)
    x_back = mm_exact(mask, xv * back, NT)[0:heads]
    y_back = mm_exact(mask, gyv * (y[...] - skips * xv), NT)[0:heads]
    whole = jnp.concatenate(
        [jnp.broadcast_to(last[h : h + 1], (width // heads, N)) for h in range(heads)], axis=0
    )
    final = jnp.exp(whole) * sin[...] + own[...]
    ends = jnp.sum(mm_exact(mask, after * final), axis=1, keepdims=True)[0:heads]
    grad_log = running_sum_back(y_back - step * x_back) + ends
    grad_step = x_back - jnp.exp(per_row(rate, x_back.shape)) * grad_log
    grad_raw = grad_step * rows[2 * heads : 3 * heads]
    grad_raw = jnp.concatenate([grad_raw, jnp.zeros_like(grad_raw)], axis=0)
    graw[...] = grad_raw
    dt = mm(grad_raw, series[...])
    piece = depth // count
    for at in range(count):
        dt_msg[at] = dt[:, at * piece : (at + 1) * piece]
    grad_b = gb[...] + mm(xv * widen(cols[:, 2 * heads :], heads, width), after)
    zeros = jnp.zeros((RIM, 2 * width), F32)
    wide[0:RIM, :] = zeros
    wide[RIM + length :, :] = zeros[0:8]
    for cut, grad in (
        (slice(0, width), grad_x),
        (slice(width, width + N), grad_b),
        (slice(width + N, 2 * width), gc[...]),
    ):
        v = conv[:, cut]
        sig = sigmoid(v)
        wide[RIM : RIM + length, cut] = grad * (sig * (1.0 + v * (1.0 - sig)))
    for s in range(2):
        cut = slice(s * width, (s + 1) * width)
        acc = cw[0, s : s + 1, :] * wide[KW - 1 : KW - 1 + RIM + length, cut]
        for k in range(1, KW):
            low = KW - 1 - k
            acc = acc + cw[k, s : s + 1, :] * wide[low : low + RIM + length, cut]
        acc = acc.astype(BF16)
        edge[:, cut] = acc[0:RIM]
        gp[:, cut] = acc[RIM:]
        grad_w = (mm(series[...], acc[RIM:], TN) + mm(rim[...], acc[0:RIM], TN)).astype(BF16)
        for at in range(count):
            wi_msg[at, :, cut] = grad_w[at * piece : (at + 1) * piece, :]


def rows_kernel(parts, sg, gp, graw, edge, w, dtw, msg):
    length = gp.shape[0]
    width = w.shape[2]
    heads = dtw.shape[0]
    total = sg[...] + mm(graw[0:heads, :], dtw[...], TN)
    total = total + mm(gp[:, 0:width], w[1], NT) + mm(gp[:, width:], w[2], NT)
    late = mm(edge[:, 0:width], w[1], NT) + mm(edge[:, width:], w[2], NT)
    piece = length // parts
    for at in range(parts - 1):
        msg[at] = total[at * piece : (at + 1) * piece, :].astype(BF16)
    tail = total[(parts - 1) * piece :, :]
    late = jnp.concatenate([jnp.zeros((piece - RIM, late.shape[1]), F32), late], axis=0)
    msg[parts - 1] = (tail + late).astype(BF16)


def total_kernel(count, width, wo, wi, w_in, w_out):
    def sum_of(ref, cut):
        acc = ref[0, :, cut].astype(F32)
        if count <= 8:
            for at in range(1, count):
                acc = acc + ref[at, :, cut].astype(F32)
            return acc
        return lax.fori_loop(1, count, lambda at, a: a + ref[at, :, cut].astype(F32), acc)

    w_out[...] = sum_of(wo, slice(0, width))
    w_in[0] = sum_of(wo, slice(width, 2 * width))
    w_in[1] = sum_of(wi, slice(0, width))
    w_in[2] = sum_of(wi, slice(width, 2 * width))


VMEM = pl.BlockSpec(memory_space=pltpu.VMEM)
SMEM = pl.BlockSpec(memory_space=pltpu.SMEM)


def run(kernel, name, outs, args, scalars=(), scratch=(), flops=10**8):
    moved = sum(a.size * a.dtype.itemsize for a in args)
    return pl.pallas_call(
        kernel,
        name=name,
        out_shape=[jax.ShapeDtypeStruct(shape, kind) for shape, kind in outs],
        in_specs=[SMEM if i in scalars else VMEM for i in range(len(args))],
        out_specs=[VMEM] * len(outs),
        scratch_shapes=list(scratch),
        compiler_params=pltpu.CompilerParams(vmem_limit_bytes=40 * 2**20),
        cost_estimate=pl.CostEstimate(flops=flops, bytes_accessed=2 * moved, transcendentals=0),
    )(*args)


def shifted(block, axis, distance):
    devices = range(lax.axis_size(axis))
    route = [(i - distance, i) for i in devices if i - distance in devices]
    return lax.ppermute(block, axis, route)


def exchange(blocks, axis):
    return lax.all_to_all(blocks, axis, 0, 0)


def body(
    series,
    in_weight,
    step_weight,
    step_bias,
    log_rate,
    conv_weight,
    conv_bias,
    skip_gain,
    norm_gain,
    out_weight,
    cotangent,
):
    length, depth = series.shape
    width = in_weight.shape[2]
    heads = step_weight.shape[1]
    count = lax.axis_size("tm")
    parts = lax.axis_size("head")
    every = width * parts
    assert width == 2 * N and heads == 4
    part = functools.partial
    w = in_weight.transpose(1, 0, 2)
    dtw = step_weight.T
    gain = norm_gain.reshape(1, width)
    position = lax.axis_index("tm").astype(jnp.int32).reshape(1)
    rim = shifted(series[length - RIM :], "tm", 1)

    gate, pre, scal = run(
        part(project_kernel, heads), "project",
        [((length, width), BF16), ((length, 2 * width), BF16), ((4 * heads, length), F32)],
        [series, w, dtw, step_bias, log_rate], (3, 4),
    )
    x, bc, conv, own, msg = run(
        part(conv_kernel, heads, count), "conv",
        [
            ((length, width), BF16),
            ((length, width), BF16),
            ((length, 2 * width), F32),
            ((width, N), F32),
            ((count, width + LOGS, N), BF16),
        ],
        [pre, rim, w, conv_weight, conv_bias, scal],
        scratch=[pltpu.VMEM((length + 8, 2 * width), F32)],
    )
    msg = exchange(msg, "tm")
    inside, gg = run(
        part(inside_kernel, heads), "inside",
        [((length, width), F32), ((length, width), F32)],
        [x, bc, scal, skip_gain, cotangent, out_weight, gain], (3,),
    )
    y, sin, sums = run(
        part(join_kernel, heads, count), "join",
        [((length, width), F32), ((width, N), F32), ((8, length), F32)],
        [position, msg, inside, gg, gate, bc, scal], (0,),
    )
    total = lax.psum(sums, "head")
    gy, back = run(
        part(grad_y_kernel, heads, count, every), "grad_y",
        [((length, width), F32), ((count, width, N), BF16)],
        [total, y, gate, gg, bc, scal],
    )
    back = exchange(back, "tm")
    lo_msg, wo_msg, sg, bb, gb, gc = run(
        part(beside_kernel, heads, count, parts, every), "beside",
        [
            ((parts, length // parts, depth), BF16),
            ((count, depth // count, 2 * width), BF16),
            ((length, depth), F32),
            ((length, width), F32),
            ((length, N), F32),
            ((length, N), F32),
        ],
        [total, y, gate, gg, gain, gy, x, bc, scal, sin, cotangent, out_weight, series, w],
    )
    lo_msg = exchange(lo_msg, "head")
    layer_out = jnp.sum(lo_msg.astype(F32), axis=0).astype(BF16)
    wo_msg = exchange(wo_msg, "tm")
    wi_msg, dt_msg, gp, edge, graw = run(
        part(close_kernel, heads, count), "close",
        [
            ((count, depth // count, 2 * width), BF16),
            ((count, 2 * heads, depth // count), F32),
            ((length, 2 * width), BF16),
            ((RIM, 2 * width), BF16),
            ((2 * heads, length), F32),
        ],
        [
            position, back, msg, x, bc, scal, gy, y, bb, gb, gc, sin, own, conv, series, rim,
            conv_weight, skip_gain, log_rate,
        ],
        (0, 17, 18),
        scratch=[pltpu.VMEM((length + RIM + 8, 2 * width), F32)],
    )
    wi_msg = exchange(wi_msg, "tm")
    edge = shifted(edge, "tm", -1)
    (sg_msg,) = run(
        part(rows_kernel, parts), "rows",
        [((parts, length // parts, depth), BF16)],
        [sg, gp, graw, edge, w, dtw],
    )
    sg_msg = exchange(sg_msg, "head")
    series_grad = jnp.sum(sg_msg.astype(F32), axis=0)
    dt_msg = exchange(dt_msg, "tm")
    w_dt_grad = jnp.sum(dt_msg, axis=0)[0:heads].T
    w_in_grad, w_out_grad = run(
        part(total_kernel, count, width), "total",
        [((3, depth // count, width), F32), ((depth // count, width), F32)],
        [wo_msg, wi_msg],
    )
    return (layer_out, series_grad, w_in_grad.transpose(1, 0, 2), w_dt_grad, w_out_grad)


def solution(mesh):
    in_specs = (
        P("tm", None),
        P(None, None, "head"),
        P(None, "head"),
        P("head"),
        P("head"),
        P(None, None, "head"),
        P(None, "head"),
        P("head"),
        P("head"),
        P(None, "head"),
        P("tm", None),
    )
    out_specs = (
        P(("tm", "head"), None),
        P(("tm", "head"), None),
        P("tm", None, "head"),
        P("tm", "head"),
        P("tm", "head"),
    )
    return jax.shard_map(body, mesh=mesh, in_specs=in_specs, out_specs=out_specs, check_vma=False)
```

time: 371 us -> 134 us (0.36)
  waiting for transfers between devices: 261 us -> 31.5 us
  other arithmetic: 27.9 us -> 2.06 us
  starting transfers between devices: 6.45 us -> 24.7 us
  matrix products: 17.1 us -> 0 us
  blocking collectives: 25.4 us -> 42 us
  between operations: 14.9 us -> 0.85 us
  Pallas kernels: 0 us -> 12.9 us
    unnamed x9 -> x0, waiting for transfers between devices: 111 us -> none
    reduce_scatter x3 -> x0, waiting for transfers between devices: 93.6 us -> none  [the longest x1 70 us: body(): lax.psum_scatter(grad_in, 'tm', scatter_dimension=0, tiled=True)]
    all_gather x2 -> x0, waiting for transfers between devices: 53.5 us -> none  [carried_in(): everything = jax.tree.map(lambda part: lax.all_gather(part, axis), x)]
    all_to_all x0 -> x3, blocking collectives: none -> 36.2 us  [exchange(): return lax.all_to_all(blocks, axis, 0, 0)]
    all_to_all x0 -> x4, waiting for transfers between devices: none -> 27.2 us  [exchange(): return lax.all_to_all(blocks, axis, 0, 0)]
    all_gather x1 -> x0, blocking collectives: 19.8 us -> none  [carried_in(): everything = jax.tree.map(lambda part: lax.all_gather(part, axis), x)]
    all_to_all x0 -> x4, starting transfers between devices: none -> 18.5 us  [exchange(): return lax.all_to_all(blocks, axis, 0, 0)]
    dot_general x22 -> x0, matrix products: 17.1 us -> none  [the longest x6 4.14 us: contract(): lax.dot_general(left_side, right_side, (((left_dim,), (right_dim,)), ((),...]
  transfers between devices with their start and end apart: 9 -> 6, of which waited for: 7 -> 4; matrix products, arithmetic and copies ran while one was open for 12% -> 3% of each run, Pallas kernels for 0% -> 5%
where the time goes in v2:
time: 134 us; the launch traced here: 133 us
  blocking collectives  42 us (31%)
  waiting for transfers between devices  31.5 us (24%)
  starting transfers between devices  24.7 us (18%)
  local copies, waits for them, and re-layouts  18.6 us (14%)
  Pallas kernels  12.9 us (10%)
  other arithmetic  2.06 us (2%)
    all_to_all x3, blocking collectives, exchange(): return lax.all_to_all(blocks, axis, 0, 0)  36.2 us
    all_to_all x4, waiting for transfers between devices, exchange(): return lax.all_to_all(blocks, axis, 0, 0)  27.2 us
    all_to_all x4, starting transfers between devices, exchange(): return lax.all_to_all(blocks, axis, 0, 0)  18.5 us
    unnamed x68, local copies, waits for them, and re-layouts  16.7 us
    pallas_call x9, Pallas kernels, run(): pl.pallas_call(kernel, name=name, out_shape=[jax.ShapeDtypeStruct(shape,...  12.9 us
    ppermute x2, starting transfers between devices, shifted(): return lax.ppermute(block, axis, route)  6.14 us
    psum x1, blocking collectives, body(): total = lax.psum(sums, 'head')  5.77 us
    ppermute x2, waiting for transfers between devices, shifted(): return lax.ppermute(block, axis, route)  4.36 us
  transfers between devices with their start and end apart: 6, of which 4 were waited for; matrix products, arithmetic and copies ran while one was open for 3% of the time, Pallas kernels for 5%

profile of v2, /device:TPU:0, one launch (start us, length us, event | category | flops | bytes accessed | tf_op | source)
XLA Modules:
  0.0 132.6 jit_solution(7109203608914580303)
XLA Ops:
  1.4 4.9 %collective-permute-start = (bf16[16,512]{1,0:T(8,128)(2,1)S(1)}, bf16[16,512]{1,0:T(8,128)(2,1)S(1)}, u32[]{:S(2)}, u32[]{:S(2)}) collective-permute-start(bf16[16,512]{1,0:T(8,128)(2,1)S(1)} %slice.6), channel_id=1, source_target_pairs={{0,4},{4,8},{8,12},{12,16},{16,20},{20,24},{24,28},{1,5},{5,9},{9,... | collective-permute-start | bytes 49160 | tf_op jit(solution)/shard_map/ppermute | solution.py:393
  6.9 1.1 copy-done
  8.0 0.9 copy-done.2
  9.0 1.5 %project.1 = (bf16[256,256]{1,0:T(8,128)(2,1)S(1)}, bf16[256,512]{1,0:T(8,128)(2,1)S(1)}, f32[16,256]{1,0:T(8,128)S(1)}) custom-call(bf16[256,512]{1,0:T(8,128)(2,1)S(1)} %copy-done.2, bf16[3,512,256]{2,1,0:T(8,128)(2,1)S(1)} %bitcast.7, bf16[4,512]{1,0:T(4,128)(2,1)S(1)} %bitcast.11, f32[4]{0:T(128)S(1)} %copy-done.31, f32[4]{0:T(128)S(1)} %copy-done.29), custom_call_target="tpu_custom_call" | custom-call | flops 100000000 | bytes 2105408 | tf_op jit(solution)/shard_map/project/pallas_call | solution.py:378
  11.2 1.8 %conv.1 = (bf16[256,256]{1,0:T(8,128)(2,1)S(1)}, bf16[256,256]{1,0:T(8,128)(2,1)S(1)}, f32[256,512]{1,0:T(8,128)S(1)}, f32[256,128]{1,0:T(8,128)S(1)}, bf16[8,272,128]{2,1,0:T(8,128)(2,1)}) custom-call(bf16[256,512]{1,0:T(8,128)(2,1)S(1)} %get-tuple-element.33.pre, bf16[16,512]{1,0:T(8,128)(2,1)S(1)} %collective-permute-done.rim, ...), custom_call_target="tpu_custom_call" | custom-call | flops 100000000 | bytes 2183168 | tf_op jit(solution)/shard_map/conv/pallas_call | solution.py:378
  14.4 5.0 %all-to-all-start = ((bf16[8,272,128]{2,1,0:T(8,128)(2,1)}), bf16[8,272,128]{2,1,0:T(8,128)(2,1)S(1)}, u32[]{:S(2)}, u32[]{:S(2)}) async-start(bf16[8,272,128]{2,1,0:T(8,128)(2,1)} %get-tuple-element.35), calls=%async_computation | async-start | bytes 1114112 | tf_op jit(solution)/shard_map/all_to_all | solution.py:397
  20.1 1.2 inside.1
  21.3 13.1 %all-to-all-done.msg.log_msg = bf16[8,272,128]{2,1,0:T(8,128)(2,1)S(1)} async-done(((bf16[8,272,128]{2,1,0:T(8,128)(2,1)}), bf16[8,272,128]{2,1,0:T(8,128)(2,1)S(1)}, u32[]{:S(2)}, u32[]{:S(2)}) %all-to-all-start) | async-done | bytes 557088 | tf_op jit(solution)/shard_map/all_to_all | solution.py:397
  35.2 5.8 %psum.7.total = f32[8,256]{1,0:T(8,128)S(1)} all-reduce(f32[8,256]{1,0:T(8,128)S(1)} %get-tuple-element.41), channel_id=1, replica_groups=mesh['tm'=8,'head'=4] {'head'}, use_global_device_ids=true, to_apply=%region_0.0 | all-reduce | flops 2048 | bytes 16384 | tf_op jit(solution)/shard_map/psum | solution.py:455
  42.0 1.8 %beside.1 = (bf16[4,64,512]{2,1,0:T(8,128)(2,1)S(1)}, bf16[8,64,512]{2,1,0:T(8,128)(2,1)S(1)}, f32[256,512]{1,0:T(8,128)S(1)}, f32[256,256]{1,0:T(8,128)S(1)}, f...) custom-call(f32[8,256]{1,0:T(8,128)S(1)} %psum.7.total, f32[256,256]{1,0:T(8,128)S(1)} %get-tuple-element.42.y, ...), custom_call_target="tpu_custom_call" | custom-call | flops 100000000 | bytes 5818368 | tf_op jit(solution)/shard_map/beside/pallas_call | solution.py:378
  45.8 9.1 %all_to_all.35 = bf16[4,64,512]{2,1,0:T(8,128)(2,1)} all-to-all(bf16[4,64,512]{2,1,0:T(8,128)(2,1)S(1)} %get-tuple-element.45), channel_id=1, replica_groups=mesh['tm'=8,'head'=4] {'head'}, dimensions={0} | all-to-all | bytes 524288 | tf_op jit(solution)/shard_map/all_to_all | solution.py:397
  54.8 18.7 %all_to_all.36.msg = bf16[8,256,128]{2,1,0:T(8,128)(2,1)S(1)} all-to-all(bf16[8,256,128]{2,1,0:T(8,128)(2,1)S(1)} %get-tuple-element.47), channel_id=1, replica_groups=mesh['tm'=8,'head'=4] {'tm'}, dimensions={0} | all-to-all | bytes 1048576 | tf_op jit(solution)/shard_map/all_to_all | solution.py:397
  73.6 3.8 %all-to-all-start.4 = ((bf16[8,64,512]{2,1,0:T(8,128)(2,1)}), bf16[8,64,512]{2,1,0:T(8,128)(2,1)S(1)}, u32[]{:S(2)}, u32[]{:S(2)}) async-start(bf16[8,64,512]{2,1,0:T(8,128)(2,1)} %copy-done.10), calls=%async_computation.4 | async-start | bytes 1048576 | tf_op jit(solution)/shard_map/all_to_all | solution.py:397
  77.4 1.0 copy-done.12
  79.3 0.9 copy-done.18
  83.0 3.8 %close.1 = (bf16[8,64,512]{2,1,0:T(8,128)(2,1)}, f32[8,8,64]{2,1,0:T(8,128)S(1)}, bf16[256,512]{1,0:T(8,128)(2,1)S(1)}, bf16[16,512]{1,0:T(8,128)(2,1)S(1)}, f32[8,256]{1,0:T(8,128)S(1)}) custom-call(s32[1]{0:T(128)} %bitcast.pos, bf16[8,256,128]{2,1,0:T(8,128)(2,1)S(1)} %all_to_all.36.msg, bf16[8,272,128]{2,1,0:T(8,128)(2,1)S(1)} %all-to-all-done.msg.log_msg, ...), custom_call_target="tpu_custom_call" | custom-call | flops 100000000 | bytes 6963272 | tf_op jit(solution)/shard_map/close/pallas_call | solution.py:378
  88.2 3.2 %all-to-all-done.4.wo = bf16[8,64,512]{2,1,0:T(8,128)(2,1)S(1)} async-done(((bf16[8,64,512]{2,1,0:T(8,128)(2,1)}), bf16[8,64,512]{2,1,0:T(8,128)(2,1)S(1)}, u32[]{:S(2)}, u32[]{:S(2)}) %all-to-all-start.4) | async-done | bytes 524320 | tf_op jit(solution)/shard_map/all_to_all | solution.py:397
  91.4 3.6 %all-to-all-start.6 = ((f32[8,1,512]{2,1,0:T(1,128)}), f32[8,1,512]{2,1,0:T(1,128)S(1)}, u32[]{:S(2)}, u32[]{:S(2)}) async-start(f32[8,1,512]{2,1,0:T(1,128)} %reshape.18), calls=%async_computation.6 | async-start | bytes 32768 | tf_op jit(solution)/shard_map/all_to_all | solution.py:397
  95.0 1.3 collective-permute-start.1
  96.3 4.4 %collective-permute-done.1.edge = bf16[16,512]{1,0:T(8,128)(2,1)S(1)} collective-permute-done((bf16[16,512]{1,0:T(8,128)(2,1)S(1)}, bf16[16,512]{1,0:T(8,128)(2,1)S(1)}, u32[]{:S(2)}, u32[]{:S(2)}) %collective-permute-start.1) | collective-permute-done | bytes 16416 | tf_op jit(solution)/shard_map/ppermute | solution.py:393
  100.7 1.0 copy-done.9
  103.1 8.4 %all_to_all.37 = bf16[4,64,512]{2,1,0:T(8,128)(2,1)S(1)} all-to-all(bf16[4,64,512]{2,1,0:T(8,128)(2,1)S(1)} %rows.1), channel_id=1, replica_groups=mesh['tm'=8,'head'=4] {'head'}, dimensions={0} | all-to-all | bytes 524288 | tf_op jit(solution)/shard_map/all_to_all | solution.py:397
  111.5 6.1 %all-to-all-start.5 = ((bf16[8,64,512]{2,1,0:T(8,128)(2,1)}), bf16[8,64,512]{2,1,0:T(8,128)(2,1)S(1)}, u32[]{:S(2)}, u32[]{:S(2)}) async-start(bf16[8,64,512]{2,1,0:T(8,128)(2,1)} %get-tuple-element.57), calls=%async_computation.5 | async-start | bytes 1048576 | tf_op jit(solution)/shard_map/all_to_all | solution.py:397
  120.9 10.9 %all-to-all-done.5.wi = bf16[8,64,512]{2,1,0:T(8,128)(2,1)S(1)} async-done(((bf16[8,64,512]{2,1,0:T(8,128)(2,1)}), bf16[8,64,512]{2,1,0:T(8,128)(2,1)S(1)}, u32[]{:S(2)}, u32[]{:S(2)}) %all-to-all-start.5) | async-done | bytes 524320 | tf_op jit(solution)/shard_map/all_to_all | solution.py:397
  (76 shorter events, 18.4 us)
Async XLA Ops:
  0.6 5.6 %copy-start.26 = (bf16[512,4]{0,1:T(4,128)(2,1)S(1)}, bf16[512,4]{0,1:T(4,128)(2,1)}, u32[]{:S(2)}) copy-start(bf16[512,4]{0,1:T(4,128)(2,1)} %param.13) | copy-start | bytes 12292
  1.4 9.1 %collective-permute-start = (bf16[16,512]{1,0:T(8,128)(2,1)S(1)}, bf16[16,512]{1,0:T(8,128)(2,1)S(1)}, u32[]{:S(2)}, u32[]{:S(2)}) collective-permute-start(bf16[16,512]{1,0:T(8,128)(2,1)S(1)} %slice.6), channel_id=1, source_target_pairs={{0,4},{4,8},{8,12},{12,16},{16,20},{20,24},{24,28},{1,5},{5,9},{9,... | collective-permute-start | bytes 49160 | tf_op jit(solution)/shard_map/ppermute | solution.py:393
  6.9 1.1 copy-start
  8.0 0.9 copy-start.2
  9.0 1.5 %copy-start.1 = (bf16[512,3,256]{2,0,1:T(8,128)(2,1)S(1)}, bf16[512,3,256]{2,0,1:T(8,128)(2,1)}, u32[]{:S(2)}) copy-start(bf16[512,3,256]{2,0,1:T(8,128)(2,1)} %param.12) | copy-start | bytes 2359300
  9.0 1.5 %copy-start.25 = (f32[4,2,256]{2,1,0:T(2,128)S(1)}, f32[4,2,256]{2,1,0:T(2,128)}, u32[]{:S(2)}) copy-start(f32[4,2,256]{2,1,0:T(2,128)} %cw.3) | copy-start | bytes 24580
  14.4 5.0 %copy-start.4 = (bf16[256,512]{1,0:T(8,128)(2,1)S(1)}, bf16[256,512]{1,0:T(8,128)(2,1)}, u32[]{:S(2)}) copy-start(bf16[256,512]{1,0:T(8,128)(2,1)} %cot.3) | copy-start | bytes 786436
  14.4 5.0 %copy-start.5 = (bf16[512,256]{1,0:T(8,128)(2,1)S(1)}, bf16[512,256]{1,0:T(8,128)(2,1)}, u32[]{:S(2)}) copy-start(bf16[512,256]{1,0:T(8,128)(2,1)} %ow.3) | copy-start | bytes 786436
  14.4 20.0 %all-to-all-start = ((bf16[8,272,128]{2,1,0:T(8,128)(2,1)}), bf16[8,272,128]{2,1,0:T(8,128)(2,1)S(1)}, u32[]{:S(2)}, u32[]{:S(2)}) async-start(bf16[8,272,128]{2,1,0:T(8,128)(2,1)} %get-tuple-element.35), calls=%async_computation | async-start | bytes 1114112 | tf_op jit(solution)/shard_map/all_to_all | solution.py:397
  35.2 6.6 %copy-start.13 = (f32[256,128]{1,0:T(8,128)}, f32[256,128]{1,0:T(8,128)S(1)}, u32[]{:S(2)}) copy-start(f32[256,128]{1,0:T(8,128)S(1)} %get-tuple-element.44.sin) | copy-start | bytes 393220
  41.0 1.0 copy-start.3
  41.8 2.0 %copy-start.6 = (f32[256,256]{1,0:T(8,128)}, f32[256,256]{1,0:T(8,128)S(1)}, u32[]{:S(2)}) copy-start(f32[256,256]{1,0:T(8,128)S(1)} %get-tuple-element.43.gy) | copy-start | bytes 786436
  45.7 27.8 %copy-start.8 = (f32[256,512]{1,0:T(8,128)}, f32[256,512]{1,0:T(8,128)S(1)}, u32[]{:S(2)}) copy-start(f32[256,512]{1,0:T(8,128)S(1)} %get-tuple-element.46.sg) | copy-start | bytes 1572868
  45.7 27.8 %copy-start.10 = (bf16[8,64,512]{2,1,0:T(8,128)(2,1)}, bf16[8,64,512]{2,1,0:T(8,128)(2,1)S(1)}, u32[]{:S(2)}) copy-start(bf16[8,64,512]{2,1,0:T(8,128)(2,1)S(1)} %get-tuple-element.56) | copy-start | bytes 1572868
  73.6 3.8 %copy-start.7 = (f32[256,256]{1,0:T(8,128)S(1)}, f32[256,256]{1,0:T(8,128)}, u32[]{:S(2)}) copy-start(f32[256,256]{1,0:T(8,128)} %copy-done.6) | copy-start | bytes 786436
  73.6 17.8 %all-to-all-start.4 = ((bf16[8,64,512]{2,1,0:T(8,128)(2,1)}), bf16[8,64,512]{2,1,0:T(8,128)(2,1)S(1)}, u32[]{:S(2)}, u32[]{:S(2)}) async-start(bf16[8,64,512]{2,1,0:T(8,128)(2,1)} %copy-done.10), calls=%async_computation.4 | async-start | bytes 1048576 | tf_op jit(solution)/shard_map/all_to_all | solution.py:397
  77.3 1.0 copy-start.12
  79.3 0.9 copy-start.18
  91.4 11.7 %all-to-all-start.6 = ((f32[8,1,512]{2,1,0:T(1,128)}), f32[8,1,512]{2,1,0:T(1,128)S(1)}, u32[]{:S(2)}, u32[]{:S(2)}) async-start(f32[8,1,512]{2,1,0:T(1,128)} %reshape.18), calls=%async_computation.6 | async-start | bytes 32768 | tf_op jit(solution)/shard_map/all_to_all | solution.py:397
  95.0 5.6 %collective-permute-start.1 = (bf16[16,512]{1,0:T(8,128)(2,1)S(1)}, bf16[16,512]{1,0:T(8,128)(2,1)S(1)}, u32[]{:S(2)}, u32[]{:S(2)}) collective-permute-start(bf16[16,512]{1,0:T(8,128)(2,1)S(1)} %get-tuple-element.55), channel_id=1, source_target_pairs={{4,0},{8,4},{12,8},{16,12},{20,16},{24,20},{28,24},{5,1},{9,5},{13... | collective-permute-start | bytes 49160 | tf_op jit(solution)/shard_map/ppermute | solution.py:393
  100.7 1.0 copy-start.9
  101.7 0.9 copy-start.16
  111.5 6.1 %copy-start.32 = (bf16[4,64,512]{2,1,0:T(8,128)(2,1)S(1)}, bf16[4,64,512]{2,1,0:T(8,128)(2,1)}, u32[]{:S(2)}) copy-start(bf16[4,64,512]{2,1,0:T(8,128)(2,1)} %all_to_all.35) | copy-start | bytes 786436
  111.5 20.3 %all-to-all-start.5 = ((bf16[8,64,512]{2,1,0:T(8,128)(2,1)}), bf16[8,64,512]{2,1,0:T(8,128)(2,1)S(1)}, u32[]{:S(2)}, u32[]{:S(2)}) async-start(bf16[8,64,512]{2,1,0:T(8,128)(2,1)} %get-tuple-element.57), calls=%async_computation.5 | async-start | bytes 1048576 | tf_op jit(solution)/shard_map/all_to_all | solution.py:397
  (15 other events, 11.1 us)

commit v3 on v2

v3 whole, which is shorter than its diff:
```python
import functools

import jax
import jax.numpy as jnp
from jax import lax
from jax.experimental import pallas as pl
from jax.experimental.pallas import tpu as pltpu
from jax.sharding import PartitionSpec as P

N = 128
KW = 4
RIM = 16
LOGS = 16
NORM_EPSILON = 1e-05

F32 = jnp.float32
BF16 = jnp.bfloat16
NN = (((1,), (0,)), ((), ()))
NT = (((1,), (1,)), ((), ()))
TN = (((0,), (0,)), ((), ()))


def mm(a, b, dims=NN):
    return lax.dot_general(a.astype(BF16), b.astype(BF16), dims, preferred_element_type=F32)


def mm_exact(a, b, dims=NN):
    return lax.dot_general(
        a, b, dims, precision=lax.Precision.HIGHEST, preferred_element_type=F32
    )


def lanes_of(shape):
    return lax.broadcasted_iota(jnp.int32, shape, len(shape) - 1)


def rows_of(shape):
    return lax.broadcasted_iota(jnp.int32, shape, len(shape) - 2)


def per_row(ref, shape):
    rows = rows_of(shape)
    out = jnp.full(shape, ref[0], F32)
    for h in range(1, shape[0]):
        out = jnp.where(rows == h, ref[h], out)
    return out


def per_lane(ref, heads, width):
    head = lanes_of((1, width)) // (width // heads)
    out = jnp.full((1, width), ref[0], F32)
    for h in range(1, heads):
        out = jnp.where(head == h, ref[h], out)
    return out


def widen(cols, heads, width):
    head = lanes_of((cols.shape[0], width)) // (width // heads)
    out = jnp.broadcast_to(cols[:, 0:1], (cols.shape[0], width))
    for h in range(1, heads):
        out = jnp.where(head == h, cols[:, h : h + 1], out)
    return out


def head_mask(heads, width):
    shape = (8, width)
    return jnp.where(lanes_of(shape) // (width // heads) == rows_of(shape), 1.0, 0.0)


def only_head(x, h, heads):
    width = x.shape[1]
    return jnp.where(lanes_of(x.shape) // (width // heads) == h, x, jnp.zeros_like(x))


def columns(rows):
    short = -rows.shape[0] % 8
    if short:
        rows = jnp.concatenate([rows, jnp.zeros((short, rows.shape[1]), F32)], axis=0)
    return jnp.transpose(rows)


def sigmoid(v):
    return 1.0 / (1.0 + jnp.exp(-v))


def running_sum(x):
    width = x.shape[1]
    lanes = lanes_of(x.shape)
    hop = 1
    while hop < width:
        x = x + jnp.where(lanes >= hop, pltpu.roll(x, hop, 1), 0.0)
        hop *= 2
    return x


def running_sum_back(x):
    width = x.shape[1]
    lanes = lanes_of(x.shape)
    hop = 1
    while hop < width:
        x = x + jnp.where(lanes < width - hop, pltpu.roll(x, width - hop, 1), 0.0)
        hop *= 2
    return x


def decay_of(cols, rows, h):
    length = cols.shape[0]
    gap = cols[:, h : h + 1] - rows[h : h + 1, :]
    shape = (length, length)
    return jnp.exp(jnp.where(lanes_of(shape) <= rows_of(shape), gap, -1e30))


def logs_of(msg, heads):
    logs = msg[msg.shape[0] - LOGS :].astype(F32)
    return logs[0:heads] + logs[heads : 2 * heads] + logs[2 * heads : 3 * heads]


def spread_rows(logs, heads, size):
    return jnp.concatenate(
        [jnp.broadcast_to(logs[h : h + 1], (size // heads, N)) for h in range(heads)], axis=0
    )


def state_of(msg):
    return msg[0 : msg.shape[0] - LOGS].astype(F32)


def packed(state, logs):
    high = logs.astype(BF16).astype(F32)
    middle = (logs - high).astype(BF16).astype(F32)
    low = logs - high - middle
    logs = jnp.concatenate([high, middle, low, jnp.zeros_like(low)], axis=0)
    return jnp.concatenate([state.astype(BF16), logs.astype(BF16)], axis=0)


def carried(own_turn, partner, others, heads):
    state = jnp.zeros((partner.shape[0] - LOGS, N), F32)
    size = state.shape[0]
    for msg in others:
        state = jnp.exp(spread_rows(logs_of(msg, heads), heads, size)) * state + state_of(msg)
    with_partner = jnp.exp(spread_rows(logs_of(partner, heads), heads, size)) * state
    return jnp.where(own_turn, with_partner + state_of(partner), state)


def project_kernel(heads, series, w, dtw, bias, rate, gate, pre, scal):
    width = w.shape[2]
    s = series[...]
    gate[...] = mm(s, w[0]).astype(BF16)
    pre[:, 0:width] = mm(s, w[1]).astype(BF16)
    pre[:, width:] = mm(s, w[2]).astype(BF16)
    raw = mm(dtw[...], s, NT)
    shifted = raw + per_row(bias, raw.shape)
    step = jnp.maximum(shifted, 0.0) + jnp.log1p(jnp.exp(-jnp.abs(shifted)))
    running = running_sum(-step * jnp.exp(per_row(rate, raw.shape)))
    scal[0:heads, :] = running
    scal[heads : 2 * heads, :] = step
    scal[2 * heads : 3 * heads, :] = sigmoid(shifted)
    scal[3 * heads :, :] = jnp.zeros_like(running)


def conv_kernel(heads, pre, rim, w, cw, cb, scal, x, bc, conv, own, msg, wide):
    length, both = pre.shape
    width = both // 2
    for s in range(2):
        cut = slice(s * width, (s + 1) * width)
        rims = mm(rim[...], w[1 + s]).astype(BF16).astype(F32)
        wide[0:8, cut] = rims[RIM - 8 :, :]
        wide[8:, cut] = pre[:, cut].astype(F32)
        acc = cb[s : s + 1, :] + cw[0, s : s + 1, :] * wide[5 : 5 + length, cut]
        for k in range(1, KW):
            acc = acc + cw[k, s : s + 1, :] * wide[5 + k : 5 + k + length, cut]
        conv[:, cut] = acc
        act = (acc * sigmoid(acc)).astype(BF16)
        if s == 0:
            x[...] = act
        else:
            bc[...] = act
    running = scal[0:heads, :]
    last = running[:, length - 1 : length]
    remain = jnp.exp(last - running) * scal[heads : 2 * heads, :]
    scaled = x[...].astype(F32) * widen(columns(remain), heads, width)
    state = mm(scaled, bc[:, 0:N], TN)
    own[...] = state
    msg[...] = packed(state, jnp.broadcast_to(last, (heads, N)))


def pair_kernel(heads, back, low, mine, other, msg):
    mine, other = mine[...], other[...]
    size = mine.shape[0] - LOGS
    mine_first = low[0] == 0
    mine_logs, other_logs = logs_of(mine, heads), logs_of(other, heads)
    crossed = jnp.logical_not(mine_first) if back else mine_first
    mine_scale = jnp.where(crossed, jnp.exp(other_logs), 1.0)
    other_scale = jnp.where(crossed, 1.0, jnp.exp(mine_logs))
    state = spread_rows(mine_scale, heads, size) * state_of(mine)
    state = state + spread_rows(other_scale, heads, size) * state_of(other)
    msg[...] = packed(state, mine_logs + other_logs)


def inside_kernel(heads, x, bc, scal, skip, cot, ow, gain, conv, y, gg, slope):
    length, width = x.shape
    xv = x[...].astype(F32)
    rows = scal[...]
    cols = columns(rows)
    scores = mm(bc[:, N:], bc[:, 0:N], NT)
    acc = per_lane(skip, heads, width) * xv
    for h in range(heads):
        mixing = scores * decay_of(cols, rows, h) * rows[heads + h : heads + h + 1, :]
        acc = acc + mm(mixing, only_head(xv, h, heads))
    y[...] = acc
    gg[...] = gain[...] * mm(cot[...], ow[...])
    v = conv[...]
    sig = sigmoid(v)
    slope[...] = sig * (1.0 + v * (1.0 - sig))


def join_kernel(heads, low, yi, gg, gate, bc, scal, partner, *rest):
    *others, y, sin, sums = rest
    length, width = yi.shape
    start = carried(low[0] == 1, partner[...], [o[...] for o in others], heads)
    sin[...] = start
    grow = widen(columns(jnp.exp(scal[0:heads, :])), heads, width)
    yv = yi[...] + grow * mm(bc[:, N:], start, NT)
    y[...] = yv
    g = gate[...].astype(F32)
    gated = yv * (g * sigmoid(g))
    ones = jnp.ones((8, width), F32)
    square = mm_exact(ones, gated * gated, NT)
    inner = mm_exact(ones, gated * gg[...], NT)
    sums[...] = jnp.where(rows_of(square.shape) == 0, square, inner)


def norm_columns(total, every):
    inv = lax.rsqrt(total[0:1, :] / every + NORM_EPSILON)
    coef = inv * inv * inv * total[1:2, :] / every
    return columns(jnp.concatenate([inv, coef], axis=0))


def grad_y_kernel(heads, every, total, y, gate, gg, bc, scal, gy, msg):
    length, width = y.shape
    cols = norm_columns(total[...], every)
    g = gate[...].astype(F32)
    act = g * sigmoid(g)
    gated = y[...] * act
    grad = (cols[:, 0:1] * gg[...] - gated * cols[:, 1:2]) * act
    gy[...] = grad
    grow = widen(columns(jnp.exp(scal[0:heads, :])), heads, width)
    last = scal[0:heads, length - 1 : length]
    msg[...] = packed(mm(grad * grow, bc[:, N:], TN), jnp.broadcast_to(last, (heads, N)))


def conv_back(cw, wide, cut, length, slot, slot_cut):
    acc = cw[0, slot : slot + 1, slot_cut] * wide[KW - 1 : KW - 1 + RIM + length, cut]
    for k in range(1, KW):
        at = KW - 1 - k
        acc = acc + cw[k, slot : slot + 1, slot_cut] * wide[at : at + RIM + length, cut]
    return acc.astype(BF16)


def clear_ends(wide, length):
    zeros = jnp.zeros((RIM, wide.shape[1]), F32)
    wide[0:RIM, :] = zeros
    wide[RIM + length :, :] = zeros[0:8]


def stack_columns(msg, grad, at, base, piece):
    for q in range(grad.shape[1] // N):
        msg[at, (base + q) * piece : (base + q + 1) * piece, :] = grad[
            at * piece : (at + 1) * piece, q * N : (q + 1) * N
        ]


def split_pair(low, every, keep, send):
    for at in range(keep.shape[0]):
        keep[at] = every[2 * at + low]
        send[at] = every[2 * at + 1 - low]


def beside_kernel(
    heads, count, every,
    low, total, y, gate, gg, gain, gy, x, bc, scal, sin, cot, ow, series, rim, w, cw, slope, skip,
    out, keep, send, sg, bb, gb, edge, yb, wide, stage,
):
    length, width = y.shape
    depth = series.shape[1]
    cols = norm_columns(total[...], every)
    g = gate[...].astype(F32)
    sig = sigmoid(g)
    act = g * sig
    yv = y[...]
    gated = yv * act
    normed = (gated * cols[:, 0:1] * gain[...]).astype(BF16)
    out[...] = mm(normed, ow[...], NT).astype(BF16)
    grad_gated = cols[:, 0:1] * gg[...] - gated * cols[:, 1:2]
    grad_gate = (grad_gated * yv * (sig * (1.0 + g * (1.0 - sig)))).astype(BF16)
    rows = scal[...]
    cols = columns(rows)
    xv = x[...].astype(F32)
    gyv = gy[...]
    b, c = bc[:, 0:N], bc[:, N:]
    scores = mm(c, b, NT)
    back = jnp.zeros((length, width), F32)
    group = jnp.zeros((length, length), F32)
    for h in range(heads):
        decay = decay_of(cols, rows, h)
        gh = only_head(gyv, h, heads)
        back = back + mm(scores * decay, gh, TN)
        group = group + decay * mm(gh, xv, NT) * rows[heads + h : heads + h + 1, :]
    bb[...] = back
    gb[...] = mm(group, c, TN)
    grow = widen(columns(jnp.exp(rows[0:heads])), heads, width)
    grad_c = mm(group, b) + mm(gyv * grow, sin[...])
    yb[...] = mm_exact(head_mask(heads, width), gyv * (yv - per_lane(skip, heads, width) * xv), NT)
    clear_ends(wide, length)
    wide[RIM : RIM + length, :] = grad_c * slope[:, 2 * width - N :]
    grad_pre = conv_back(cw, wide, slice(0, N), length, 1, slice(width - N, width))
    edge[...] = grad_pre[0:RIM]
    sg[...] = mm(grad_gate, w[0], NT) + mm(grad_pre[RIM:], w[2, :, width - N :], NT)
    w_out = mm(cot[...], normed, TN).astype(BF16)
    w_gate = mm(series[...], grad_gate, TN).astype(BF16)
    w_c = (mm(series[...], grad_pre[RIM:], TN) + mm(rim[...], grad_pre[0:RIM], TN)).astype(BF16)
    piece = depth // count
    for at in range(count):
        stack_columns(stage, w_out, at, 0, piece)
        stack_columns(stage, w_gate, at, 2, piece)
        stack_columns(stage, w_c, at, 4, piece)
    split_pair(low[0], stage, keep, send)


def close_kernel(
    heads, count,
    low, x, bc, scal, gy, bb, gb, yb, sin, own, slope, series, rim, cw, skip, rate, partner, *rest,
):
    *others, keep, send, gp, edge, graw, wide, stage = rest
    length, width = gy.shape
    depth = series.shape[1]
    after = carried(low[0] == 0, partner[...], [o[...] for o in others], heads)
    rows = scal[...]
    running, step = rows[0:heads], rows[heads : 2 * heads]
    last = running[:, length - 1 : length]
    remain = jnp.exp(last - running)
    cols = columns(jnp.concatenate([remain, step, remain * step], axis=0))
    xv = x[...].astype(F32)
    back = bb[...] + widen(cols, heads, width) * mm(bc[:, 0:N], after, NT)
    grad_x = per_lane(skip, heads, width) * gy[...] + widen(cols[:, heads:], heads, width) * back
    grad_b = gb[...] + mm(xv * widen(cols[:, 2 * heads :], heads, width), after)
    clear_ends(wide, length)
    wide[RIM : RIM + length, 0:width] = grad_x * slope[:, 0:width]
    wide[RIM : RIM + length, width:] = grad_b * slope[:, width : width + N]
    grad_x = conv_back(cw, wide, slice(0, width), length, 0, slice(0, width))
    grad_b = conv_back(cw, wide, slice(width, width + N), length, 1, slice(0, N))
    edge[:, 0:width] = grad_x[0:RIM]
    edge[:, width:] = grad_b[0:RIM]
    gp[:, 0:width] = grad_x[RIM:]
    gp[:, width:] = grad_b[RIM:]
    w_x = (mm(series[...], grad_x[RIM:], TN) + mm(rim[...], grad_x[0:RIM], TN)).astype(BF16)
    w_b = (mm(series[...], grad_b[RIM:], TN) + mm(rim[...], grad_b[0:RIM], TN)).astype(BF16)
    mask = head_mask(heads, width)
    x_back = mm_exact(mask, xv * back, NT)[0:heads]
    final = jnp.exp(spread_rows(jnp.broadcast_to(last, (heads, N)), heads, width)) * sin[...]
    ends = jnp.sum(mm_exact(mask, after * (final + own[...])), axis=1, keepdims=True)[0:heads]
    grad_log = running_sum_back(yb[0:heads, :] - step * x_back) + ends
    grad_step = x_back - jnp.exp(per_row(rate, x_back.shape)) * grad_log
    grad_raw = grad_step * rows[2 * heads : 3 * heads]
    grad_raw = jnp.concatenate([grad_raw, jnp.zeros_like(grad_raw)], axis=0)
    graw[...] = grad_raw
    dt = mm(grad_raw, series[...])
    piece = depth // count
    blank = jnp.zeros((LOGS, N), F32)
    for at in range(count):
        stack_columns(stage, w_x, at, 0, piece)
        stack_columns(stage, w_b, at, 2, piece)
        dt_piece = jnp.concatenate(
            [dt[:, at * piece : (at + 1) * piece], blank[0 : 2 * heads, 0 : N - piece]], axis=1
        )
        dt_piece = jnp.concatenate([dt_piece, blank[0 : LOGS - 2 * heads]], axis=0)
        stage[at, 3 * piece :, :] = dt_piece.astype(BF16)
    split_pair(low[0], stage, keep, send)


def halve_kernel(high, keep, other, own, *parts):
    at = high[0]
    own[...] = keep[at].astype(F32) + other[at].astype(F32)
    for k, part in enumerate(parts):
        at = high[0] ^ (k + 1)
        part[...] = (keep[at].astype(F32) + other[at].astype(F32)).astype(BF16)


def rows_kernel(spot, out, sg, gp, graw, edge, edge_c, w, dtw, *rest):
    *parts, stage = rest
    length, depth = sg.shape
    width = w.shape[2]
    heads = dtw.shape[0]
    total = sg[...] + mm(graw[0:heads, :], dtw[...], TN)
    total = total + mm(gp[:, 0:width], w[1], NT) + mm(gp[:, width:], w[2, :, 0:N], NT)
    late = mm(edge[:, 0:width], w[1], NT) + mm(edge[:, width:], w[2, :, 0:N], NT)
    late = late + mm(edge_c[...], w[2, :, N:], NT)
    stage[:, 0:depth] = out[...]
    stage[:, depth:] = total.astype(BF16)
    stage[length - RIM :, depth:] = (total[length - RIM :, :] + late).astype(BF16)
    piece = length // len(parts)
    for k, part in enumerate(parts):
        start = pl.multiple_of((spot[0] ^ k) * piece, piece)
        part[...] = stage[pl.ds(start, piece), :]


def outputs_kernel(*refs):
    *parts, layer, grad = refs
    depth = layer.shape[1]
    total = parts[0][...].astype(F32)
    for part in parts[1:]:
        total = total + part[...].astype(F32)
    layer[...] = total[:, 0:depth].astype(BF16)
    grad[...] = total[:, depth:]


def total_kernel(hops, *refs):
    early, late = refs[0:hops], refs[hops : 2 * hops]
    w_in, w_dt, w_out = refs[2 * hops :]
    piece = w_out.shape[0]

    def sum_of(parts):
        total = parts[0][...]
        for part in parts[1:]:
            total = total + part[...].astype(F32)
        return total

    def laid(total, base):
        return total[base * piece : (base + 1) * piece, :]

    early, late = sum_of(early), sum_of(late)
    for q in range(2):
        cut = slice(q * N, (q + 1) * N)
        w_out[:, cut] = laid(early, q)
        w_in[0, :, cut] = laid(early, 2 + q)
        w_in[1, :, cut] = laid(late, q)
    w_in[2, :, 0:N] = laid(late, 2)
    w_in[2, :, N:] = laid(early, 4)
    w_dt[...] = late[3 * piece : 3 * piece + w_dt.shape[0], 0:piece]


VMEM = pl.BlockSpec(memory_space=pltpu.VMEM)
SMEM = pl.BlockSpec(memory_space=pltpu.SMEM)


def run(kernel, name, outs, args, scalars=(), scratch=(), flops=10**8):
    moved = sum(a.size * a.dtype.itemsize for a in args)
    return pl.pallas_call(
        kernel,
        name=name,
        out_shape=[jax.ShapeDtypeStruct(shape, kind) for shape, kind in outs],
        in_specs=[SMEM if i in scalars else VMEM for i in range(len(args))],
        out_specs=[VMEM] * len(outs),
        scratch_shapes=list(scratch),
        compiler_params=pltpu.CompilerParams(vmem_limit_bytes=16 * 2**20),
        cost_estimate=pl.CostEstimate(flops=flops, bytes_accessed=2 * moved, transcendentals=0),
    )(*args)


def shifted(block, axis, distance):
    devices = range(lax.axis_size(axis))
    route = [(i - distance, i) for i in devices if i - distance in devices]
    return lax.ppermute(block, axis, route)


def swapped(block, axis, flip):
    return lax.ppermute(block, axis, [(i, i ^ flip) for i in range(lax.axis_size(axis))])


def body(
    series,
    in_weight,
    step_weight,
    step_bias,
    log_rate,
    conv_weight,
    conv_bias,
    skip_gain,
    norm_gain,
    out_weight,
    cotangent,
):
    length, depth = series.shape
    width = in_weight.shape[2]
    heads = step_weight.shape[1]
    count = lax.axis_size("tm")
    parts = lax.axis_size("head")
    every = width * parts
    assert width == 2 * N and heads == 4
    part = functools.partial
    w = in_weight.transpose(1, 0, 2)
    dtw = step_weight.T
    gain = norm_gain.reshape(1, width)
    hops = count // 2
    piece = depth // count
    position = lax.axis_index("tm").astype(jnp.int32)
    low, high = (position % 2).reshape(1), (position // 2).reshape(1)
    spot = lax.axis_index("head").astype(jnp.int32).reshape(1)
    rim = shifted(series[length - RIM :], "tm", 1)
    state_msg = ((width + LOGS, N), BF16)

    def passed(msg, back):
        partner = swapped(msg, "tm", 1)
        (both,) = run(part(pair_kernel, heads, back), "pair", [state_msg], [low, msg, partner], (0,))
        sign = -1 if back else 1
        return [partner] + [shifted(both, "tm", sign * 2 * d) for d in range(hops - 1, 0, -1)]

    def summed(keep, send, name):
        rows = keep.shape[1]
        own, *parts = run(
            halve_kernel, name, [((rows, N), F32)] + [((rows, N), BF16)] * (hops - 1),
            [high, keep, swapped(send, "tm", 1)], (0,),
        )
        return [own] + [swapped(block, "tm", 2 * (k + 1)) for k, block in enumerate(parts)]

    gate, pre, scal = run(
        part(project_kernel, heads), "project",
        [((length, width), BF16), ((length, 2 * width), BF16), ((4 * heads, length), F32)],
        [series, w, dtw, step_bias, log_rate], (3, 4),
    )
    x, bc, conv, own, msg = run(
        part(conv_kernel, heads), "conv",
        [
            ((length, width), BF16),
            ((length, width), BF16),
            ((length, 2 * width), F32),
            ((width, N), F32),
            state_msg,
        ],
        [pre, rim, w, conv_weight, conv_bias, scal],
        scratch=[pltpu.VMEM((length + 8, 2 * width), F32)],
    )
    ahead = passed(msg, False)
    inside, gg, slope = run(
        part(inside_kernel, heads), "inside",
        [((length, width), F32), ((length, width), F32), ((length, 2 * width), F32)],
        [x, bc, scal, skip_gain, cotangent, out_weight, gain, conv], (3,),
    )
    y, sin, sums = run(
        part(join_kernel, heads), "join",
        [((length, width), F32), ((width, N), F32), ((8, length), F32)],
        [low, inside, gg, gate, bc, scal] + ahead, (0,),
    )
    total = lax.psum(sums, "head")
    gy, msg = run(
        part(grad_y_kernel, heads, every), "grad_y",
        [((length, width), F32), state_msg],
        [total, y, gate, gg, bc, scal],
    )
    behind = passed(msg, True)
    early, late = 5 * piece, 3 * piece + LOGS
    out, keep, send, sg, bb, gb, edge_c, yb = run(
        part(beside_kernel, heads, count, every), "beside",
        [
            ((length, depth), BF16),
            ((hops, early, N), BF16),
            ((hops, early, N), BF16),
            ((length, depth), F32),
            ((length, width), F32),
            ((length, N), F32),
            ((RIM, N), BF16),
            ((8, length), F32),
        ],
        [
            low, total, y, gate, gg, gain, gy, x, bc, scal, sin, cotangent, out_weight, series,
            rim, w, conv_weight, slope, skip_gain,
        ],
        (0, 18),
        scratch=[
            pltpu.VMEM((length + RIM + 8, N), F32),
            pltpu.VMEM((count, early, N), BF16),
        ],
    )
    early_parts = summed(keep, send, "halve_early")
    keep, send, gp, edge, graw = run(
        part(close_kernel, heads, count), "close",
        [
            ((hops, late, N), BF16),
            ((hops, late, N), BF16),
            ((length, width + N), BF16),
            ((RIM, width + N), BF16),
            ((2 * heads, length), F32),
        ],
        [
            low, x, bc, scal, gy, bb, gb, yb, sin, own, slope, series, rim, conv_weight,
            skip_gain, log_rate,
        ]
        + behind,
        (0, 14, 15),
        scratch=[
            pltpu.VMEM((length + RIM + 8, width + N), F32),
            pltpu.VMEM((count, late, N), BF16),
        ],
    )
    late_parts = summed(keep, send, "halve_late")
    edge, edge_c = shifted(edge, "tm", -1), shifted(edge_c, "tm", -1)
    both = run(
        rows_kernel, "rows",
        [((length // parts, 2 * depth), BF16)] * parts,
        [spot, out, sg, gp, graw, edge, edge_c, w, dtw], (0,),
        scratch=[pltpu.VMEM((length, 2 * depth), BF16)],
    )
    both = [both[0]] + [swapped(both[k], "head", k) for k in range(1, parts)]
    layer_out, series_grad = run(
        outputs_kernel, "outputs",
        [((length // parts, depth), BF16), ((length // parts, depth), F32)], both,
    )
    w_in_grad, w_dt_grad, w_out_grad = run(
        part(total_kernel, hops), "total",
        [((3, piece, width), F32), ((heads, piece), F32), ((piece, width), F32)],
        early_parts + late_parts,
    )
    return (layer_out, series_grad, w_in_grad.transpose(1, 0, 2), w_dt_grad.T, w_out_grad)


def solution(mesh):
    in_specs = (
        P("tm", None),
        P(None, None, "head"),
        P(None, "head"),
        P("head"),
        P("head"),
        P(None, None, "head"),
        P(None, "head"),
        P("head"),
        P("head"),
        P(None, "head"),
        P("tm", None),
    )
    out_specs = (
        P(("tm", "head"), None),
        P(("tm", "head"), None),
        P("tm", None, "head"),
        P("tm", "head"),
        P("tm", "head"),
    )
    return jax.shard_map(body, mesh=mesh, in_specs=in_specs, out_specs=out_specs, check_vma=False)
```

time: 134 us -> 87.2 us (0.65)
  blocking collectives: 42 us -> 5.77 us
  starting transfers between devices: 24.7 us -> 38.2 us
  waiting for transfers between devices: 31.5 us -> 20 us
  local copies, waits for them, and re-layouts: 18.6 us -> 7.25 us
  other arithmetic: 2.06 us -> 0 us
  Pallas kernels: 12.9 us -> 14.4 us
    all_to_all x3 -> x0, blocking collectives: 36.2 us -> none  [exchange(): return lax.all_to_all(blocks, axis, 0, 0)]
    all_to_all x4 -> x0, waiting for transfers between devices: 27.2 us -> none  [exchange(): return lax.all_to_all(blocks, axis, 0, 0)]
    all_to_all x4 -> x0, starting transfers between devices: 18.5 us -> none  [exchange(): return lax.all_to_all(blocks, axis, 0, 0)]
    ppermute x0 -> x13, starting transfers between devices: none -> 17.6 us  [swapped(): lax.ppermute(block, axis, [(i, i ^ flip) for i in range(lax.axis_size(axi...]
    ppermute x2 -> x9, starting transfers between devices: 6.14 us -> 20.6 us  [shifted(): return lax.ppermute(block, axis, route)]
    unnamed x68 -> x42, local copies, waits for them, and re-layouts: 16.7 us -> 6.52 us
    ppermute x0 -> x13, waiting for transfers between devices: none -> 8.31 us  [swapped(): lax.ppermute(block, axis, [(i, i ^ flip) for i in range(lax.axis_size(axi...]
    ppermute x2 -> x9, waiting for transfers between devices: 4.36 us -> 11.7 us  [shifted(): return lax.ppermute(block, axis, route)]
  transfers between devices with their start and end apart: 6 -> 22, of which waited for: 4 -> 5; matrix products, arithmetic and copies ran while one was open for 3% -> 0% of each run, Pallas kernels for 5% -> 13%
where the time goes in v3:
time: 87.2 us; the launch traced here: 86.6 us
  starting transfers between devices  38.2 us (44%)
  waiting for transfers between devices  20 us (23%)
  Pallas kernels  14.4 us (17%)
  local copies, waits for them, and re-layouts  7.25 us (8%)
  blocking collectives  5.77 us (7%)
  between operations  0.98 us (1%)
    ppermute x9, starting transfers between devices, shifted(): return lax.ppermute(block, axis, route)  20.6 us
    ppermute x13, starting transfers between devices, swapped(): lax.ppermute(block, axis, [(i, i ^ flip) for i in range(lax.axis_size(axi...  17.6 us
    pallas_call x14, Pallas kernels, run(): pl.pallas_call(kernel, name=name, out_shape=[jax.ShapeDtypeStruct(shape,...  14.4 us
    ppermute x9, waiting for transfers between devices, shifted(): return lax.ppermute(block, axis, route)  11.7 us
    ppermute x13, waiting for transfers between devices, swapped(): lax.ppermute(block, axis, [(i, i ^ flip) for i in range(lax.axis_size(axi...  8.31 us
    unnamed x42, local copies, waits for them, and re-layouts  6.52 us
    psum x1, blocking collectives, body(): total = lax.psum(sums, 'head')  5.77 us
  transfers between devices with their start and end apart: 22, of which 5 were waited for; matrix products, arithmetic and copies ran while one was open for 0% of the time, Pallas kernels for 13%

profile of v3, /device:TPU:0, one launch (start us, length us, event | category | flops | bytes accessed | tf_op | source)
XLA Modules:
  0.0 86.6 jit_solution(16734900605396657969)
XLA Ops:
  1.4 4.9 %collective-permute-start = (bf16[16,512]{1,0:T(8,128)(2,1)S(1)}, bf16[16,512]{1,0:T(8,128)(2,1)S(1)}, u32[]{:S(2)}, u32[]{:S(2)}) collective-permute-start(bf16[16,512]{1,0:T(8,128)(2,1)S(1)} %slice.3), channel_id=1, source_target_pairs={{0,4},{4,8},{8,12},{12,16},{16,20},{20,24},{24,28},{1,5},{5,9},{9,... | collective-permute-start | bytes 49160 | tf_op jit(solution)/shard_map/ppermute | solution.py:463
  9.0 1.5 %project.1 = (bf16[256,256]{1,0:T(8,128)(2,1)S(1)}, bf16[256,512]{1,0:T(8,128)(2,1)S(1)}, f32[16,256]{1,0:T(8,128)S(1)}) custom-call(bf16[256,512]{1,0:T(8,128)(2,1)S(1)} %copy-done.2, bf16[3,512,256]{2,1,0:T(8,128)(2,1)S(1)} %bitcast.8, bf16[4,512]{1,0:T(4,128)(2,1)S(1)} %bitcast.12, f32[4]{0:T(128)S(1)} %copy-done.20, f32[4]{0:T(128)S(1)} %copy-done.18), custom_call_target="tpu_custom_call" | custom-call | flops 100000000 | bytes 2105408 | tf_op jit(solution)/shard_map/project/pallas_call | solution.py:448
  12.1 1.6 %collective-permute-start.1 = (bf16[272,128]{1,0:T(8,128)(2,1)S(1)}, bf16[272,128]{1,0:T(8,128)(2,1)S(1)}, u32[]{:S(2)}, u32[]{:S(2)}) collective-permute-start(bf16[272,128]{1,0:T(8,128)(2,1)S(1)} %get-tuple-element.59.mine), channel_id=1, source_target_pairs={{0,4},{4,0},{8,12},{12,8},{16,20},{20,16},{24,28},{28,24},{1,5},{5... | collective-permute-start | bytes 208904 | tf_op jit(solution)/shard_map/ppermute | solution.py:467
  13.7 2.8 %collective-permute-done.1.other.partner = bf16[272,128]{1,0:T(8,128)(2,1)S(1)} collective-permute-done((bf16[272,128]{1,0:T(8,128)(2,1)S(1)}, bf16[272,128]{1,0:T(8,128)(2,1)S(1)}, u32[]{:S(2)}, u32[]{:S(2)}) %collective-permute-start.1) | collective-permute-done | bytes 69664 | tf_op jit(solution)/shard_map/ppermute | solution.py:467
  16.6 5.5 %collective-permute-start.2 = (bf16[272,128]{1,0:T(8,128)(2,1)S(1)}, bf16[272,128]{1,0:T(8,128)(2,1)S(1)}, u32[]{:S(2)}, u32[]{:S(2)}) collective-permute-start(bf16[272,128]{1,0:T(8,128)(2,1)S(1)} %pair.2), channel_id=1, source_target_pairs={{0,24},{4,28},{1,25},{5,29},{2,26},{6,30},{3,27},{7,31}} | collective-permute-start | bytes 208904 | tf_op jit(solution)/shard_map/ppermute | solution.py:463
  22.1 1.3 %collective-permute-start.3 = (bf16[272,128]{1,0:T(8,128)(2,1)S(1)}, bf16[272,128]{1,0:T(8,128)(2,1)S(1)}, u32[]{:S(2)}, u32[]{:S(2)}) collective-permute-start(bf16[272,128]{1,0:T(8,128)(2,1)S(1)} %pair.2), channel_id=1, source_target_pairs={{0,16},{4,20},{8,24},{12,28},{1,17},{5,21},{9,25},{13,29},{2,18},{... | collective-permute-start | bytes 208904 | tf_op jit(solution)/shard_map/ppermute | solution.py:463
  23.4 2.5 %collective-permute-start.4 = (bf16[272,128]{1,0:T(8,128)(2,1)S(1)}, bf16[272,128]{1,0:T(8,128)(2,1)S(1)}, u32[]{:S(2)}, u32[]{:S(2)}) collective-permute-start(bf16[272,128]{1,0:T(8,128)(2,1)S(1)} %pair.2), channel_id=1, source_target_pairs={{0,8},{4,12},{8,16},{12,20},{16,24},{20,28},{1,9},{5,13},{9,17},{1... | collective-permute-start | bytes 208904 | tf_op jit(solution)/shard_map/ppermute | solution.py:463
  26.6 1.4 %inside.1 = (f32[256,256]{1,0:T(8,128)S(1)}, f32[256,256]{1,0:T(8,128)S(1)}, f32[256,512]{1,0:T(8,128)S(1)}) custom-call(bf16[256,256]{1,0:T(8,128)(2,1)S(1)} %get-tuple-element.53.x, bf16[256,256]{1,0:T(8,128)(2,1)S(1)} %get-tuple-element.54.bc, f32[16,256]{1,0:T(8,128)S(1)} %get-tuple-element.52.scal, f32[4]{0:T(128)S(1)} %copy-done.16, ...), custom_call_target="tpu_custom_call" | custom-call | flops 100000000 | bytes 2656288 | tf_op jit(solution)/shard_map/inside/pallas_call | solution.py:448
  28.8 5.8 %psum.7.total = f32[8,256]{1,0:T(8,128)S(1)} all-reduce(f32[8,256]{1,0:T(8,128)S(1)} %get-tuple-element.60), channel_id=1, replica_groups=mesh['tm'=8,'head'=4] {'head'}, use_global_device_ids=true, to_apply=%region_0.1 | all-reduce | flops 2048 | bytes 16384 | tf_op jit(solution)/shard_map/psum | solution.py:544
  35.5 3.6 %beside.1 = (bf16[256,512]{1,0:T(8,128)(2,1)S(1)}, bf16[4,320,128]{2,1,0:T(8,128)(2,1)S(1)}, bf16[4,320,128]{2,1,0:T(8,128)(2,1)}, f32[256,512]{1,0:T(8,128)S(1)...) custom-call(s32[1]{0:T(128)} %bitcast.1.low, ...), custom_call_target="tpu_custom_call" | custom-call | flops 100000000 | bytes 6916136 | tf_op jit(solution)/shard_map/beside/pallas_call | solution.py:448
  39.9 1.9 %collective-permute-start.14 = (bf16[4,320,128]{2,1,0:T(8,128)(2,1)}, bf16[4,320,128]{2,1,0:T(8,128)(2,1)S(1)}, u32[]{:S(2)}, u32[]{:S(2)}) collective-permute-start(bf16[4,320,128]{2,1,0:T(8,128)(2,1)} %get-tuple-element.83), channel_id=1, source_target_pairs={{0,4},{4,0},{8,12},{12,8},{16,20},{20,16},{24,28},{28,24},{1,5},{5... | collective-permute-start | bytes 983048 | tf_op jit(solution)/shard_map/ppermute | solution.py:467
  41.8 1.3 %collective-permute-start.6 = (bf16[272,128]{1,0:T(8,128)(2,1)S(1)}, bf16[272,128]{1,0:T(8,128)(2,1)S(1)}, u32[]{:S(2)}, u32[]{:S(2)}) collective-permute-start(bf16[272,128]{1,0:T(8,128)(2,1)S(1)} %pair.3), channel_id=1, source_target_pairs={{24,0},{28,4},{25,1},{29,5},{26,2},{30,6},{27,3},{31,7}} | collective-permute-start | bytes 208904 | tf_op jit(solution)/shard_map/ppermute | solution.py:463
  43.1 1.3 %collective-permute-start.7 = (bf16[272,128]{1,0:T(8,128)(2,1)S(1)}, bf16[272,128]{1,0:T(8,128)(2,1)S(1)}, u32[]{:S(2)}, u32[]{:S(2)}) collective-permute-start(bf16[272,128]{1,0:T(8,128)(2,1)S(1)} %pair.3), channel_id=1, source_target_pairs={{16,0},{20,4},{24,8},{28,12},{17,1},{21,5},{25,9},{29,13},{18,2},{... | collective-permute-start | bytes 208904 | tf_op jit(solution)/shard_map/ppermute | solution.py:463
  45.7 4.7 %collective-permute-done.6.rest_0_ = bf16[272,128]{1,0:T(8,128)(2,1)S(1)} collective-permute-done((bf16[272,128]{1,0:T(8,128)(2,1)S(1)}, bf16[272,128]{1,0:T(8,128)(2,1)S(1)}, u32[]{:S(2)}, u32[]{:S(2)}) %collective-permute-start.6) | collective-permute-done | bytes 69664 | tf_op jit(solution)/shard_map/ppermute | solution.py:463
  50.4 2.2 %collective-permute-done.7.rest_1_ = bf16[272,128]{1,0:T(8,128)(2,1)S(1)} collective-permute-done((bf16[272,128]{1,0:T(8,128)(2,1)S(1)}, bf16[272,128]{1,0:T(8,128)(2,1)S(1)}, u32[]{:S(2)}, u32[]{:S(2)}) %collective-permute-start.7) | collective-permute-done | bytes 69664 | tf_op jit(solution)/shard_map/ppermute | solution.py:463
  52.6 3.3 %close.1 = (bf16[4,208,128]{2,1,0:T(8,128)(2,1)S(1)}, bf16[4,208,128]{2,1,0:T(8,128)(2,1)}, bf16[256,384]{1,0:T(8,128)(2,1)S(1)}, bf16[16,384]{1,0:T(8,128)(2,1)S(1)}, f32[8,256]{1,0:T(8,128)S(1)}) custom-call(s32[1]{0:T(128)} %bitcast.1.low, bf16[256,256]{1,0:T(8,128)(2,1)S(1)} %get-tuple-element.53.x, bf16[256,256]{1,0:T(8,128)(2,1)S(1)} %get-tuple-element.54.bc, ...), custom_call_target="tpu_custom_call" | custom-call | flops 100000000 | bytes 4587592 | tf_op jit(solution)/shard_map/close/pallas_call | solution.py:448
  59.6 4.8 %collective-permute-done.10.edge_c = bf16[16,128]{1,0:T(8,128)(2,1)S(1)} collective-permute-done((bf16[16,128]{1,0:T(8,128)(2,1)S(1)}, bf16[16,128]{1,0:T(8,128)(2,1)S(1)}, u32[]{:S(2)}, u32[]{:S(2)}) %collective-permute-start.10) | collective-permute-done | bytes 4128 | tf_op jit(solution)/shard_map/ppermute | solution.py:463
  66.0 1.6 %collective-permute-start.12 = (bf16[64,1024]{1,0:T(8,128)(2,1)S(1)}, bf16[64,1024]{1,0:T(8,128)(2,1)S(1)}, u32[]{:S(2)}, u32[]{:S(2)}) collective-permute-start(bf16[64,1024]{1,0:T(8,128)(2,1)S(1)} %get-tuple-element.78), channel_id=1, source_target_pairs={{0,2},{1,3},{2,0},{3,1},{4,6},{5,7},{6,4},{7,5},{8,10},{9,11},{10,... | collective-permute-start | bytes 393224 | tf_op jit(solution)/shard_map/ppermute | solution.py:467
  67.9 3.1 %collective-permute-start.19 = (bf16[208,128]{1,0:T(8,128)(2,1)S(1)}, bf16[208,128]{1,0:T(8,128)(2,1)S(1)}, u32[]{:S(2)}, u32[]{:S(2)}) collective-permute-start(bf16[208,128]{1,0:T(8,128)(2,1)S(1)} %get-tuple-element.91), channel_id=1, source_target_pairs={{0,8},{4,12},{8,0},{12,4},{16,24},{20,28},{24,16},{28,20},{1,9},{5... | collective-permute-start | bytes 159752 | tf_op jit(solution)/shard_map/ppermute | solution.py:467
  71.2 2.7 %collective-permute-start.16 = (bf16[320,128]{1,0:T(8,128)(2,1)S(1)}, bf16[320,128]{1,0:T(8,128)(2,1)S(1)}, u32[]{:S(2)}, u32[]{:S(2)}) collective-permute-start(bf16[320,128]{1,0:T(8,128)(2,1)S(1)} %get-tuple-element.86), channel_id=1, source_target_pairs={{0,16},{4,20},{8,24},{12,28},{16,0},{20,4},{24,8},{28,12},{1,17},{... | collective-permute-start | bytes 245768 | tf_op jit(solution)/shard_map/ppermute | solution.py:467
  73.9 2.4 %collective-permute-start.17 = (bf16[320,128]{1,0:T(8,128)(2,1)S(1)}, bf16[320,128]{1,0:T(8,128)(2,1)S(1)}, u32[]{:S(2)}, u32[]{:S(2)}) collective-permute-start(bf16[320,128]{1,0:T(8,128)(2,1)S(1)} %get-tuple-element.87), channel_id=1, source_target_pairs={{0,24},{4,28},{8,16},{12,20},{16,8},{20,12},{24,0},{28,4},{1,25},{... | collective-permute-start | bytes 245768 | tf_op jit(solution)/shard_map/ppermute | solution.py:467
  76.4 1.7 %collective-permute-start.20 = (bf16[208,128]{1,0:T(8,128)(2,1)S(1)}, bf16[208,128]{1,0:T(8,128)(2,1)S(1)}, u32[]{:S(2)}, u32[]{:S(2)}) collective-permute-start(bf16[208,128]{1,0:T(8,128)(2,1)S(1)} %get-tuple-element.92), channel_id=1, source_target_pairs={{0,16},{4,20},{8,24},{12,28},{16,0},{20,4},{24,8},{28,12},{1,17},{... | collective-permute-start | bytes 159752 | tf_op jit(solution)/shard_map/ppermute | solution.py:467
  78.0 1.6 %collective-permute-start.21 = (bf16[208,128]{1,0:T(8,128)(2,1)S(1)}, bf16[208,128]{1,0:T(8,128)(2,1)S(1)}, u32[]{:S(2)}, u32[]{:S(2)}) collective-permute-start(bf16[208,128]{1,0:T(8,128)(2,1)S(1)} %get-tuple-element.93), channel_id=1, source_target_pairs={{0,24},{4,28},{8,16},{12,20},{16,8},{20,12},{24,0},{28,4},{1,25},{... | collective-permute-start | bytes 159752 | tf_op jit(solution)/shard_map/ppermute | solution.py:467
  80.4 5.5 %collective-permute-done.20.refs_6_ = bf16[208,128]{1,0:T(8,128)(2,1)S(1)} collective-permute-done((bf16[208,128]{1,0:T(8,128)(2,1)S(1)}, bf16[208,128]{1,0:T(8,128)(2,1)S(1)}, u32[]{:S(2)}, u32[]{:S(2)}) %collective-permute-start.20) | collective-permute-done | bytes 53280 | tf_op jit(solution)/shard_map/ppermute | solution.py:467
  (78 shorter events, 16.8 us)
Async XLA Ops:
  1.4 9.1 %collective-permute-start = (bf16[16,512]{1,0:T(8,128)(2,1)S(1)}, bf16[16,512]{1,0:T(8,128)(2,1)S(1)}, u32[]{:S(2)}, u32[]{:S(2)}) collective-permute-start(bf16[16,512]{1,0:T(8,128)(2,1)S(1)} %slice.3), channel_id=1, source_target_pairs={{0,4},{4,8},{8,12},{12,16},{16,20},{20,24},{24,28},{1,5},{5,9},{9,... | collective-permute-start | bytes 49160 | tf_op jit(solution)/shard_map/ppermute | solution.py:463
  11.2 14.7 %copy-start.5 = (bf16[512,256]{1,0:T(8,128)(2,1)S(1)}, bf16[512,256]{1,0:T(8,128)(2,1)}, u32[]{:S(2)}) copy-start(bf16[512,256]{1,0:T(8,128)(2,1)} %ow.3) | copy-start | bytes 786436
  12.1 4.4 %collective-permute-start.1 = (bf16[272,128]{1,0:T(8,128)(2,1)S(1)}, bf16[272,128]{1,0:T(8,128)(2,1)S(1)}, u32[]{:S(2)}, u32[]{:S(2)}) collective-permute-start(bf16[272,128]{1,0:T(8,128)(2,1)S(1)} %get-tuple-element.59.mine), channel_id=1, source_target_pairs={{0,4},{4,0},{8,12},{12,8},{16,20},{20,16},{24,28},{28,24},{1,5},{5... | collective-permute-start | bytes 208904 | tf_op jit(solution)/shard_map/ppermute | solution.py:467
  16.6 11.4 %collective-permute-start.2 = (bf16[272,128]{1,0:T(8,128)(2,1)S(1)}, bf16[272,128]{1,0:T(8,128)(2,1)S(1)}, u32[]{:S(2)}, u32[]{:S(2)}) collective-permute-start(bf16[272,128]{1,0:T(8,128)(2,1)S(1)} %pair.2), channel_id=1, source_target_pairs={{0,24},{4,28},{1,25},{5,29},{2,26},{6,30},{3,27},{7,31}} | collective-permute-start | bytes 208904 | tf_op jit(solution)/shard_map/ppermute | solution.py:463
  22.1 5.9 %collective-permute-start.3 = (bf16[272,128]{1,0:T(8,128)(2,1)S(1)}, bf16[272,128]{1,0:T(8,128)(2,1)S(1)}, u32[]{:S(2)}, u32[]{:S(2)}) collective-permute-start(bf16[272,128]{1,0:T(8,128)(2,1)S(1)} %pair.2), channel_id=1, source_target_pairs={{0,16},{4,20},{8,24},{12,28},{1,17},{5,21},{9,25},{13,29},{2,18},{... | collective-permute-start | bytes 208904 | tf_op jit(solution)/shard_map/ppermute | solution.py:463
  23.4 4.6 %collective-permute-start.4 = (bf16[272,128]{1,0:T(8,128)(2,1)S(1)}, bf16[272,128]{1,0:T(8,128)(2,1)S(1)}, u32[]{:S(2)}, u32[]{:S(2)}) collective-permute-start(bf16[272,128]{1,0:T(8,128)(2,1)S(1)} %pair.2), channel_id=1, source_target_pairs={{0,8},{4,12},{8,16},{12,20},{16,24},{20,28},{1,9},{5,13},{9,17},{1... | collective-permute-start | bytes 208904 | tf_op jit(solution)/shard_map/ppermute | solution.py:463
  35.3 6.4 %collective-permute-start.5 = (bf16[272,128]{1,0:T(8,128)(2,1)S(1)}, bf16[272,128]{1,0:T(8,128)(2,1)S(1)}, u32[]{:S(2)}, u32[]{:S(2)}) collective-permute-start(bf16[272,128]{1,0:T(8,128)(2,1)S(1)} %get-tuple-element.71.mine), channel_id=1, source_target_pairs={{0,4},{4,0},{8,12},{12,8},{16,20},{20,16},{24,28},{28,24},{1,5},{5... | collective-permute-start | bytes 208904 | tf_op jit(solution)/shard_map/ppermute | solution.py:467
  39.8 16.0 %copy-start.6 = (bf16[4,320,128]{2,1,0:T(8,128)(2,1)}, bf16[4,320,128]{2,1,0:T(8,128)(2,1)S(1)}, u32[]{:S(2)}) copy-start(bf16[4,320,128]{2,1,0:T(8,128)(2,1)S(1)} %get-tuple-element.82.keep) | copy-start | bytes 983044
  39.9 31.1 %collective-permute-start.14 = (bf16[4,320,128]{2,1,0:T(8,128)(2,1)}, bf16[4,320,128]{2,1,0:T(8,128)(2,1)S(1)}, u32[]{:S(2)}, u32[]{:S(2)}) collective-permute-start(bf16[4,320,128]{2,1,0:T(8,128)(2,1)} %get-tuple-element.83), channel_id=1, source_target_pairs={{0,4},{4,0},{8,12},{12,8},{16,20},{20,16},{24,28},{28,24},{1,5},{5... | collective-permute-start | bytes 983048 | tf_op jit(solution)/shard_map/ppermute | solution.py:467
  41.8 8.6 %collective-permute-start.6 = (bf16[272,128]{1,0:T(8,128)(2,1)S(1)}, bf16[272,128]{1,0:T(8,128)(2,1)S(1)}, u32[]{:S(2)}, u32[]{:S(2)}) collective-permute-start(bf16[272,128]{1,0:T(8,128)(2,1)S(1)} %pair.3), channel_id=1, source_target_pairs={{24,0},{28,4},{25,1},{29,5},{26,2},{30,6},{27,3},{31,7}} | collective-permute-start | bytes 208904 | tf_op jit(solution)/shard_map/ppermute | solution.py:463
  43.1 9.5 %collective-permute-start.7 = (bf16[272,128]{1,0:T(8,128)(2,1)S(1)}, bf16[272,128]{1,0:T(8,128)(2,1)S(1)}, u32[]{:S(2)}, u32[]{:S(2)}) collective-permute-start(bf16[272,128]{1,0:T(8,128)(2,1)S(1)} %pair.3), channel_id=1, source_target_pairs={{16,0},{20,4},{24,8},{28,12},{17,1},{21,5},{25,9},{29,13},{18,2},{... | collective-permute-start | bytes 208904 | tf_op jit(solution)/shard_map/ppermute | solution.py:463
  44.4 8.2 %collective-permute-start.8 = (bf16[272,128]{1,0:T(8,128)(2,1)S(1)}, bf16[272,128]{1,0:T(8,128)(2,1)S(1)}, u32[]{:S(2)}, u32[]{:S(2)}) collective-permute-start(bf16[272,128]{1,0:T(8,128)(2,1)S(1)} %pair.3), channel_id=1, source_target_pairs={{8,0},{12,4},{16,8},{20,12},{24,16},{28,20},{9,1},{13,5},{17,9},{2... | collective-permute-start | bytes 208904 | tf_op jit(solution)/shard_map/ppermute | solution.py:463
  56.6 11.3 %collective-permute-start.18 = (bf16[4,208,128]{2,1,0:T(8,128)(2,1)}, bf16[4,208,128]{2,1,0:T(8,128)(2,1)S(1)}, u32[]{:S(2)}, u32[]{:S(2)}) collective-permute-start(bf16[4,208,128]{2,1,0:T(8,128)(2,1)} %get-tuple-element.89), channel_id=1, source_target_pairs={{0,4},{4,0},{8,12},{12,8},{16,20},{20,16},{24,28},{28,24},{1,5},{5... | collective-permute-start | bytes 638984 | tf_op jit(solution)/shard_map/ppermute | solution.py:467
  57.0 7.4 %collective-permute-start.9 = (bf16[16,384]{1,0:T(8,128)(2,1)S(1)}, bf16[16,384]{1,0:T(8,128)(2,1)S(1)}, u32[]{:S(2)}, u32[]{:S(2)}) collective-permute-start(bf16[16,384]{1,0:T(8,128)(2,1)S(1)} %get-tuple-element.74), channel_id=1, source_target_pairs={{4,0},{8,4},{12,8},{16,12},{20,16},{24,20},{28,24},{5,1},{9,5},{13... | collective-permute-start | bytes 36872 | tf_op jit(solution)/shard_map/ppermute | solution.py:463
  58.3 6.1 %collective-permute-start.10 = (bf16[16,128]{1,0:T(8,128)(2,1)S(1)}, bf16[16,128]{1,0:T(8,128)(2,1)S(1)}, u32[]{:S(2)}, u32[]{:S(2)}) collective-permute-start(bf16[16,128]{1,0:T(8,128)(2,1)S(1)} %get-tuple-element.75), channel_id=1, source_target_pairs={{4,0},{8,4},{12,8},{16,12},{20,16},{24,20},{28,24},{5,1},{9,5},{13... | collective-permute-start | bytes 12296 | tf_op jit(solution)/shard_map/ppermute | solution.py:463
  65.9 5.3 %collective-permute-start.11 = (bf16[64,1024]{1,0:T(8,128)(2,1)S(1)}, bf16[64,1024]{1,0:T(8,128)(2,1)S(1)}, u32[]{:S(2)}, u32[]{:S(2)}) collective-permute-start(bf16[64,1024]{1,0:T(8,128)(2,1)S(1)} %get-tuple-element.77), channel_id=1, source_target_pairs={{0,1},{1,0},{2,3},{3,2},{4,5},{5,4},{6,7},{7,6},{8,9},{9,8},{10,11... | collective-permute-start | bytes 393224 | tf_op jit(solution)/shard_map/ppermute | solution.py:467
  66.0 8.0 %collective-permute-start.12 = (bf16[64,1024]{1,0:T(8,128)(2,1)S(1)}, bf16[64,1024]{1,0:T(8,128)(2,1)S(1)}, u32[]{:S(2)}, u32[]{:S(2)}) collective-permute-start(bf16[64,1024]{1,0:T(8,128)(2,1)S(1)} %get-tuple-element.78), channel_id=1, source_target_pairs={{0,2},{1,3},{2,0},{3,1},{4,6},{5,7},{6,4},{7,5},{8,10},{9,11},{10,... | collective-permute-start | bytes 393224 | tf_op jit(solution)/shard_map/ppermute | solution.py:467
  67.5 8.8 %collective-permute-start.13 = (bf16[64,1024]{1,0:T(8,128)(2,1)S(1)}, bf16[64,1024]{1,0:T(8,128)(2,1)S(1)}, u32[]{:S(2)}, u32[]{:S(2)}) collective-permute-start(bf16[64,1024]{1,0:T(8,128)(2,1)S(1)} %get-tuple-element.79), channel_id=1, source_target_pairs={{0,3},{1,2},{2,1},{3,0},{4,7},{5,6},{6,5},{7,4},{8,11},{9,10},{10,... | collective-permute-start | bytes 393224 | tf_op jit(solution)/shard_map/ppermute | solution.py:467
  67.9 10.1 %collective-permute-start.19 = (bf16[208,128]{1,0:T(8,128)(2,1)S(1)}, bf16[208,128]{1,0:T(8,128)(2,1)S(1)}, u32[]{:S(2)}, u32[]{:S(2)}) collective-permute-start(bf16[208,128]{1,0:T(8,128)(2,1)S(1)} %get-tuple-element.91), channel_id=1, source_target_pairs={{0,8},{4,12},{8,0},{12,4},{16,24},{20,28},{24,16},{28,20},{1,9},{5... | collective-permute-start | bytes 159752 | tf_op jit(solution)/shard_map/ppermute | solution.py:467
  71.1 14.8 %collective-permute-start.15 = (bf16[320,128]{1,0:T(8,128)(2,1)S(1)}, bf16[320,128]{1,0:T(8,128)(2,1)S(1)}, u32[]{:S(2)}, u32[]{:S(2)}) collective-permute-start(bf16[320,128]{1,0:T(8,128)(2,1)S(1)} %get-tuple-element.85), channel_id=1, source_target_pairs={{0,8},{4,12},{8,0},{12,4},{16,24},{20,28},{24,16},{28,20},{1,9},{5... | collective-permute-start | bytes 245768 | tf_op jit(solution)/shard_map/ppermute | solution.py:467
  71.2 14.7 %collective-permute-start.16 = (bf16[320,128]{1,0:T(8,128)(2,1)S(1)}, bf16[320,128]{1,0:T(8,128)(2,1)S(1)}, u32[]{:S(2)}, u32[]{:S(2)}) collective-permute-start(bf16[320,128]{1,0:T(8,128)(2,1)S(1)} %get-tuple-element.86), channel_id=1, source_target_pairs={{0,16},{4,20},{8,24},{12,28},{16,0},{20,4},{24,8},{28,12},{1,17},{... | collective-permute-start | bytes 245768 | tf_op jit(solution)/shard_map/ppermute | solution.py:467
  73.9 12.0 %collective-permute-start.17 = (bf16[320,128]{1,0:T(8,128)(2,1)S(1)}, bf16[320,128]{1,0:T(8,128)(2,1)S(1)}, u32[]{:S(2)}, u32[]{:S(2)}) collective-permute-start(bf16[320,128]{1,0:T(8,128)(2,1)S(1)} %get-tuple-element.87), channel_id=1, source_target_pairs={{0,24},{4,28},{8,16},{12,20},{16,8},{20,12},{24,0},{28,4},{1,25},{... | collective-permute-start | bytes 245768 | tf_op jit(solution)/shard_map/ppermute | solution.py:467
  76.4 9.5 %collective-permute-start.20 = (bf16[208,128]{1,0:T(8,128)(2,1)S(1)}, bf16[208,128]{1,0:T(8,128)(2,1)S(1)}, u32[]{:S(2)}, u32[]{:S(2)}) collective-permute-start(bf16[208,128]{1,0:T(8,128)(2,1)S(1)} %get-tuple-element.92), channel_id=1, source_target_pairs={{0,16},{4,20},{8,24},{12,28},{16,0},{20,4},{24,8},{28,12},{1,17},{... | collective-permute-start | bytes 159752 | tf_op jit(solution)/shard_map/ppermute | solution.py:467
  78.0 7.8 %collective-permute-start.21 = (bf16[208,128]{1,0:T(8,128)(2,1)S(1)}, bf16[208,128]{1,0:T(8,128)(2,1)S(1)}, u32[]{:S(2)}, u32[]{:S(2)}) collective-permute-start(bf16[208,128]{1,0:T(8,128)(2,1)S(1)} %get-tuple-element.93), channel_id=1, source_target_pairs={{0,24},{4,28},{8,16},{12,20},{16,8},{20,12},{24,0},{28,4},{1,25},{... | collective-permute-start | bytes 159752 | tf_op jit(solution)/shard_map/ppermute | solution.py:467
  (19 other events, 65.2 us)

commit v4 on v3

--- a/solution.py
+++ b/solution.py
@@ -10,6 +10,7 @@
 N = 128
 KW = 4
 RIM = 16
+LIMIT = 12 * 2**20
 LOGS = 16
 NORM_EPSILON = 1e-05
 
@@ -197,6 +198,14 @@
     msg[...] = packed(state, mine_logs + other_logs)
 
 
+def link_kernel(heads, farther, nearer, msg):
+    farther, nearer = farther[...], nearer[...]
+    size = nearer.shape[0] - LOGS
+    logs = logs_of(nearer, heads)
+    state = jnp.exp(spread_rows(logs, heads, size)) * state_of(farther) + state_of(nearer)
+    msg[...] = packed(state, logs + logs_of(farther, heads))
+
+
 def inside_kernel(heads, x, bc, scal, skip, cot, ow, gain, conv, y, gg, slope):
     length, width = x.shape
     xv = x[...].astype(F32)
@@ -236,8 +245,9 @@
     return columns(jnp.concatenate([inv, coef], axis=0))
 
 
-def grad_y_kernel(heads, every, total, y, gate, gg, bc, scal, gy, msg):
+def grad_y_kernel(heads, every, sums, other, y, gate, gg, bc, scal, gy, msg, total):
     length, width = y.shape
+    total[...] = sums[...] + other[...]
     cols = norm_columns(total[...], every)
     g = gate[...].astype(F32)
     act = g * sigmoid(g)
@@ -276,49 +286,41 @@
         send[at] = every[2 * at + 1 - low]
 
 
-def beside_kernel(
+def early_kernel(
     heads, count, every,
-    low, total, y, gate, gg, gain, gy, x, bc, scal, sin, cot, ow, series, rim, w, cw, slope, skip,
-    out, keep, send, sg, bb, gb, edge, yb, wide, stage,
+    low, total, y, gate, gg, gain, gy, x, bc, scal, sin, cot, series, rim, cw, slope,
+    normed, grad_gate, gp, gb, edge, keep, send, wide, stage,
 ):
     length, width = y.shape
     depth = series.shape[1]
-    cols = norm_columns(total[...], every)
-    g = gate[...].astype(F32)
-    sig = sigmoid(g)
-    act = g * sig
-    yv = y[...]
-    gated = yv * act
-    normed = (gated * cols[:, 0:1] * gain[...]).astype(BF16)
-    out[...] = mm(normed, ow[...], NT).astype(BF16)
-    grad_gated = cols[:, 0:1] * gg[...] - gated * cols[:, 1:2]
-    grad_gate = (grad_gated * yv * (sig * (1.0 + g * (1.0 - sig)))).astype(BF16)
     rows = scal[...]
     cols = columns(rows)
-    xv = x[...].astype(F32)
-    gyv = gy[...]
+    xv = x[...]
+    gyv = gy[...].astype(BF16)
     b, c = bc[:, 0:N], bc[:, N:]
-    scores = mm(c, b, NT)
-    back = jnp.zeros((length, width), F32)
     group = jnp.zeros((length, length), F32)
     for h in range(heads):
-        decay = decay_of(cols, rows, h)
-        gh = only_head(gyv, h, heads)
-        back = back + mm(scores * decay, gh, TN)
-        group = group + decay * mm(gh, xv, NT) * rows[heads + h : heads + h + 1, :]
-    bb[...] = back
+        pairs = mm(only_head(gyv, h, heads), xv, NT)
+        group = group + decay_of(cols, rows, h) * pairs * rows[heads + h : heads + h + 1, :]
     gb[...] = mm(group, c, TN)
     grow = widen(columns(jnp.exp(rows[0:heads])), heads, width)
-    grad_c = mm(group, b) + mm(gyv * grow, sin[...])
-    yb[...] = mm_exact(head_mask(heads, width), gyv * (yv - per_lane(skip, heads, width) * xv), NT)
+    grad_c = mm(group, b) + mm(gy[...] * grow, sin[...])
     clear_ends(wide, length)
     wide[RIM : RIM + length, :] = grad_c * slope[:, 2 * width - N :]
     grad_pre = conv_back(cw, wide, slice(0, N), length, 1, slice(width - N, width))
     edge[...] = grad_pre[0:RIM]
-    sg[...] = mm(grad_gate, w[0], NT) + mm(grad_pre[RIM:], w[2, :, width - N :], NT)
-    w_out = mm(cot[...], normed, TN).astype(BF16)
-    w_gate = mm(series[...], grad_gate, TN).astype(BF16)
-    w_c = (mm(series[...], grad_pre[RIM:], TN) + mm(rim[...], grad_pre[0:RIM], TN)).astype(BF16)
+    gp[...] = grad_pre[RIM:]
+    cols = norm_columns(total[...], every)
+    g = gate[...].astype(F32)
+    sig = sigmoid(g)
+    yv = y[...]
+    gated = yv * (g * sig)
+    normed[...] = (gated * cols[:, 0:1] * gain[...]).astype(BF16)
+    grad_gated = cols[:, 0:1] * gg[...] - gated * cols[:, 1:2]
+    grad_gate[...] = (grad_gated * yv * (sig * (1.0 + g * (1.0 - sig)))).astype(BF16)
+    w_out = mm(cot[...], normed[...], TN).astype(BF16)
+    w_gate = mm(series[...], grad_gate[...], TN).astype(BF16)
+    w_c = (mm(series[...], gp[...], TN) + mm(rim[...], edge[...], TN)).astype(BF16)
     piece = depth // count
     for at in range(count):
         stack_columns(stage, w_out, at, 0, piece)
@@ -327,9 +329,29 @@
     split_pair(low[0], stage, keep, send)
 
 
+def beside_kernel(
+    heads, normed, grad_gate, gp, y, gy, x, bc, scal, ow, w, skip,
+    out, sg, bb, yb,
+):
+    length, width = y.shape
+    rows = scal[...]
+    cols = columns(rows)
+    xv = x[...].astype(F32)
+    gyv = gy[...]
+    scores = mm(bc[:, N:], bc[:, 0:N], NT)
+    back = jnp.zeros((length, width), F32)
+    for h in range(heads):
+        back = back + mm(scores * decay_of(cols, rows, h), only_head(gyv, h, heads), TN)
+    bb[...] = back
+    skips = per_lane(skip, heads, width)
+    yb[...] = mm_exact(head_mask(heads, width), gyv * (y[...] - skips * xv), NT)
+    out[...] = mm(normed[...], ow[...], NT).astype(BF16)
+    sg[...] = mm(grad_gate[...], w[0], NT) + mm(gp[...], w[2, :, width - N :], NT)
+
+
 def close_kernel(
     heads, count,
-    low, x, bc, scal, gy, bb, gb, yb, sin, own, slope, series, rim, cw, skip, rate, partner, *rest,
+    low, x, bc, scal, gy, bb, gb, yb, sin, own, slope, series, rim, cw, edge_c, skip, rate, partner, *rest,
 ):
     *others, keep, send, gp, edge, graw, wide, stage = rest
     length, width = gy.shape
@@ -350,7 +372,8 @@
     grad_x = conv_back(cw, wide, slice(0, width), length, 0, slice(0, width))
     grad_b = conv_back(cw, wide, slice(width, width + N), length, 1, slice(0, N))
     edge[:, 0:width] = grad_x[0:RIM]
-    edge[:, width:] = grad_b[0:RIM]
+    edge[:, width : width + N] = grad_b[0:RIM]
+    edge[:, width + N :] = edge_c[...]
     gp[:, 0:width] = grad_x[RIM:]
     gp[:, width:] = grad_b[RIM:]
     w_x = (mm(series[...], grad_x[RIM:], TN) + mm(rim[...], grad_x[0:RIM], TN)).astype(BF16)
@@ -386,22 +409,22 @@
         part[...] = (keep[at].astype(F32) + other[at].astype(F32)).astype(BF16)
 
 
-def rows_kernel(spot, out, sg, gp, graw, edge, edge_c, w, dtw, *rest):
-    *parts, stage = rest
+def rows_kernel(low, out, sg, gp, graw, edge, w, dtw, keep, send, stage):
     length, depth = sg.shape
     width = w.shape[2]
     heads = dtw.shape[0]
     total = sg[...] + mm(graw[0:heads, :], dtw[...], TN)
     total = total + mm(gp[:, 0:width], w[1], NT) + mm(gp[:, width:], w[2, :, 0:N], NT)
-    late = mm(edge[:, 0:width], w[1], NT) + mm(edge[:, width:], w[2, :, 0:N], NT)
-    late = late + mm(edge_c[...], w[2, :, N:], NT)
+    late = mm(edge[:, 0:width], w[1], NT) + mm(edge[:, width:], w[2], NT)
     stage[:, 0:depth] = out[...]
     stage[:, depth:] = total.astype(BF16)
     stage[length - RIM :, depth:] = (total[length - RIM :, :] + late).astype(BF16)
-    piece = length // len(parts)
-    for k, part in enumerate(parts):
-        start = pl.multiple_of((spot[0] ^ k) * piece, piece)
-        part[...] = stage[pl.ds(start, piece), :]
+    piece = keep.shape[1]
+    for at in range(keep.shape[0]):
+        start = pl.multiple_of((2 * at + low[0]) * piece, piece)
+        keep[at] = stage[pl.ds(start, piece), :]
+        start = pl.multiple_of((2 * at + 1 - low[0]) * piece, piece)
+        send[at] = stage[pl.ds(start, piece), :]
 
 
 def outputs_kernel(*refs):
@@ -441,18 +464,44 @@
 
 VMEM = pl.BlockSpec(memory_space=pltpu.VMEM)
 SMEM = pl.BlockSpec(memory_space=pltpu.SMEM)
-
-
-def run(kernel, name, outs, args, scalars=(), scratch=(), flops=10**8):
+HBM = pl.BlockSpec(memory_space=pltpu.HBM)
+
+
+def run(kernel, name, outs, args, scalars=(), fetched=(), scratch=(), flops=10**8):
     moved = sum(a.size * a.dtype.itemsize for a in args)
+
+    def place(i):
+        if i in fetched:
+            return HBM
+        return SMEM if i in scalars else VMEM
+
+    def whole(*refs):
+        held, sems = refs[len(refs) - len(fetched) - 1 : -1], refs[-1]
+        refs = list(refs[: len(refs) - len(fetched) - 1])
+        copies = []
+        for k, i in enumerate(fetched):
+            copies.append(pltpu.make_async_copy(refs[i], held[k], sems.at[k]))
+            refs[i] = held[k]
+        for copy in copies:
+            copy.start()
+        for copy in copies:
+            copy.wait()
+        kernel(*refs)
+
+    holders = []
+    if fetched:
+        for i in fetched:
+            kind = pltpu.SMEM if i in scalars else pltpu.VMEM
+            holders.append(kind(args[i].shape, args[i].dtype))
+        holders.append(pltpu.SemaphoreType.DMA((len(fetched),)))
     return pl.pallas_call(
-        kernel,
+        whole if fetched else kernel,
         name=name,
         out_shape=[jax.ShapeDtypeStruct(shape, kind) for shape, kind in outs],
-        in_specs=[SMEM if i in scalars else VMEM for i in range(len(args))],
+        in_specs=[place(i) for i in range(len(args))],
         out_specs=[VMEM] * len(outs),
-        scratch_shapes=list(scratch),
-        compiler_params=pltpu.CompilerParams(vmem_limit_bytes=16 * 2**20),
+        scratch_shapes=list(scratch) + holders,
+        compiler_params=pltpu.CompilerParams(vmem_limit_bytes=LIMIT),
         cost_estimate=pl.CostEstimate(flops=flops, bytes_accessed=2 * moved, transcendentals=0),
     )(*args)
 
@@ -494,29 +543,47 @@
     hops = count // 2
     piece = depth // count
     position = lax.axis_index("tm").astype(jnp.int32)
+    spot = lax.axis_index("head").astype(jnp.int32)
     low, high = (position % 2).reshape(1), (position // 2).reshape(1)
-    spot = lax.axis_index("head").astype(jnp.int32).reshape(1)
+    low_spot, high_spot = (spot % 2).reshape(1), (spot // 2).reshape(1)
     rim = shifted(series[length - RIM :], "tm", 1)
     state_msg = ((width + LOGS, N), BF16)
 
-    def passed(msg, back):
-        partner = swapped(msg, "tm", 1)
-        (both,) = run(part(pair_kernel, heads, back), "pair", [state_msg], [low, msg, partner], (0,))
-        sign = -1 if back else 1
-        return [partner] + [shifted(both, "tm", sign * 2 * d) for d in range(hops - 1, 0, -1)]
-
-    def summed(keep, send, name):
-        rows = keep.shape[1]
-        own, *parts = run(
-            halve_kernel, name, [((rows, N), F32)] + [((rows, N), BF16)] * (hops - 1),
-            [high, keep, swapped(send, "tm", 1)], (0,),
+    def passed(msg, back, during):
+        made = []
+
+        def meanwhile(k, block):
+            if k < len(during):
+                block, extra = lax.optimization_barrier((block, during[k](made)))
+                made.append(extra)
+            return block
+
+        partner = meanwhile(0, swapped(msg, "tm", 1))
+        (msg,) = run(part(pair_kernel, heads, back), "pair", [state_msg], [low, msg, partner], (0,))
+        entered = []
+        hop = 1
+        while hop < hops:
+            other = meanwhile(len(made), shifted(msg, "tm", (-2 if back else 2) * hop))
+            entered.append(other)
+            hop *= 2
+            if hop < hops:
+                (msg,) = run(part(link_kernel, heads), "link", [state_msg], [other, msg])
+        return [partner] + entered[::-1], made
+
+    def halved(keep, send, axis, where, name):
+        most, rows, cols = keep.shape
+        return run(
+            halve_kernel, name, [((rows, cols), F32)] + [((rows, cols), BF16)] * (most - 1),
+            [where, keep, swapped(send, axis, 1)], (0,),
         )
-        return [own] + [swapped(block, "tm", 2 * (k + 1)) for k, block in enumerate(parts)]
+
+    def gathered(blocks, axis):
+        return [blocks[0]] + [swapped(block, axis, 2 * k) for k, block in enumerate(blocks) if k]
 
     gate, pre, scal = run(
         part(project_kernel, heads), "project",
         [((length, width), BF16), ((length, 2 * width), BF16), ((4 * heads, length), F32)],
-        [series, w, dtw, step_bias, log_rate], (3, 4),
+        [series, w, dtw, step_bias, log_rate], (3, 4), (0, 1, 2, 3, 4),
     )
     x, bc, conv, own, msg = run(
         part(conv_kernel, heads), "conv",
@@ -527,83 +594,109 @@
             ((width, N), F32),
             state_msg,
         ],
-        [pre, rim, w, conv_weight, conv_bias, scal],
+        [pre, rim, w, conv_weight, conv_bias, scal], (), (2, 3, 4),
         scratch=[pltpu.VMEM((length + 8, 2 * width), F32)],
     )
-    ahead = passed(msg, False)
-    inside, gg, slope = run(
-        part(inside_kernel, heads), "inside",
-        [((length, width), F32), ((length, width), F32), ((length, 2 * width), F32)],
-        [x, bc, scal, skip_gain, cotangent, out_weight, gain, conv], (3,),
-    )
+
+    def inner(made):
+        return run(
+            part(inside_kernel, heads), "inside",
+            [((length, width), F32), ((length, width), F32), ((length, 2 * width), F32)],
+            [x, bc, scal, skip_gain, cotangent, out_weight, gain, conv], (3,), (3, 4, 5, 6),
+        )
+
+    ahead, ((inside, gg, slope),) = passed(msg, False, [inner])
     y, sin, sums = run(
         part(join_kernel, heads), "join",
         [((length, width), F32), ((width, N), F32), ((8, length), F32)],
         [low, inside, gg, gate, bc, scal] + ahead, (0,),
     )
-    total = lax.psum(sums, "head")
-    gy, msg = run(
+    flip = 1
+    while 2 * flip < parts:
+        sums = sums + swapped(sums, "head", flip)
+        flip *= 2
+    gy, msg, total = run(
         part(grad_y_kernel, heads, every), "grad_y",
-        [((length, width), F32), state_msg],
-        [total, y, gate, gg, bc, scal],
-    )
-    behind = passed(msg, True)
+        [((length, width), F32), state_msg, ((8, length), F32)],
+        [sums, swapped(sums, "head", flip), y, gate, gg, bc, scal],
+    )
     early, late = 5 * piece, 3 * piece + LOGS
-    out, keep, send, sg, bb, gb, edge_c, yb = run(
-        part(beside_kernel, heads, count, every), "beside",
-        [
-            ((length, depth), BF16),
-            ((hops, early, N), BF16),
-            ((hops, early, N), BF16),
-            ((length, depth), F32),
-            ((length, width), F32),
-            ((length, N), F32),
-            ((RIM, N), BF16),
-            ((8, length), F32),
-        ],
-        [
-            low, total, y, gate, gg, gain, gy, x, bc, scal, sin, cotangent, out_weight, series,
-            rim, w, conv_weight, slope, skip_gain,
-        ],
-        (0, 18),
-        scratch=[
-            pltpu.VMEM((length + RIM + 8, N), F32),
-            pltpu.VMEM((count, early, N), BF16),
-        ],
-    )
-    early_parts = summed(keep, send, "halve_early")
+
+    def early_part(made):
+        return run(
+            part(early_kernel, heads, count, every), "early",
+            [
+                ((length, width), BF16),
+                ((length, width), BF16),
+                ((length, N), BF16),
+                ((length, N), F32),
+                ((RIM, N), BF16),
+                ((hops, early, N), BF16),
+                ((hops, early, N), BF16),
+            ],
+            [
+                low, total, y, gate, gg, gain, gy, x, bc, scal, sin, cotangent, series, rim,
+                conv_weight, slope,
+            ],
+            (0,), (5, 11, 12, 14),
+            scratch=[
+                pltpu.VMEM((length + RIM + 8, N), F32),
+                pltpu.VMEM((count, early, N), BF16),
+            ],
+        )
+
+    def beside_part(made):
+        normed, grad_gate, gp_c = made[0][0:3]
+        return run(
+            part(beside_kernel, heads), "beside",
+            [
+                ((length, depth), BF16),
+                ((length, depth), F32),
+                ((length, width), F32),
+                ((8, length), F32),
+            ],
+            [normed, grad_gate, gp_c, y, gy, x, bc, scal, out_weight, w, skip_gain],
+            (10,), (8, 9, 10),
+        )
+
+    behind, (firsts, (out, sg, bb, yb)) = passed(msg, True, [early_part, beside_part])
+    gb, edge_c, keep, send = firsts[3:]
+    early_parts = halved(keep, send, "tm", high, "halve_early")
+    behind, early_parts = lax.optimization_barrier((behind, early_parts))
+    early_parts = gathered(early_parts, "tm")
     keep, send, gp, edge, graw = run(
         part(close_kernel, heads, count), "close",
         [
             ((hops, late, N), BF16),
             ((hops, late, N), BF16),
             ((length, width + N), BF16),
-            ((RIM, width + N), BF16),
+            ((RIM, 2 * width), BF16),
             ((2 * heads, length), F32),
         ],
         [
-            low, x, bc, scal, gy, bb, gb, yb, sin, own, slope, series, rim, conv_weight,
+            low, x, bc, scal, gy, bb, gb, yb, sin, own, slope, series, rim, conv_weight, edge_c,
             skip_gain, log_rate,
         ]
         + behind,
-        (0, 14, 15),
+        (0, 15, 16), (11, 13, 15, 16),
         scratch=[
             pltpu.VMEM((length + RIM + 8, width + N), F32),
             pltpu.VMEM((count, late, N), BF16),
         ],
     )
-    late_parts = summed(keep, send, "halve_late")
-    edge, edge_c = shifted(edge, "tm", -1), shifted(edge_c, "tm", -1)
-    both = run(
+    late_parts = halved(keep, send, "tm", high, "halve_late")
+    late_parts = gathered(late_parts, "tm")
+    edge = shifted(edge, "tm", -1)
+    rows = length // parts
+    keep, send = run(
         rows_kernel, "rows",
-        [((length // parts, 2 * depth), BF16)] * parts,
-        [spot, out, sg, gp, graw, edge, edge_c, w, dtw], (0,),
+        [((parts // 2, rows, 2 * depth), BF16)] * 2,
+        [low_spot, out, sg, gp, graw, edge, w, dtw], (0,), (6, 7),
         scratch=[pltpu.VMEM((length, 2 * depth), BF16)],
     )
-    both = [both[0]] + [swapped(both[k], "head", k) for k in range(1, parts)]
+    both = gathered(halved(keep, send, "head", high_spot, "halve_rows"), "head")
     layer_out, series_grad = run(
-        outputs_kernel, "outputs",
-        [((length // parts, depth), BF16), ((length // parts, depth), F32)], both,
+        outputs_kernel, "outputs", [((rows, depth), BF16), ((rows, depth), F32)], both,
     )
     w_in_grad, w_dt_grad, w_out_grad = run(
         part(total_kernel, hops), "total",

time: 87.2 us -> 90 us (1.032)
  local copies, waits for them, and re-layouts: 7.25 us -> 14.1 us
  blocking collectives: 5.77 us -> 0 us
  waiting for transfers between devices: 20 us -> 24.6 us
  starting transfers between devices: 38.2 us -> 33.7 us
  Pallas kernels: 14.4 us -> 15.9 us
    unnamed x42 -> x74, local copies, waits for them, and re-layouts: 6.52 us -> 13.3 us
    psum x1 -> x0, blocking collectives: 5.77 us -> none  [body(): total = lax.psum(sums, 'head')]
    ppermute x13 -> x14, waiting for transfers between devices: 8.31 us -> 11.8 us  [swapped(): lax.ppermute(block, axis, [(i, i ^ flip) for i in range(lax.axis_size(axi...]
    ppermute x9 -> x6, starting transfers between devices: 20.6 us -> 17.5 us  [shifted(): return lax.ppermute(block, axis, route)]
    pallas_call x14 -> x18, Pallas kernels: 14.4 us -> 15.9 us  [run(): pl.pallas_call(whole if fetched else kernel, name=name, out_shape=[jax.Sh...]
    ppermute x13 -> x14, starting transfers between devices: 17.6 us -> 16.3 us  [swapped(): lax.ppermute(block, axis, [(i, i ^ flip) for i in range(lax.axis_size(axi...]
    ppermute x9 -> x6, waiting for transfers between devices: 11.7 us -> 12.8 us  [shifted(): return lax.ppermute(block, axis, route)]
  transfers between devices with their start and end apart: 22 -> 20, of which waited for: 5 -> 12; matrix products, arithmetic and copies ran while one was open for 0% -> 0% of each run, Pallas kernels for 13% -> 10%
where the time goes in v4:
time: 90 us; the launch traced here: 89.4 us
  starting transfers between devices  33.7 us (37%)
  waiting for transfers between devices  24.6 us (27%)
  Pallas kernels  15.9 us (18%)
  local copies, waits for them, and re-layouts  14.1 us (16%)
  between operations  1.04 us (1%)
    ppermute x6, starting transfers between devices, shifted(): return lax.ppermute(block, axis, route)  17.5 us
    ppermute x14, starting transfers between devices, swapped(): lax.ppermute(block, axis, [(i, i ^ flip) for i in range(lax.axis_size(axi...  16.3 us
    pallas_call x18, Pallas kernels, run(): pl.pallas_call(whole if fetched else kernel, name=name, out_shape=[jax.Sh...  15.9 us
    unnamed x74, local copies, waits for them, and re-layouts  13.3 us
    ppermute x6, waiting for transfers between devices, shifted(): return lax.ppermute(block, axis, route)  12.8 us
    ppermute x14, waiting for transfers between devices, swapped(): lax.ppermute(block, axis, [(i, i ^ flip) for i in range(lax.axis_size(axi...  11.8 us
  transfers between devices with their start and end apart: 20, of which 12 were waited for; matrix products, arithmetic and copies ran while one was open for 0% of the time, Pallas kernels for 10%

profile of v4, /device:TPU:0, one launch (start us, length us, event | category | flops | bytes accessed | tf_op | source)
XLA Modules:
  0.0 89.4 jit_solution(7236795103666407746)
XLA Ops:
  1.4 4.9 %collective-permute-start = (bf16[16,512]{1,0:T(8,128)(2,1)S(1)}, bf16[16,512]{1,0:T(8,128)(2,1)S(1)}, u32[]{:S(2)}, u32[]{:S(2)}) collective-permute-start(bf16[16,512]{1,0:T(8,128)(2,1)S(1)} %slice.3), channel_id=1, source_target_pairs={{0,4},{4,8},{8,12},{12,16},{16,20},{20,24},{24,28},{1,5},{5,9},{9,... | collective-permute-start | bytes 49160 | tf_op jit(solution)/shard_map/ppermute | solution.py:512
  9.0 1.6 %project.1 = (bf16[256,256]{1,0:T(8,128)(2,1)S(1)}, bf16[256,512]{1,0:T(8,128)(2,1)S(1)}, f32[16,256]{1,0:T(8,128)S(1)}) custom-call(bf16[256,512]{1,0:T(8,128)(2,1)S(1)} %copy-done.2, bf16[3,512,256]{2,1,0:T(8,128)(2,1)S(1)} %bitcast.9, bf16[4,512]{1,0:T(4,128)(2,1)S(1)} %bitcast.13, f32[4]{0:T(128)S(1)} %copy-done.28, f32[4]{0:T(128)S(1)} %copy-done.26), custom_call_target="tpu_custom_call" | custom-call | flops 100000000 | bytes 2105408 | tf_op jit(solution)/shard_map/project/pallas_call | solution.py:497
  13.0 1.5 %collective-permute-start.1 = (bf16[272,128]{1,0:T(8,128)(2,1)S(1)}, bf16[272,128]{1,0:T(8,128)(2,1)S(1)}, u32[]{:S(2)}, u32[]{:S(2)}) collective-permute-start(bf16[272,128]{1,0:T(8,128)(2,1)S(1)} %get-tuple-element.81.mine), channel_id=1, source_target_pairs={{0,4},{4,0},{8,12},{12,8},{16,20},{20,16},{24,28},{28,24},{1,5},{5... | collective-permute-start | bytes 208904 | tf_op jit(solution)/shard_map/ppermute | solution.py:516
  17.4 3.5 %collective-permute-start.2 = (bf16[272,128]{1,0:T(8,128)(2,1)S(1)}, bf16[272,128]{1,0:T(8,128)(2,1)S(1)}, u32[]{:S(2)}, u32[]{:S(2)}) collective-permute-start(bf16[272,128]{1,0:T(8,128)(2,1)S(1)} %pair.2.nearer), channel_id=1, source_target_pairs={{0,8},{4,12},{8,16},{12,20},{16,24},{20,28},{1,9},{5,13},{9,17},{1... | collective-permute-start | bytes 208904 | tf_op jit(solution)/shard_map/ppermute | solution.py:512
  20.9 1.9 %collective-permute-done.2.farther.rest_1_ = bf16[272,128]{1,0:T(8,128)(2,1)S(1)} collective-permute-done((bf16[272,128]{1,0:T(8,128)(2,1)S(1)}, bf16[272,128]{1,0:T(8,128)(2,1)S(1)}, u32[]{:S(2)}, u32[]{:S(2)}) %collective-permute-start.2) | collective-permute-done | bytes 69664 | tf_op jit(solution)/shard_map/ppermute | solution.py:512
  22.8 5.3 %collective-permute-start.3 = (bf16[272,128]{1,0:T(8,128)(2,1)S(1)}, bf16[272,128]{1,0:T(8,128)(2,1)S(1)}, u32[]{:S(2)}, u32[]{:S(2)}) collective-permute-start(bf16[272,128]{1,0:T(8,128)(2,1)S(1)} %link.2), channel_id=1, source_target_pairs={{0,16},{4,20},{8,24},{12,28},{1,17},{5,21},{9,25},{13,29},{2,18},{... | collective-permute-start | bytes 208904 | tf_op jit(solution)/shard_map/ppermute | solution.py:512
  28.1 1.9 %collective-permute-done.3.rest_0_ = bf16[272,128]{1,0:T(8,128)(2,1)S(1)} collective-permute-done((bf16[272,128]{1,0:T(8,128)(2,1)S(1)}, bf16[272,128]{1,0:T(8,128)(2,1)S(1)}, u32[]{:S(2)}, u32[]{:S(2)}) %collective-permute-start.3) | collective-permute-done | bytes 69664 | tf_op jit(solution)/shard_map/ppermute | solution.py:512
  32.1 1.5 %collective-permute-start.5 = (f32[8,256]{1,0:T(8,128)S(1)}, f32[8,256]{1,0:T(8,128)S(1)}, u32[]{:S(2)}, u32[]{:S(2)}) collective-permute-start(f32[8,256]{1,0:T(8,128)S(1)} %add.14.sums), channel_id=1, source_target_pairs={{0,2},{1,3},{2,0},{3,1},{4,6},{5,7},{6,4},{7,5},{8,10},{9,11},{10,... | collective-permute-start | bytes 24584 | tf_op jit(solution)/shard_map/ppermute | solution.py:516
  33.6 2.2 %collective-permute-done.5.other = f32[8,256]{1,0:T(8,128)S(1)} collective-permute-done((f32[8,256]{1,0:T(8,128)S(1)}, f32[8,256]{1,0:T(8,128)S(1)}, u32[]{:S(2)}, u32[]{:S(2)}) %collective-permute-start.5) | collective-permute-done | bytes 8224 | tf_op jit(solution)/shard_map/ppermute | solution.py:516
  36.5 1.6 %collective-permute-start.6 = (bf16[272,128]{1,0:T(8,128)(2,1)S(1)}, bf16[272,128]{1,0:T(8,128)(2,1)S(1)}, u32[]{:S(2)}, u32[]{:S(2)}) collective-permute-start(bf16[272,128]{1,0:T(8,128)(2,1)S(1)} %get-tuple-element.94.mine), channel_id=1, source_target_pairs={{0,4},{4,0},{8,12},{12,8},{16,20},{20,16},{24,28},{28,24},{1,5},{5... | collective-permute-start | bytes 208904 | tf_op jit(solution)/shard_map/ppermute | solution.py:516
  38.1 2.2 %early.1 = (bf16[256,256]{1,0:T(8,128)(2,1)S(1)}, bf16[256,256]{1,0:T(8,128)(2,1)S(1)}, bf16[256,128]{1,0:T(8,128)(2,1)S(1)}, f32[256,128]{1,0:T(8,128)S(1)}, bf...) custom-call(s32[1]{0:T(128)} %bitcast.2.low.refs_0_, ...), custom_call_target="tpu_custom_call" | custom-call | flops 100000000 | bytes 4818952 | tf_op jit(solution)/shard_map/early/pallas_call | solution.py:497
  43.7 1.7 %beside.1 = (bf16[256,512]{1,0:T(8,128)(2,1)S(1)}, f32[256,512]{1,0:T(8,128)S(1)}, f32[256,256]{1,0:T(8,128)S(1)}, f32[8,256]{1,0:T(8,128)S(1)}) custom-call(bf16[256,256]{1,0:T(8,128)(2,1)S(1)} %get-tuple-element.107.refs_0_, bf16[256,256]{1,0:T(8,128)(2,1)S(1)} %get-tuple-element.108.refs_1_, bf16[256,128]{1,0:T(8,128)(2,1)S(1)} %get-tuple-element.109.refs_2_, ...), custom_call_target="tpu_custom_call" | custom-call | flops 100000000 | bytes 4358176 | tf_op jit(solution)/shard_map/beside/pallas_call | solution.py:497
  46.9 1.7 %collective-permute-done.7.farther.refs_19_ = bf16[272,128]{1,0:T(8,128)(2,1)S(1)} collective-permute-done((bf16[272,128]{1,0:T(8,128)(2,1)S(1)}, bf16[272,128]{1,0:T(8,128)(2,1)S(1)}, u32[]{:S(2)}, u32[]{:S(2)}) %collective-permute-start.7) | collective-permute-done | bytes 69664 | tf_op jit(solution)/shard_map/ppermute | solution.py:512
  53.6 2.7 %collective-permute-done.8.refs_18_ = bf16[272,128]{1,0:T(8,128)(2,1)S(1)} collective-permute-done((bf16[272,128]{1,0:T(8,128)(2,1)S(1)}, bf16[272,128]{1,0:T(8,128)(2,1)S(1)}, u32[]{:S(2)}, u32[]{:S(2)}) %collective-permute-start.8) | collective-permute-done | bytes 69664 | tf_op jit(solution)/shard_map/ppermute | solution.py:512
  57.9 3.1 %close.1 = (bf16[4,208,128]{2,1,0:T(8,128)(2,1)S(1)}, bf16[4,208,128]{2,1,0:T(8,128)(2,1)S(1)}, bf16[256,384]{1,0:T(8,128)(2,1)S(1)}, bf16[16,512]{1,0:T(8,128)(2,1)}, f32[8,256]{1,0:T(8,128)S(1)}) custom-call(s32[1]{0:T(128)} %bitcast.2.low.refs_0_, bf16[256,256]{1,0:T(8,128)(2,1)S(1)} %get-tuple-element.82.refs_0_.refs_7_.refs_5_.refs_1_, ...), custom_call_target="tpu_custom_call" | custom-call | flops 100000000 | bytes 4456520 | tf_op jit(solution)/shard_map/close/pallas_call | solution.py:497
  63.6 4.5 %collective-permute-done.10.refs_5_ = bf16[16,512]{1,0:T(8,128)(2,1)S(1)} collective-permute-done((bf16[16,512]{1,0:T(8,128)(2,1)}, bf16[16,512]{1,0:T(8,128)(2,1)S(1)}, u32[]{:S(2)}, u32[]{:S(2)}) %collective-permute-start.10) | collective-permute-done | bytes 16416 | tf_op jit(solution)/shard_map/ppermute | solution.py:512
  70.0 1.5 %collective-permute-start.16 = (bf16[4,208,128]{2,1,0:T(8,128)(2,1)S(1)}, bf16[4,208,128]{2,1,0:T(8,128)(2,1)S(1)}, u32[]{:S(2)}, u32[]{:S(2)}) collective-permute-start(bf16[4,208,128]{2,1,0:T(8,128)(2,1)S(1)} %copy-done.30), channel_id=1, source_target_pairs={{0,4},{4,0},{8,12},{12,8},{16,20},{20,16},{24,28},{28,24},{1,5},{5... | collective-permute-start | bytes 638984 | tf_op jit(solution)/shard_map/ppermute | solution.py:516
  71.5 2.0 %collective-permute-start.13 = (bf16[320,128]{1,0:T(8,128)(2,1)S(1)}, bf16[320,128]{1,0:T(8,128)(2,1)S(1)}, u32[]{:S(2)}, u32[]{:S(2)}) collective-permute-start(bf16[320,128]{1,0:T(8,128)(2,1)S(1)} %copy-done.36), channel_id=1, source_target_pairs={{0,8},{4,12},{8,0},{12,4},{16,24},{20,28},{24,16},{28,20},{1,9},{5... | collective-permute-start | bytes 245768 | tf_op jit(solution)/shard_map/ppermute | solution.py:516
  73.6 1.6 %collective-permute-start.12 = (bf16[64,1024]{1,0:T(8,128)(2,1)S(1)}, bf16[64,1024]{1,0:T(8,128)(2,1)S(1)}, u32[]{:S(2)}, u32[]{:S(2)}) collective-permute-start(bf16[64,1024]{1,0:T(8,128)(2,1)S(1)} %get-tuple-element.137), channel_id=1, source_target_pairs={{0,2},{1,3},{2,0},{3,1},{4,6},{5,7},{6,4},{7,5},{8,10},{9,11},{10,... | collective-permute-start | bytes 393224 | tf_op jit(solution)/shard_map/ppermute | solution.py:516
  75.1 2.4 %collective-permute-start.15 = (bf16[320,128]{1,0:T(8,128)(2,1)S(1)}, bf16[320,128]{1,0:T(8,128)(2,1)S(1)}, u32[]{:S(2)}, u32[]{:S(2)}) collective-permute-start(bf16[320,128]{1,0:T(8,128)(2,1)S(1)} %copy-done.32), channel_id=1, source_target_pairs={{0,24},{4,28},{8,16},{12,20},{16,8},{20,12},{24,0},{28,4},{1,25},{... | collective-permute-start | bytes 245768 | tf_op jit(solution)/shard_map/ppermute | solution.py:516
  77.6 1.7 %collective-permute-start.17 = (bf16[208,128]{1,0:T(8,128)(2,1)S(1)}, bf16[208,128]{1,0:T(8,128)(2,1)S(1)}, u32[]{:S(2)}, u32[]{:S(2)}) collective-permute-start(bf16[208,128]{1,0:T(8,128)(2,1)S(1)} %get-tuple-element.147), channel_id=1, source_target_pairs={{0,8},{4,12},{8,0},{12,4},{16,24},{20,28},{24,16},{28,20},{1,9},{5... | collective-permute-start | bytes 159752 | tf_op jit(solution)/shard_map/ppermute | solution.py:516
  80.2 1.8 %collective-permute-done.14.refs_2_ = bf16[320,128]{1,0:T(8,128)(2,1)S(1)} collective-permute-done((bf16[320,128]{1,0:T(8,128)(2,1)S(1)}, bf16[320,128]{1,0:T(8,128)(2,1)S(1)}, u32[]{:S(2)}, u32[]{:S(2)}) %collective-permute-start.14) | collective-permute-done | bytes 81952 | tf_op jit(solution)/shard_map/ppermute | solution.py:516
  82.9 3.6 %collective-permute-done.18.refs_6_ = bf16[208,128]{1,0:T(8,128)(2,1)S(1)} collective-permute-done((bf16[208,128]{1,0:T(8,128)(2,1)S(1)}, bf16[208,128]{1,0:T(8,128)(2,1)S(1)}, u32[]{:S(2)}, u32[]{:S(2)}) %collective-permute-start.18) | collective-permute-done | bytes 53280 | tf_op jit(solution)/shard_map/ppermute | solution.py:516
  86.5 1.5 %collective-permute-done.19.refs_7_ = bf16[208,128]{1,0:T(8,128)(2,1)S(1)} collective-permute-done((bf16[208,128]{1,0:T(8,128)(2,1)S(1)}, bf16[208,128]{1,0:T(8,128)(2,1)S(1)}, u32[]{:S(2)}, u32[]{:S(2)}) %collective-permute-start.19) | collective-permute-done | bytes 53280 | tf_op jit(solution)/shard_map/ppermute | solution.py:516
  (110 shorter events, 30.5 us)
Async XLA Ops:
  1.4 9.2 %collective-permute-start = (bf16[16,512]{1,0:T(8,128)(2,1)S(1)}, bf16[16,512]{1,0:T(8,128)(2,1)S(1)}, u32[]{:S(2)}, u32[]{:S(2)}) collective-permute-start(bf16[16,512]{1,0:T(8,128)(2,1)S(1)} %slice.3), channel_id=1, source_target_pairs={{0,4},{4,8},{8,12},{12,16},{16,20},{20,24},{24,28},{1,5},{5,9},{9,... | collective-permute-start | bytes 49160 | tf_op jit(solution)/shard_map/ppermute | solution.py:512
  13.0 4.3 %collective-permute-start.1 = (bf16[272,128]{1,0:T(8,128)(2,1)S(1)}, bf16[272,128]{1,0:T(8,128)(2,1)S(1)}, u32[]{:S(2)}, u32[]{:S(2)}) collective-permute-start(bf16[272,128]{1,0:T(8,128)(2,1)S(1)} %get-tuple-element.81.mine), channel_id=1, source_target_pairs={{0,4},{4,0},{8,12},{12,8},{16,20},{20,16},{24,28},{28,24},{1,5},{5... | collective-permute-start | bytes 208904 | tf_op jit(solution)/shard_map/ppermute | solution.py:516
  17.4 5.4 %collective-permute-start.2 = (bf16[272,128]{1,0:T(8,128)(2,1)S(1)}, bf16[272,128]{1,0:T(8,128)(2,1)S(1)}, u32[]{:S(2)}, u32[]{:S(2)}) collective-permute-start(bf16[272,128]{1,0:T(8,128)(2,1)S(1)} %pair.2.nearer), channel_id=1, source_target_pairs={{0,8},{4,12},{8,16},{12,20},{16,24},{20,28},{1,9},{5,13},{9,17},{1... | collective-permute-start | bytes 208904 | tf_op jit(solution)/shard_map/ppermute | solution.py:512
  22.8 7.2 %collective-permute-start.3 = (bf16[272,128]{1,0:T(8,128)(2,1)S(1)}, bf16[272,128]{1,0:T(8,128)(2,1)S(1)}, u32[]{:S(2)}, u32[]{:S(2)}) collective-permute-start(bf16[272,128]{1,0:T(8,128)(2,1)S(1)} %link.2), channel_id=1, source_target_pairs={{0,16},{4,20},{8,24},{12,28},{1,17},{5,21},{9,25},{13,29},{2,18},{... | collective-permute-start | bytes 208904 | tf_op jit(solution)/shard_map/ppermute | solution.py:512
  30.9 1.2 %collective-permute-start.4 = (f32[8,256]{1,0:T(8,128)S(1)}, f32[8,256]{1,0:T(8,128)S(1)}, u32[]{:S(2)}, u32[]{:S(2)}) collective-permute-start(f32[8,256]{1,0:T(8,128)S(1)} %get-tuple-element.92), channel_id=1, source_target_pairs={{0,1},{1,0},{2,3},{3,2},{4,5},{5,4},{6,7},{7,6},{8,9},{9,8},{10,11... | collective-permute-start | bytes 24584 | tf_op jit(solution)/shard_map/ppermute | solution.py:516
  32.1 3.7 %collective-permute-start.5 = (f32[8,256]{1,0:T(8,128)S(1)}, f32[8,256]{1,0:T(8,128)S(1)}, u32[]{:S(2)}, u32[]{:S(2)}) collective-permute-start(f32[8,256]{1,0:T(8,128)S(1)} %add.14.sums), channel_id=1, source_target_pairs={{0,2},{1,3},{2,0},{3,1},{4,6},{5,7},{6,4},{7,5},{8,10},{9,11},{10,... | collective-permute-start | bytes 24584 | tf_op jit(solution)/shard_map/ppermute | solution.py:516
  36.5 4.5 %collective-permute-start.6 = (bf16[272,128]{1,0:T(8,128)(2,1)S(1)}, bf16[272,128]{1,0:T(8,128)(2,1)S(1)}, u32[]{:S(2)}, u32[]{:S(2)}) collective-permute-start(bf16[272,128]{1,0:T(8,128)(2,1)S(1)} %get-tuple-element.94.mine), channel_id=1, source_target_pairs={{0,4},{4,0},{8,12},{12,8},{16,20},{20,16},{24,28},{28,24},{1,5},{5... | collective-permute-start | bytes 208904 | tf_op jit(solution)/shard_map/ppermute | solution.py:516
  40.9 9.6 %collective-permute-start.9 = (bf16[4,320,128]{2,1,0:T(8,128)(2,1)}, bf16[4,320,128]{2,1,0:T(8,128)(2,1)}, u32[]{:S(2)}, u32[]{:S(2)}) collective-permute-start(bf16[4,320,128]{2,1,0:T(8,128)(2,1)} %get-tuple-element.123), channel_id=1, source_target_pairs={{0,4},{4,0},{8,12},{12,8},{16,20},{20,16},{24,28},{28,24},{1,5},{5... | collective-permute-start | bytes 983048 | tf_op jit(solution)/shard_map/ppermute | solution.py:516
  42.4 6.2 %collective-permute-start.7 = (bf16[272,128]{1,0:T(8,128)(2,1)S(1)}, bf16[272,128]{1,0:T(8,128)(2,1)S(1)}, u32[]{:S(2)}, u32[]{:S(2)}) collective-permute-start(bf16[272,128]{1,0:T(8,128)(2,1)S(1)} %pair.3.nearer), channel_id=1, source_target_pairs={{8,0},{12,4},{16,8},{20,12},{24,16},{28,20},{9,1},{13,5},{17,9},{2... | collective-permute-start | bytes 208904 | tf_op jit(solution)/shard_map/ppermute | solution.py:512
  49.3 7.1 %collective-permute-start.8 = (bf16[272,128]{1,0:T(8,128)(2,1)S(1)}, bf16[272,128]{1,0:T(8,128)(2,1)S(1)}, u32[]{:S(2)}, u32[]{:S(2)}) collective-permute-start(bf16[272,128]{1,0:T(8,128)(2,1)S(1)} %link.3), channel_id=1, source_target_pairs={{16,0},{20,4},{24,8},{28,12},{17,1},{21,5},{25,9},{29,13},{18,2},{... | collective-permute-start | bytes 208904 | tf_op jit(solution)/shard_map/ppermute | solution.py:512
  50.6 6.4 %copy-start.9 = (f32[256,256]{1,0:T(8,128)S(1)}, f32[256,256]{1,0:T(8,128)}, u32[]{:S(2)}) copy-start(f32[256,256]{1,0:T(8,128)} %copy-done.8) | copy-start | bytes 786436
  50.6 6.4 %copy-start.15 = (f32[256,128]{1,0:T(8,128)S(1)}, f32[256,128]{1,0:T(8,128)}, u32[]{:S(2)}) copy-start(f32[256,128]{1,0:T(8,128)} %copy-done.14) | copy-start | bytes 393220
  50.6 6.4 %copy-start.17 = (f32[256,128]{1,0:T(8,128)S(1)}, f32[256,128]{1,0:T(8,128)}, u32[]{:S(2)}) copy-start(f32[256,128]{1,0:T(8,128)} %copy-done.16) | copy-start | bytes 393220
  57.9 10.3 %copy-start.11 = (bf16[256,512]{1,0:T(8,128)(2,1)S(1)}, bf16[256,512]{1,0:T(8,128)(2,1)}, u32[]{:S(2)}) copy-start(bf16[256,512]{1,0:T(8,128)(2,1)} %copy-done.10) | copy-start | bytes 786436
  62.3 5.8 %collective-permute-start.10 = (bf16[16,512]{1,0:T(8,128)(2,1)}, bf16[16,512]{1,0:T(8,128)(2,1)S(1)}, u32[]{:S(2)}, u32[]{:S(2)}) collective-permute-start(bf16[16,512]{1,0:T(8,128)(2,1)} %get-tuple-element.133), channel_id=1, source_target_pairs={{4,0},{8,4},{12,8},{16,12},{20,16},{24,20},{28,24},{5,1},{9,5},{13... | collective-permute-start | bytes 49160 | tf_op jit(solution)/shard_map/ppermute | solution.py:512
  69.7 3.8 %collective-permute-start.11 = (bf16[2,64,1024]{2,1,0:T(8,128)(2,1)S(1)}, bf16[2,64,1024]{2,1,0:T(8,128)(2,1)S(1)}, u32[]{:S(2)}, u32[]{:S(2)}) collective-permute-start(bf16[2,64,1024]{2,1,0:T(8,128)(2,1)S(1)} %get-tuple-element.135), channel_id=1, source_target_pairs={{0,1},{1,0},{2,3},{3,2},{4,5},{5,4},{6,7},{7,6},{8,9},{9,8},{10,11... | collective-permute-start | bytes 786440 | tf_op jit(solution)/shard_map/ppermute | solution.py:516
  70.0 7.6 %collective-permute-start.16 = (bf16[4,208,128]{2,1,0:T(8,128)(2,1)S(1)}, bf16[4,208,128]{2,1,0:T(8,128)(2,1)S(1)}, u32[]{:S(2)}, u32[]{:S(2)}) collective-permute-start(bf16[4,208,128]{2,1,0:T(8,128)(2,1)S(1)} %copy-done.30), channel_id=1, source_target_pairs={{0,4},{4,0},{8,12},{12,8},{16,20},{20,16},{24,28},{28,24},{1,5},{5... | collective-permute-start | bytes 638984 | tf_op jit(solution)/shard_map/ppermute | solution.py:516
  71.5 7.8 %collective-permute-start.13 = (bf16[320,128]{1,0:T(8,128)(2,1)S(1)}, bf16[320,128]{1,0:T(8,128)(2,1)S(1)}, u32[]{:S(2)}, u32[]{:S(2)}) collective-permute-start(bf16[320,128]{1,0:T(8,128)(2,1)S(1)} %copy-done.36), channel_id=1, source_target_pairs={{0,8},{4,12},{8,0},{12,4},{16,24},{20,28},{24,16},{28,20},{1,9},{5... | collective-permute-start | bytes 245768 | tf_op jit(solution)/shard_map/ppermute | solution.py:516
  73.5 8.4 %collective-permute-start.14 = (bf16[320,128]{1,0:T(8,128)(2,1)S(1)}, bf16[320,128]{1,0:T(8,128)(2,1)S(1)}, u32[]{:S(2)}, u32[]{:S(2)}) collective-permute-start(bf16[320,128]{1,0:T(8,128)(2,1)S(1)} %copy-done.34), channel_id=1, source_target_pairs={{0,16},{4,20},{8,24},{12,28},{16,0},{20,4},{24,8},{28,12},{1,17},{... | collective-permute-start | bytes 245768 | tf_op jit(solution)/shard_map/ppermute | solution.py:516
  73.6 15.1 %collective-permute-start.12 = (bf16[64,1024]{1,0:T(8,128)(2,1)S(1)}, bf16[64,1024]{1,0:T(8,128)(2,1)S(1)}, u32[]{:S(2)}, u32[]{:S(2)}) collective-permute-start(bf16[64,1024]{1,0:T(8,128)(2,1)S(1)} %get-tuple-element.137), channel_id=1, source_target_pairs={{0,2},{1,3},{2,0},{3,1},{4,6},{5,7},{6,4},{7,5},{8,10},{9,11},{10,... | collective-permute-start | bytes 393224 | tf_op jit(solution)/shard_map/ppermute | solution.py:516
  75.1 6.9 %collective-permute-start.15 = (bf16[320,128]{1,0:T(8,128)(2,1)S(1)}, bf16[320,128]{1,0:T(8,128)(2,1)S(1)}, u32[]{:S(2)}, u32[]{:S(2)}) collective-permute-start(bf16[320,128]{1,0:T(8,128)(2,1)S(1)} %copy-done.32), channel_id=1, source_target_pairs={{0,24},{4,28},{8,16},{12,20},{16,8},{20,12},{24,0},{28,4},{1,25},{... | collective-permute-start | bytes 245768 | tf_op jit(solution)/shard_map/ppermute | solution.py:516
  77.6 5.3 %collective-permute-start.17 = (bf16[208,128]{1,0:T(8,128)(2,1)S(1)}, bf16[208,128]{1,0:T(8,128)(2,1)S(1)}, u32[]{:S(2)}, u32[]{:S(2)}) collective-permute-start(bf16[208,128]{1,0:T(8,128)(2,1)S(1)} %get-tuple-element.147), channel_id=1, source_target_pairs={{0,8},{4,12},{8,0},{12,4},{16,24},{20,28},{24,16},{28,20},{1,9},{5... | collective-permute-start | bytes 159752 | tf_op jit(solution)/shard_map/ppermute | solution.py:516
  79.3 7.1 %collective-permute-start.18 = (bf16[208,128]{1,0:T(8,128)(2,1)S(1)}, bf16[208,128]{1,0:T(8,128)(2,1)S(1)}, u32[]{:S(2)}, u32[]{:S(2)}) collective-permute-start(bf16[208,128]{1,0:T(8,128)(2,1)S(1)} %get-tuple-element.148), channel_id=1, source_target_pairs={{0,16},{4,20},{8,24},{12,28},{16,0},{20,4},{24,8},{28,12},{1,17},{... | collective-permute-start | bytes 159752 | tf_op jit(solution)/shard_map/ppermute | solution.py:516
  81.9 6.0 %collective-permute-start.19 = (bf16[208,128]{1,0:T(8,128)(2,1)S(1)}, bf16[208,128]{1,0:T(8,128)(2,1)S(1)}, u32[]{:S(2)}, u32[]{:S(2)}) collective-permute-start(bf16[208,128]{1,0:T(8,128)(2,1)S(1)} %get-tuple-element.149), channel_id=1, source_target_pairs={{0,24},{4,28},{8,16},{12,20},{16,8},{20,12},{24,0},{28,4},{1,25},{... | collective-permute-start | bytes 159752 | tf_op jit(solution)/shard_map/ppermute | solution.py:516
  (33 other events, 53.2 us)

commit v5 on v4

--- a/solution.py
+++ b/solution.py
@@ -350,38 +350,48 @@
 
 
 def close_kernel(
-    heads, count,
-    low, x, bc, scal, gy, bb, gb, yb, sin, own, slope, series, rim, cw, edge_c, skip, rate, partner, *rest,
+    heads,
+    low, x, bc, scal, gy, bb, gb, slope, cw, edge_c, skip, partner, *rest,
 ):
-    *others, keep, send, gp, edge, graw, wide, stage = rest
+    *others, after, back, gp, lead, edge, wide = rest
     length, width = gy.shape
-    depth = series.shape[1]
-    after = carried(low[0] == 0, partner[...], [o[...] for o in others], heads)
+    state = carried(low[0] == 0, partner[...], [o[...] for o in others], heads)
+    after[...] = state
     rows = scal[...]
     running, step = rows[0:heads], rows[heads : 2 * heads]
-    last = running[:, length - 1 : length]
-    remain = jnp.exp(last - running)
+    remain = jnp.exp(running[:, length - 1 : length] - running)
     cols = columns(jnp.concatenate([remain, step, remain * step], axis=0))
-    xv = x[...].astype(F32)
-    back = bb[...] + widen(cols, heads, width) * mm(bc[:, 0:N], after, NT)
-    grad_x = per_lane(skip, heads, width) * gy[...] + widen(cols[:, heads:], heads, width) * back
-    grad_b = gb[...] + mm(xv * widen(cols[:, 2 * heads :], heads, width), after)
+    grown = bb[...] + widen(cols, heads, width) * mm(bc[:, 0:N], state, NT)
+    back[...] = grown
+    grad_x = per_lane(skip, heads, width) * gy[...] + widen(cols[:, heads:], heads, width) * grown
+    grad_b = gb[...] + mm(x[...].astype(F32) * widen(cols[:, 2 * heads :], heads, width), state)
     clear_ends(wide, length)
     wide[RIM : RIM + length, 0:width] = grad_x * slope[:, 0:width]
     wide[RIM : RIM + length, width:] = grad_b * slope[:, width : width + N]
     grad_x = conv_back(cw, wide, slice(0, width), length, 0, slice(0, width))
     grad_b = conv_back(cw, wide, slice(width, width + N), length, 1, slice(0, N))
-    edge[:, 0:width] = grad_x[0:RIM]
-    edge[:, width : width + N] = grad_b[0:RIM]
+    for out, cut in ((lead, slice(0, RIM)), (gp, slice(RIM, RIM + length))):
+        out[:, 0:width] = grad_x[cut]
+        out[:, width:] = grad_b[cut]
+    edge[:, 0 : width + N] = lead[...]
     edge[:, width + N :] = edge_c[...]
-    gp[:, 0:width] = grad_x[RIM:]
-    gp[:, width:] = grad_b[RIM:]
-    w_x = (mm(series[...], grad_x[RIM:], TN) + mm(rim[...], grad_x[0:RIM], TN)).astype(BF16)
-    w_b = (mm(series[...], grad_b[RIM:], TN) + mm(rim[...], grad_b[0:RIM], TN)).astype(BF16)
+
+
+def late_kernel(
+    heads, count,
+    low, x, scal, after, back, gp, lead, yb, sin, own, series, rim, rate,
+    keep, send, graw, stage,
+):
+    length, width = back.shape
+    depth = series.shape[1]
+    w_xb = (mm(series[...], gp[...], TN) + mm(rim[...], lead[...], TN)).astype(BF16)
+    rows = scal[...]
+    step = rows[heads : 2 * heads]
+    last = jnp.broadcast_to(rows[0:heads, length - 1 : length], (heads, N))
     mask = head_mask(heads, width)
-    x_back = mm_exact(mask, xv * back, NT)[0:heads]
-    final = jnp.exp(spread_rows(jnp.broadcast_to(last, (heads, N)), heads, width)) * sin[...]
-    ends = jnp.sum(mm_exact(mask, after * (final + own[...])), axis=1, keepdims=True)[0:heads]
+    x_back = mm_exact(mask, x[...].astype(F32) * back[...], NT)[0:heads]
+    final = jnp.exp(spread_rows(last, heads, width)) * sin[...] + own[...]
+    ends = jnp.sum(mm_exact(mask, after[...] * final), axis=1, keepdims=True)[0:heads]
     grad_log = running_sum_back(yb[0:heads, :] - step * x_back) + ends
     grad_step = x_back - jnp.exp(per_row(rate, x_back.shape)) * grad_log
     grad_raw = grad_step * rows[2 * heads : 3 * heads]
@@ -391,8 +401,7 @@
     piece = depth // count
     blank = jnp.zeros((LOGS, N), F32)
     for at in range(count):
-        stack_columns(stage, w_x, at, 0, piece)
-        stack_columns(stage, w_b, at, 2, piece)
+        stack_columns(stage, w_xb, at, 0, piece)
         dt_piece = jnp.concatenate(
             [dt[:, at * piece : (at + 1) * piece], blank[0 : 2 * heads, 0 : N - piece]], axis=1
         )
@@ -467,8 +476,11 @@
 HBM = pl.BlockSpec(memory_space=pltpu.HBM)
 
 
-def run(kernel, name, outs, args, scalars=(), fetched=(), scratch=(), flops=10**8):
-    moved = sum(a.size * a.dtype.itemsize for a in args)
+def run(kernel, name, outs, args, scalars=(), fetched=(), scratch=()):
+    args = [
+        pltpu.with_memory_space_constraint(a, pltpu.HBM) if i in fetched else a
+        for i, a in enumerate(args)
+    ]
 
     def place(i):
         if i in fetched:
@@ -502,7 +514,7 @@
         out_specs=[VMEM] * len(outs),
         scratch_shapes=list(scratch) + holders,
         compiler_params=pltpu.CompilerParams(vmem_limit_bytes=LIMIT),
-        cost_estimate=pl.CostEstimate(flops=flops, bytes_accessed=2 * moved, transcendentals=0),
+        cost_estimate=pl.CostEstimate(flops=10**6, bytes_accessed=2**14, transcendentals=0),
     )(*args)
 
 
@@ -664,29 +676,29 @@
     early_parts = halved(keep, send, "tm", high, "halve_early")
     behind, early_parts = lax.optimization_barrier((behind, early_parts))
     early_parts = gathered(early_parts, "tm")
-    keep, send, gp, edge, graw = run(
-        part(close_kernel, heads, count), "close",
+    after, back, gp, lead, edge = run(
+        part(close_kernel, heads), "close",
         [
-            ((hops, late, N), BF16),
-            ((hops, late, N), BF16),
+            ((width, N), F32),
+            ((length, width), F32),
             ((length, width + N), BF16),
+            ((RIM, width + N), BF16),
             ((RIM, 2 * width), BF16),
-            ((2 * heads, length), F32),
         ],
-        [
-            low, x, bc, scal, gy, bb, gb, yb, sin, own, slope, series, rim, conv_weight, edge_c,
-            skip_gain, log_rate,
-        ]
-        + behind,
-        (0, 15, 16), (11, 13, 15, 16),
-        scratch=[
-            pltpu.VMEM((length + RIM + 8, width + N), F32),
-            pltpu.VMEM((count, late, N), BF16),
-        ],
+        [low, x, bc, scal, gy, bb, gb, slope, conv_weight, edge_c, skip_gain] + behind,
+        (0, 10), (8, 10),
+        scratch=[pltpu.VMEM((length + RIM + 8, width + N), F32)],
+    )
+    edge = shifted(edge, "tm", -1)
+    keep, send, graw = run(
+        part(late_kernel, heads, count), "late",
+        [((hops, late, N), BF16), ((hops, late, N), BF16), ((2 * heads, length), F32)],
+        [low, x, scal, after, back, gp, lead, yb, sin, own, series, rim, log_rate],
+        (0, 12), (10, 12),
+        scratch=[pltpu.VMEM((count, late, N), BF16)],
     )
     late_parts = halved(keep, send, "tm", high, "halve_late")
     late_parts = gathered(late_parts, "tm")
-    edge = shifted(edge, "tm", -1)
     rows = length // parts
     keep, send = run(
         rows_kernel, "rows",

time: 90 us -> 85.4 us (0.949)
  local copies, waits for them, and re-layouts: 14.1 us -> 2.96 us
  Pallas kernels: 15.9 us -> 20.9 us
    unnamed x74 -> x24, local copies, waits for them, and re-layouts: 13.3 us -> 2.24 us
    pallas_call x18 -> x19, Pallas kernels: 15.9 us -> 20.9 us  [run(): pl.pallas_call(whole if fetched else kernel, name=name, out_shape=[jax.Sh...]
  transfers between devices with their start and end apart: 20 -> 20, of which waited for: 12 -> 13; matrix products, arithmetic and copies ran while one was open for 0% -> 0% of each run, Pallas kernels for 10% -> 15%
where the time goes in v5:
time: 85.4 us; the launch traced here: 84.9 us
  starting transfers between devices  34.5 us (40%)
  waiting for transfers between devices  25.5 us (30%)
  Pallas kernels  20.9 us (24%)
  local copies, waits for them, and re-layouts  2.96 us (3%)
  between operations  0.97 us (1%)
    pallas_call x19, Pallas kernels, run(): pl.pallas_call(whole if fetched else kernel, name=name, out_shape=[jax.Sh...  20.9 us
    ppermute x6, starting transfers between devices, shifted(): return lax.ppermute(block, axis, route)  18.4 us
    ppermute x14, starting transfers between devices, swapped(): lax.ppermute(block, axis, [(i, i ^ flip) for i in range(lax.axis_size(axi...  16.2 us
    ppermute x6, waiting for transfers between devices, shifted(): return lax.ppermute(block, axis, route)  13.1 us
    ppermute x14, waiting for transfers between devices, swapped(): lax.ppermute(block, axis, [(i, i ^ flip) for i in range(lax.axis_size(axi...  12.4 us
    unnamed x24, local copies, waits for them, and re-layouts  2.24 us
  transfers between devices with their start and end apart: 20, of which 13 were waited for; matrix products, arithmetic and copies ran while one was open for 0% of the time, Pallas kernels for 15%

profile of v5, /device:TPU:0, one launch (start us, length us, event | category | flops | bytes accessed | tf_op | source)
XLA Modules:
  0.0 84.9 jit_solution(1117314050948427499)
XLA Ops:
  1.4 4.9 %collective-permute-start = (bf16[16,512]{1,0:T(8,128)(2,1)S(1)}, bf16[16,512]{1,0:T(8,128)(2,1)S(1)}, u32[]{:S(2)}, u32[]{:S(2)}) collective-permute-start(bf16[16,512]{1,0:T(8,128)(2,1)S(1)} %slice.3), channel_id=1, source_target_pairs={{0,4},{4,8},{8,12},{12,16},{16,20},{20,24},{24,28},{1,5},{5,9},{9,... | collective-permute-start | bytes 49160 | tf_op jit(solution)/shard_map/ppermute | solution.py:524
  6.2 2.2 %project.1 = (bf16[256,256]{1,0:T(8,128)(2,1)S(1)}, bf16[256,512]{1,0:T(8,128)(2,1)S(1)}, f32[16,256]{1,0:T(8,128)S(1)}) custom-call(bf16[256,512]{1,0:T(8,128)(2,1)} %refs_10_.5, bf16[3,512,256]{2,1,0:T(8,128)(2,1)} %bitcast.9, bf16[4,512]{1,0:T(4,128)(2,1)} %bitcast.13, f32[4]{0:T(128)} %refs_3_.3, f32[4]{0:T(128)} %refs_12_.3), custom_call_target="tpu_custom_call" | custom-call | flops 1000000 | bytes 16384 | tf_op jit(solution)/shard_map/project/pallas_call | solution.py:509
  8.5 2.1 %conv.1 = (bf16[256,256]{1,0:T(8,128)(2,1)S(1)}, bf16[256,256]{1,0:T(8,128)(2,1)S(1)}, f32[256,512]{1,0:T(8,128)S(1)}, f32[256,128]{1,0:T(8,128)S(1)}, bf16[272,128]{1,0:T(8,128)(2,1)S(1)}) custom-call(bf16[256,512]{1,0:T(8,128)(2,1)S(1)} %get-tuple-element.82.refs_0_, bf16[16,512]{1,0:T(8,128)(2,1)S(1)} %collective-permute-done.refs_1_.refs_13_.refs_11_, ...), custom_call_target="tpu_custom_call" | custom-call | flops 1000000 | bytes 16384 | tf_op jit(solution)/shard_map/conv/pallas_call | solution.py:509
  11.2 1.5 %collective-permute-start.1 = (bf16[272,128]{1,0:T(8,128)(2,1)S(1)}, bf16[272,128]{1,0:T(8,128)(2,1)S(1)}, u32[]{:S(2)}, u32[]{:S(2)}) collective-permute-start(bf16[272,128]{1,0:T(8,128)(2,1)S(1)} %get-tuple-element.84.mine), channel_id=1, source_target_pairs={{0,4},{4,0},{8,12},{12,8},{16,20},{20,16},{24,28},{28,24},{1,5},{5... | collective-permute-start | bytes 208904 | tf_op jit(solution)/shard_map/ppermute | solution.py:528
  12.8 1.8 %inside.1 = (f32[256,256]{1,0:T(8,128)S(1)}, f32[256,256]{1,0:T(8,128)S(1)}, f32[256,512]{1,0:T(8,128)S(1)}) custom-call(bf16[256,256]{1,0:T(8,128)(2,1)S(1)} %get-tuple-element.85.refs_0_.refs_7_.refs_5_.refs_1_, bf16[256,256]{1,0:T(8,128)(2,1)S(1)} %get-tuple-element.86.refs_1_.bc.refs_8_.refs_6_.refs_2_, ...), custom_call_target="tpu_custom_call" | custom-call | flops 1000000 | bytes 16384 | tf_op jit(solution)/shard_map/inside/pallas_call | solution.py:509
  15.6 4.3 %collective-permute-start.2 = (bf16[272,128]{1,0:T(8,128)(2,1)S(1)}, bf16[272,128]{1,0:T(8,128)(2,1)S(1)}, u32[]{:S(2)}, u32[]{:S(2)}) collective-permute-start(bf16[272,128]{1,0:T(8,128)(2,1)S(1)} %pair.2.nearer), channel_id=1, source_target_pairs={{0,8},{4,12},{8,16},{12,20},{16,24},{20,28},{1,9},{5,13},{9,17},{1... | collective-permute-start | bytes 208904 | tf_op jit(solution)/shard_map/ppermute | solution.py:524
  20.0 1.9 %collective-permute-done.2.farther.rest_1_ = bf16[272,128]{1,0:T(8,128)(2,1)S(1)} collective-permute-done((bf16[272,128]{1,0:T(8,128)(2,1)S(1)}, bf16[272,128]{1,0:T(8,128)(2,1)S(1)}, u32[]{:S(2)}, u32[]{:S(2)}) %collective-permute-start.2) | collective-permute-done | bytes 69664 | tf_op jit(solution)/shard_map/ppermute | solution.py:524
  21.9 5.3 %collective-permute-start.3 = (bf16[272,128]{1,0:T(8,128)(2,1)S(1)}, bf16[272,128]{1,0:T(8,128)(2,1)S(1)}, u32[]{:S(2)}, u32[]{:S(2)}) collective-permute-start(bf16[272,128]{1,0:T(8,128)(2,1)S(1)} %link.2), channel_id=1, source_target_pairs={{0,16},{4,20},{8,24},{12,28},{1,17},{5,21},{9,25},{13,29},{2,18},{... | collective-permute-start | bytes 208904 | tf_op jit(solution)/shard_map/ppermute | solution.py:524
  27.2 1.9 %collective-permute-done.3.rest_0_ = bf16[272,128]{1,0:T(8,128)(2,1)S(1)} collective-permute-done((bf16[272,128]{1,0:T(8,128)(2,1)S(1)}, bf16[272,128]{1,0:T(8,128)(2,1)S(1)}, u32[]{:S(2)}, u32[]{:S(2)}) %collective-permute-start.3) | collective-permute-done | bytes 69664 | tf_op jit(solution)/shard_map/ppermute | solution.py:524
  32.7 2.2 %collective-permute-done.5.other = f32[8,256]{1,0:T(8,128)S(1)} collective-permute-done((f32[8,256]{1,0:T(8,128)S(1)}, f32[8,256]{1,0:T(8,128)S(1)}, u32[]{:S(2)}, u32[]{:S(2)}) %collective-permute-start.5) | collective-permute-done | bytes 8224 | tf_op jit(solution)/shard_map/ppermute | solution.py:528
  36.3 3.2 %early.1 = (bf16[256,256]{1,0:T(8,128)(2,1)S(1)}, bf16[256,256]{1,0:T(8,128)(2,1)S(1)}, bf16[256,128]{1,0:T(8,128)(2,1)S(1)}, f32[256,128]{1,0:T(8,128)S(1)}, bf...) custom-call(s32[1]{0:T(128)} %bitcast.2.low.refs_0_, ...), custom_call_target="tpu_custom_call" | custom-call | flops 1000000 | bytes 16384 | tf_op jit(solution)/shard_map/early/pallas_call | solution.py:509
  42.3 2.3 %beside.1 = (bf16[256,512]{1,0:T(8,128)(2,1)S(1)}, f32[256,512]{1,0:T(8,128)S(1)}, f32[256,256]{1,0:T(8,128)S(1)}, f32[8,256]{1,0:T(8,128)S(1)}) custom-call(bf16[256,256]{1,0:T(8,128)(2,1)S(1)} %get-tuple-element.110.refs_0_, bf16[256,256]{1,0:T(8,128)(2,1)S(1)} %get-tuple-element.111.refs_1_, bf16[256,128]{1,0:T(8,128)(2,1)S(1)} %get-tuple-element.112.refs_2_, ...), custom_call_target="tpu_custom_call" | custom-call | flops 1000000 | bytes 16384 | tf_op jit(solution)/shard_map/beside/pallas_call | solution.py:509
  44.6 2.6 %collective-permute-done.7.farther.refs_13_ = bf16[272,128]{1,0:T(8,128)(2,1)S(1)} collective-permute-done((bf16[272,128]{1,0:T(8,128)(2,1)S(1)}, bf16[272,128]{1,0:T(8,128)(2,1)S(1)}, u32[]{:S(2)}, u32[]{:S(2)}) %collective-permute-start.7) | collective-permute-done | bytes 69664 | tf_op jit(solution)/shard_map/ppermute | solution.py:524
  48.7 5.6 %collective-permute-done.8.refs_12_ = bf16[272,128]{1,0:T(8,128)(2,1)S(1)} collective-permute-done((bf16[272,128]{1,0:T(8,128)(2,1)S(1)}, bf16[272,128]{1,0:T(8,128)(2,1)S(1)}, u32[]{:S(2)}, u32[]{:S(2)}) %collective-permute-start.8) | collective-permute-done | bytes 69664 | tf_op jit(solution)/shard_map/ppermute | solution.py:524
  54.4 1.8 %close.1 = (f32[256,128]{1,0:T(8,128)S(1)}, f32[256,256]{1,0:T(8,128)S(1)}, bf16[256,384]{1,0:T(8,128)(2,1)S(1)}, bf16[16,384]{1,0:T(8,128)(2,1)S(1)}, bf16[16,512]{1,0:T(8,128)(2,1)S(1)}) custom-call(s32[1]{0:T(128)} %bitcast.2.low.refs_0_, bf16[256,256]{1,0:T(8,128)(2,1)S(1)} %get-tuple-element.85.refs_0_.refs_7_.refs_5_.refs_1_, ...), custom_call_target="tpu_custom_call" | custom-call | flops 1000000 | bytes 16384 | tf_op jit(solution)/shard_map/close/pallas_call | solution.py:509
  59.1 2.4 %late.1 = (bf16[4,208,128]{2,1,0:T(8,128)(2,1)S(1)}, bf16[4,208,128]{2,1,0:T(8,128)(2,1)S(1)}, f32[8,256]{1,0:T(8,128)S(1)}) custom-call(s32[1]{0:T(128)} %bitcast.2.low.refs_0_, bf16[256,256]{1,0:T(8,128)(2,1)S(1)} %get-tuple-element.85.refs_0_.refs_7_.refs_5_.refs_1_, f32[16,256]{1,0:T(8,128)S(1)} %get-tuple-element.83.refs_5_.refs_2_.scal.refs_9_.refs_7_.refs_3_, ...), custom_call_target="tpu_custom_call" | custom-call | flops 1000000 | bytes 16384 | tf_op jit(solution)/shard_map/late/pallas_call | solution.py:509
  62.5 1.7 %rows.1 = (bf16[2,64,1024]{2,1,0:T(8,128)(2,1)S(1)}, bf16[2,64,1024]{2,1,0:T(8,128)(2,1)S(1)}) custom-call(s32[1]{0:T(128)} %bitcast.1.refs_0_, bf16[256,512]{1,0:T(8,128)(2,1)S(1)} %get-tuple-element.117.refs_1_, f32[256,512]{1,0:T(8,128)S(1)} %get-tuple-element.118.refs_2_, bf16[256,384]{1,0:T(8,128)(2,1)S(1)} %get-tuple-element.132.refs_5_.refs_3_, ...), custom_call_target="tpu_custom_call" | custom-call | flops 1000000 | bytes 16384 | tf_op jit(solution)/shard_map/rows/pallas_call | solution.py:509
  64.3 2.0 %collective-permute-start.16 = (bf16[4,208,128]{2,1,0:T(8,128)(2,1)S(1)}, bf16[4,208,128]{2,1,0:T(8,128)(2,1)S(1)}, u32[]{:S(2)}, u32[]{:S(2)}) collective-permute-start(bf16[4,208,128]{2,1,0:T(8,128)(2,1)S(1)} %get-tuple-element.151), channel_id=1, source_target_pairs={{0,4},{4,0},{8,12},{12,8},{16,20},{20,16},{24,28},{28,24},{1,5},{5... | collective-permute-start | bytes 638984 | tf_op jit(solution)/shard_map/ppermute | solution.py:528
  66.3 2.0 %collective-permute-start.13 = (bf16[320,128]{1,0:T(8,128)(2,1)S(1)}, bf16[320,128]{1,0:T(8,128)(2,1)S(1)}, u32[]{:S(2)}, u32[]{:S(2)}) collective-permute-start(bf16[320,128]{1,0:T(8,128)(2,1)S(1)} %copy-done.11), channel_id=1, source_target_pairs={{0,8},{4,12},{8,0},{12,4},{16,24},{20,28},{24,16},{28,20},{1,9},{5... | collective-permute-start | bytes 245768 | tf_op jit(solution)/shard_map/ppermute | solution.py:528
  68.4 1.6 %collective-permute-start.12 = (bf16[64,1024]{1,0:T(8,128)(2,1)S(1)}, bf16[64,1024]{1,0:T(8,128)(2,1)S(1)}, u32[]{:S(2)}, u32[]{:S(2)}) collective-permute-start(bf16[64,1024]{1,0:T(8,128)(2,1)S(1)} %get-tuple-element.143), channel_id=1, source_target_pairs={{0,2},{1,3},{2,0},{3,1},{4,6},{5,7},{6,4},{7,5},{8,10},{9,11},{10,... | collective-permute-start | bytes 393224 | tf_op jit(solution)/shard_map/ppermute | solution.py:528
  70.0 2.4 %collective-permute-start.15 = (bf16[320,128]{1,0:T(8,128)(2,1)S(1)}, bf16[320,128]{1,0:T(8,128)(2,1)S(1)}, u32[]{:S(2)}, u32[]{:S(2)}) collective-permute-start(bf16[320,128]{1,0:T(8,128)(2,1)S(1)} %copy-done.7), channel_id=1, source_target_pairs={{0,24},{4,28},{8,16},{12,20},{16,8},{20,12},{24,0},{28,4},{1,25},{... | collective-permute-start | bytes 245768 | tf_op jit(solution)/shard_map/ppermute | solution.py:528
  72.4 1.8 %collective-permute-start.17 = (bf16[208,128]{1,0:T(8,128)(2,1)S(1)}, bf16[208,128]{1,0:T(8,128)(2,1)S(1)}, u32[]{:S(2)}, u32[]{:S(2)}) collective-permute-start(bf16[208,128]{1,0:T(8,128)(2,1)S(1)} %get-tuple-element.153), channel_id=1, source_target_pairs={{0,8},{4,12},{8,0},{12,4},{16,24},{20,28},{24,16},{28,20},{1,9},{5... | collective-permute-start | bytes 159752 | tf_op jit(solution)/shard_map/ppermute | solution.py:528
  75.8 1.7 %collective-permute-done.14.refs_2_ = bf16[320,128]{1,0:T(8,128)(2,1)S(1)} collective-permute-done((bf16[320,128]{1,0:T(8,128)(2,1)S(1)}, bf16[320,128]{1,0:T(8,128)(2,1)S(1)}, u32[]{:S(2)}, u32[]{:S(2)}) %collective-permute-start.14) | collective-permute-done | bytes 81952 | tf_op jit(solution)/shard_map/ppermute | solution.py:528
  78.1 4.0 %collective-permute-done.18.refs_6_ = bf16[208,128]{1,0:T(8,128)(2,1)S(1)} collective-permute-done((bf16[208,128]{1,0:T(8,128)(2,1)S(1)}, bf16[208,128]{1,0:T(8,128)(2,1)S(1)}, u32[]{:S(2)}, u32[]{:S(2)}) %collective-permute-start.18) | collective-permute-done | bytes 53280 | tf_op jit(solution)/shard_map/ppermute | solution.py:528
  (61 shorter events, 20.5 us)
Async XLA Ops:
  1.4 7.1 %collective-permute-start = (bf16[16,512]{1,0:T(8,128)(2,1)S(1)}, bf16[16,512]{1,0:T(8,128)(2,1)S(1)}, u32[]{:S(2)}, u32[]{:S(2)}) collective-permute-start(bf16[16,512]{1,0:T(8,128)(2,1)S(1)} %slice.3), channel_id=1, source_target_pairs={{0,4},{4,8},{8,12},{12,16},{16,20},{20,24},{24,28},{1,5},{5,9},{9,... | collective-permute-start | bytes 49160 | tf_op jit(solution)/shard_map/ppermute | solution.py:524
  11.2 4.3 %collective-permute-start.1 = (bf16[272,128]{1,0:T(8,128)(2,1)S(1)}, bf16[272,128]{1,0:T(8,128)(2,1)S(1)}, u32[]{:S(2)}, u32[]{:S(2)}) collective-permute-start(bf16[272,128]{1,0:T(8,128)(2,1)S(1)} %get-tuple-element.84.mine), channel_id=1, source_target_pairs={{0,4},{4,0},{8,12},{12,8},{16,20},{20,16},{24,28},{28,24},{1,5},{5... | collective-permute-start | bytes 208904 | tf_op jit(solution)/shard_map/ppermute | solution.py:528
  15.6 6.3 %collective-permute-start.2 = (bf16[272,128]{1,0:T(8,128)(2,1)S(1)}, bf16[272,128]{1,0:T(8,128)(2,1)S(1)}, u32[]{:S(2)}, u32[]{:S(2)}) collective-permute-start(bf16[272,128]{1,0:T(8,128)(2,1)S(1)} %pair.2.nearer), channel_id=1, source_target_pairs={{0,8},{4,12},{8,16},{12,20},{16,24},{20,28},{1,9},{5,13},{9,17},{1... | collective-permute-start | bytes 208904 | tf_op jit(solution)/shard_map/ppermute | solution.py:524
  21.9 7.2 %collective-permute-start.3 = (bf16[272,128]{1,0:T(8,128)(2,1)S(1)}, bf16[272,128]{1,0:T(8,128)(2,1)S(1)}, u32[]{:S(2)}, u32[]{:S(2)}) collective-permute-start(bf16[272,128]{1,0:T(8,128)(2,1)S(1)} %link.2), channel_id=1, source_target_pairs={{0,16},{4,20},{8,24},{12,28},{1,17},{5,21},{9,25},{13,29},{2,18},{... | collective-permute-start | bytes 208904 | tf_op jit(solution)/shard_map/ppermute | solution.py:524
  30.0 1.2 %collective-permute-start.4 = (f32[8,256]{1,0:T(8,128)S(1)}, f32[8,256]{1,0:T(8,128)S(1)}, u32[]{:S(2)}, u32[]{:S(2)}) collective-permute-start(f32[8,256]{1,0:T(8,128)S(1)} %get-tuple-element.95), channel_id=1, source_target_pairs={{0,1},{1,0},{2,3},{3,2},{4,5},{5,4},{6,7},{7,6},{8,9},{9,8},{10,11... | collective-permute-start | bytes 24584 | tf_op jit(solution)/shard_map/ppermute | solution.py:528
  31.2 3.7 %collective-permute-start.5 = (f32[8,256]{1,0:T(8,128)S(1)}, f32[8,256]{1,0:T(8,128)S(1)}, u32[]{:S(2)}, u32[]{:S(2)}) collective-permute-start(f32[8,256]{1,0:T(8,128)S(1)} %add.14.sums), channel_id=1, source_target_pairs={{0,2},{1,3},{2,0},{3,1},{4,6},{5,7},{6,4},{7,5},{8,10},{9,11},{10,... | collective-permute-start | bytes 24584 | tf_op jit(solution)/shard_map/ppermute | solution.py:528
  35.6 4.4 %collective-permute-start.6 = (bf16[272,128]{1,0:T(8,128)(2,1)S(1)}, bf16[272,128]{1,0:T(8,128)(2,1)S(1)}, u32[]{:S(2)}, u32[]{:S(2)}) collective-permute-start(bf16[272,128]{1,0:T(8,128)(2,1)S(1)} %get-tuple-element.97.mine), channel_id=1, source_target_pairs={{0,4},{4,0},{8,12},{12,8},{16,20},{20,16},{24,28},{28,24},{1,5},{5... | collective-permute-start | bytes 208904 | tf_op jit(solution)/shard_map/ppermute | solution.py:528
  39.9 8.7 %collective-permute-start.9 = (bf16[4,320,128]{2,1,0:T(8,128)(2,1)}, bf16[4,320,128]{2,1,0:T(8,128)(2,1)S(1)}, u32[]{:S(2)}, u32[]{:S(2)}) collective-permute-start(bf16[4,320,128]{2,1,0:T(8,128)(2,1)} %get-tuple-element.124), channel_id=1, source_target_pairs={{0,4},{4,0},{8,12},{12,8},{16,20},{20,16},{24,28},{28,24},{1,5},{5... | collective-permute-start | bytes 983048 | tf_op jit(solution)/shard_map/ppermute | solution.py:528
  41.0 6.3 %collective-permute-start.7 = (bf16[272,128]{1,0:T(8,128)(2,1)S(1)}, bf16[272,128]{1,0:T(8,128)(2,1)S(1)}, u32[]{:S(2)}, u32[]{:S(2)}) collective-permute-start(bf16[272,128]{1,0:T(8,128)(2,1)S(1)} %pair.3.nearer), channel_id=1, source_target_pairs={{8,0},{12,4},{16,8},{20,12},{24,16},{28,20},{9,1},{13,5},{17,9},{2... | collective-permute-start | bytes 208904 | tf_op jit(solution)/shard_map/ppermute | solution.py:524
  47.3 7.1 %collective-permute-start.8 = (bf16[272,128]{1,0:T(8,128)(2,1)S(1)}, bf16[272,128]{1,0:T(8,128)(2,1)S(1)}, u32[]{:S(2)}, u32[]{:S(2)}) collective-permute-start(bf16[272,128]{1,0:T(8,128)(2,1)S(1)} %link.3), channel_id=1, source_target_pairs={{16,0},{20,4},{24,8},{28,12},{17,1},{21,5},{25,9},{29,13},{18,2},{... | collective-permute-start | bytes 208904 | tf_op jit(solution)/shard_map/ppermute | solution.py:524
  48.7 7.5 %copy-start.6 = (bf16[320,128]{1,0:T(8,128)(2,1)}, bf16[320,128]{1,0:T(8,128)(2,1)S(1)}, u32[]{:S(2)}) copy-start(bf16[320,128]{1,0:T(8,128)(2,1)S(1)} %get-tuple-element.149) | copy-start | bytes 245764
  48.7 7.5 %copy-start.8 = (bf16[320,128]{1,0:T(8,128)(2,1)}, bf16[320,128]{1,0:T(8,128)(2,1)S(1)}, u32[]{:S(2)}) copy-start(bf16[320,128]{1,0:T(8,128)(2,1)S(1)} %get-tuple-element.148) | copy-start | bytes 245764
  48.7 7.5 %copy-start.10 = (bf16[320,128]{1,0:T(8,128)(2,1)}, bf16[320,128]{1,0:T(8,128)(2,1)S(1)}, u32[]{:S(2)}) copy-start(bf16[320,128]{1,0:T(8,128)(2,1)S(1)} %get-tuple-element.147) | copy-start | bytes 245764
  56.9 5.6 %collective-permute-start.10 = (bf16[16,512]{1,0:T(8,128)(2,1)S(1)}, bf16[16,512]{1,0:T(8,128)(2,1)S(1)}, u32[]{:S(2)}, u32[]{:S(2)}) collective-permute-start(bf16[16,512]{1,0:T(8,128)(2,1)S(1)} %get-tuple-element.139), channel_id=1, source_target_pairs={{4,0},{8,4},{12,8},{16,12},{20,16},{24,20},{28,24},{5,1},{9,5},{13... | collective-permute-start | bytes 49160 | tf_op jit(solution)/shard_map/ppermute | solution.py:524
  62.5 5.8 %copy-start.9 = (bf16[320,128]{1,0:T(8,128)(2,1)S(1)}, bf16[320,128]{1,0:T(8,128)(2,1)}, u32[]{:S(2)}) copy-start(bf16[320,128]{1,0:T(8,128)(2,1)} %copy-done.8) | copy-start | bytes 245764
  64.2 4.1 %collective-permute-start.11 = (bf16[2,64,1024]{2,1,0:T(8,128)(2,1)S(1)}, bf16[2,64,1024]{2,1,0:T(8,128)(2,1)S(1)}, u32[]{:S(2)}, u32[]{:S(2)}) collective-permute-start(bf16[2,64,1024]{2,1,0:T(8,128)(2,1)S(1)} %get-tuple-element.141), channel_id=1, source_target_pairs={{0,1},{1,0},{2,3},{3,2},{4,5},{5,4},{6,7},{7,6},{8,9},{9,8},{10,11... | collective-permute-start | bytes 786440 | tf_op jit(solution)/shard_map/ppermute | solution.py:528
  64.3 8.1 %collective-permute-start.16 = (bf16[4,208,128]{2,1,0:T(8,128)(2,1)S(1)}, bf16[4,208,128]{2,1,0:T(8,128)(2,1)S(1)}, u32[]{:S(2)}, u32[]{:S(2)}) collective-permute-start(bf16[4,208,128]{2,1,0:T(8,128)(2,1)S(1)} %get-tuple-element.151), channel_id=1, source_target_pairs={{0,4},{4,0},{8,12},{12,8},{16,20},{20,16},{24,28},{28,24},{1,5},{5... | collective-permute-start | bytes 638984 | tf_op jit(solution)/shard_map/ppermute | solution.py:528
  66.3 8.0 %collective-permute-start.13 = (bf16[320,128]{1,0:T(8,128)(2,1)S(1)}, bf16[320,128]{1,0:T(8,128)(2,1)S(1)}, u32[]{:S(2)}, u32[]{:S(2)}) collective-permute-start(bf16[320,128]{1,0:T(8,128)(2,1)S(1)} %copy-done.11), channel_id=1, source_target_pairs={{0,8},{4,12},{8,0},{12,4},{16,24},{20,28},{24,16},{28,20},{1,9},{5... | collective-permute-start | bytes 245768 | tf_op jit(solution)/shard_map/ppermute | solution.py:528
  68.3 9.2 %collective-permute-start.14 = (bf16[320,128]{1,0:T(8,128)(2,1)S(1)}, bf16[320,128]{1,0:T(8,128)(2,1)S(1)}, u32[]{:S(2)}, u32[]{:S(2)}) collective-permute-start(bf16[320,128]{1,0:T(8,128)(2,1)S(1)} %copy-done.9), channel_id=1, source_target_pairs={{0,16},{4,20},{8,24},{12,28},{16,0},{20,4},{24,8},{28,12},{1,17},{... | collective-permute-start | bytes 245768 | tf_op jit(solution)/shard_map/ppermute | solution.py:528
  68.4 15.8 %collective-permute-start.12 = (bf16[64,1024]{1,0:T(8,128)(2,1)S(1)}, bf16[64,1024]{1,0:T(8,128)(2,1)S(1)}, u32[]{:S(2)}, u32[]{:S(2)}) collective-permute-start(bf16[64,1024]{1,0:T(8,128)(2,1)S(1)} %get-tuple-element.143), channel_id=1, source_target_pairs={{0,2},{1,3},{2,0},{3,1},{4,6},{5,7},{6,4},{7,5},{8,10},{9,11},{10,... | collective-permute-start | bytes 393224 | tf_op jit(solution)/shard_map/ppermute | solution.py:528
  70.0 7.6 %collective-permute-start.15 = (bf16[320,128]{1,0:T(8,128)(2,1)S(1)}, bf16[320,128]{1,0:T(8,128)(2,1)S(1)}, u32[]{:S(2)}, u32[]{:S(2)}) collective-permute-start(bf16[320,128]{1,0:T(8,128)(2,1)S(1)} %copy-done.7), channel_id=1, source_target_pairs={{0,24},{4,28},{8,16},{12,20},{16,8},{20,12},{24,0},{28,4},{1,25},{... | collective-permute-start | bytes 245768 | tf_op jit(solution)/shard_map/ppermute | solution.py:528
  72.4 5.6 %collective-permute-start.17 = (bf16[208,128]{1,0:T(8,128)(2,1)S(1)}, bf16[208,128]{1,0:T(8,128)(2,1)S(1)}, u32[]{:S(2)}, u32[]{:S(2)}) collective-permute-start(bf16[208,128]{1,0:T(8,128)(2,1)S(1)} %get-tuple-element.153), channel_id=1, source_target_pairs={{0,8},{4,12},{8,0},{12,4},{16,24},{20,28},{24,16},{28,20},{1,9},{5... | collective-permute-start | bytes 159752 | tf_op jit(solution)/shard_map/ppermute | solution.py:528
  74.3 7.8 %collective-permute-start.18 = (bf16[208,128]{1,0:T(8,128)(2,1)S(1)}, bf16[208,128]{1,0:T(8,128)(2,1)S(1)}, u32[]{:S(2)}, u32[]{:S(2)}) collective-permute-start(bf16[208,128]{1,0:T(8,128)(2,1)S(1)} %get-tuple-element.154), channel_id=1, source_target_pairs={{0,16},{4,20},{8,24},{12,28},{16,0},{20,4},{24,8},{28,12},{1,17},{... | collective-permute-start | bytes 159752 | tf_op jit(solution)/shard_map/ppermute | solution.py:528
  77.5 5.9 %collective-permute-start.19 = (bf16[208,128]{1,0:T(8,128)(2,1)S(1)}, bf16[208,128]{1,0:T(8,128)(2,1)S(1)}, u32[]{:S(2)}, u32[]{:S(2)}) collective-permute-start(bf16[208,128]{1,0:T(8,128)(2,1)S(1)} %get-tuple-element.155), channel_id=1, source_target_pairs={{0,24},{4,28},{8,16},{12,20},{16,8},{20,12},{24,0},{28,4},{1,25},{... | collective-permute-start | bytes 159752 | tf_op jit(solution)/shard_map/ppermute | solution.py:528
  (8 other events, 22.3 us)
